TPU v7x, 32 devices: a whole 2x2x4 slice. The times are simulated.
32 devices in a mesh: ctx: 16 (over z, y, core), head: 2 (over x).
Axes of the slice: x: 2, y: 2, z: 4, core: 2. Of those that a mesh axis runs over, the one named last changes fastest.
Arguments:
- queries: bfloat16 [8192, 2048], P('ctx', 'head'), may hold values from -13 to 13, as said below
- keys: bfloat16 [8192, 512], P('ctx', 'head'), may hold values from -13 to 13
- values: bfloat16 [8192, 512], P('ctx', 'head'), may hold values from -24 to 24
- positions: int32 [8192], P('ctx'), may hold values from 0 to 4095, as said below
- out_weight: bfloat16 [2048, 4096], P(None, 'head'), may hold values from -0.125 to 0.125
Outputs:
- mixed: bfloat16 [8192, 4096], P('ctx', 'head')
Inputs may be any that keep to these rules, and one draw needn't show every extreme that they name: queries, keys: every entry lies in the stated range. positions[r] is 0 where the token at sequence position g(r) begins a document and one more than the position of the token at g(r) - 1 otherwise; documents begin at sequence positions 0 and 4096 and possibly elsewhere in the first half; the second half is one document.
All inputs are finite; a program needn't handle non-finite values.
Results may differ from a plain program's by a relative error of at most 0.012.
The roundings to bfloat16 on the way count: a program that leaves them out, or rounds other values in their place, can miss the bound.
Values may be sent and summed in bfloat16 or wider, within the bound.
No kernel may reach another device: no remote copies, remote signals or barrier semaphores. Data moves between devices by JAX's collectives and lax.ppermute only.
A program may use at most 128 MiB of HBM per device.

v0:
```python
import functools
import math

import jax
import jax.numpy as jnp
import numpy as np
from jax import lax
from jax.experimental import pallas as pl
from jax.experimental.pallas import tpu as pltpu
from jax.sharding import PartitionSpec as P

HEAD_SIZE = 128
LOWEST = -1e30
FAR = 1 << 16
MIB = 1 << 20
SCORE_SCALE = math.log2(math.e) / math.sqrt(HEAD_SIZE)
BF16, F32 = jnp.bfloat16, jnp.float32


def distance(rank, step, count):
    return jnp.where(rank >= step, step, count - step)


def waits_for_keys(rank):
    return (rank == 1) | (rank == 2)


def first_begin(rank, half):
    return pl.multiple_of(jnp.where(rank < 2, 0, half), half)


def half_positions(p_ref, rank, first):
    half = p_ref.shape[1] // 2
    early = (rank < 2) if first else (rank >= 2)
    return jnp.where(early, p_ref[:, :half], p_ref[:, half:])


def column(row, width):
    return jnp.broadcast_to(row, (width, row.shape[1])).T


def tile_biases(position_row, kinds):
    number = position_row.shape[1]
    position = column(position_row, number)
    query = lax.broadcasted_iota(jnp.int32, (number, number), 0)
    key = lax.broadcasted_iota(jnp.int32, (number, number), 1)
    ahead = key - query
    reach = ahead + position
    found = []
    for pieces, diagonal in kinds:
        allowed = reach >= pieces * number
        if diagonal:
            allowed = allowed & (ahead <= 0)
        found.append(jnp.where(allowed, 0.0, LOWEST).astype(F32))
    return found


def sine_cosine(angle):
    turns = jnp.floor(angle * (2.0 / math.pi) + 0.5)
    rest = ((angle - turns * 1.5703125) - turns * 4.837512969970703e-4) - turns * 7.549789954891888e-8
    square = rest * rest
    sine = ((-1.9515295891e-4 * square + 8.3321608736e-3) * square - 1.6666654611e-1) * square * rest + rest
    cosine = (
        ((2.443315711809948e-5 * square - 1.388731625493765e-3) * square + 4.166664568298827e-2) * square * square
        - 0.5 * square
        + 1.0
    )
    quarter = turns.astype(jnp.int32)
    swap = (quarter & 1) == 1
    out_sine = jnp.where(swap, cosine, sine)
    out_cosine = jnp.where(swap, sine, cosine)
    out_sine = jnp.where((quarter & 2) == 2, -out_sine, out_sine)
    out_cosine = jnp.where(((quarter + 1) & 2) == 2, -out_cosine, out_cosine)
    return out_sine, out_cosine


def turned(block, cosine, sinus):
    wide = block.astype(F32)
    return (wide * cosine + pltpu.roll(wide, HEAD_SIZE // 2, 1) * sinus).astype(BF16)


def scores_of(query, key, bias):
    raw = lax.dot_general(query, key, (((1,), (1,)), ((), ())), preferred_element_type=F32)
    return raw * SCORE_SCALE + bias


def weighted(weights, value):
    return jnp.dot(weights.astype(BF16), value, preferred_element_type=F32)


def spread(entries):
    return jnp.broadcast_to(entries, (entries.shape[0], HEAD_SIZE))


def with_ones(value):
    return jnp.concatenate([value, jnp.ones_like(value)], axis=1)


def head_slices(head, group, width):
    at = slice(head * HEAD_SIZE, (head + 1) * HEAD_SIZE)
    low = head // group * HEAD_SIZE
    return at, slice(low, low + HEAD_SIZE), slice(width + low, width + low + HEAD_SIZE)


def begin_state(query, keys, values, biases):
    scores = [scores_of(query, key, bias) for key, bias in zip(keys, biases)]
    top = jnp.max(functools.reduce(jnp.maximum, scores), axis=1, keepdims=True)
    weights = [jnp.exp2(score - top) for score in scores]
    both = functools.reduce(jnp.add, [weighted(w, value) for w, value in zip(weights, values)])
    return both[:, :HEAD_SIZE], spread(top), both[:, HEAD_SIZE:]


def added_tile(summed, top, total, query, key, value, bias):
    score = scores_of(query, key, bias)
    updated = jnp.maximum(top, spread(jnp.max(score, axis=1, keepdims=True)))
    weights = jnp.exp2(score - jnp.concatenate([updated] * (score.shape[1] // HEAD_SIZE), axis=1))
    factor = jnp.exp2(top - updated)
    both = weighted(weights, value)
    return summed * factor + both[:, :HEAD_SIZE], updated, total * factor + both[:, HEAD_SIZE:]


def finished(state):
    summed, _, total = state
    return (summed * (1.0 / total)).astype(BF16)


def keys_kernel(
    count, k_hbm, v_hbm, q_hbm, p_hbm, f_hbm, early_ref, near_ref, next_ref, rot_ref, v_ref, q_ref, p_ref, cos_ref, sin_ref,
    k_ref, f_ref, sems,
):
    pairs = ((p_hbm, p_ref), (f_hbm, f_ref), (k_hbm, k_ref), (v_hbm, v_ref), (q_hbm, q_ref))
    copies = [pltpu.make_async_copy(source, target, sems.at[i]) for i, (source, target) in enumerate(pairs)]
    for copy in copies:
        copy.start()
    rank = lax.axis_index("ctx")
    half = k_ref.shape[0] // 2
    width = k_ref.shape[1]
    copies[0].wait()
    copies[1].wait()
    position = p_ref[...].astype(F32)
    early = column(position[:, :half], HEAD_SIZE)
    late = column(position[:, half:], HEAD_SIZE)
    lane = lax.broadcasted_iota(jnp.int32, (half, HEAD_SIZE), 1)
    front = lane < HEAD_SIZE // 2
    sine, cosine = sine_cosine(jnp.where(front, early, late) * f_ref[...])
    sine_other = pltpu.roll(sine, HEAD_SIZE // 2, 1)
    cosine_other = pltpu.roll(cosine, HEAD_SIZE // 2, 1)
    cos_ref[:half] = jnp.where(front, cosine, cosine_other)
    cos_ref[half:] = jnp.where(front, cosine_other, cosine)
    sin_ref[:half] = jnp.where(front, -sine, sine_other)
    sin_ref[half:] = jnp.where(front, -sine_other, sine)
    copies[2].wait()
    for head in range(width // HEAD_SIZE):
        at = slice(head * HEAD_SIZE, (head + 1) * HEAD_SIZE)
        rot_ref[:, at] = turned(k_ref[:, at], cos_ref[...], sin_ref[...])
    copies[3].wait()
    wrap = (rank % 2 == 1) & (rank + 3 >= count)
    rows = pl.ds(pl.multiple_of(jnp.where(wrap, half, 0), half), half)
    near_ref[:, :width] = rot_ref[rows, :]
    near_ref[:, width:] = v_ref[rows, :]
    rows = pl.ds(pl.multiple_of(jnp.where(rank + 2 >= count, half, 0), half), half)
    next_ref[:, :width] = rot_ref[rows, :]
    next_ref[:, width:] = v_ref[rows, :]
    rows = pl.ds(first_begin(rank, half), half)
    begin, late = early_ref.shape[1] - 2 * HEAD_SIZE, slice(width - HEAD_SIZE, width)
    early_ref[:, begin : begin + HEAD_SIZE] = rot_ref[rows, late]
    early_ref[:, begin + HEAD_SIZE :] = v_ref[rows, late]
    copies[4].wait()
    low = q_ref.shape[1] - begin
    for head in range(begin // HEAD_SIZE):
        at = slice(head * HEAD_SIZE, (head + 1) * HEAD_SIZE)
        source = slice(low + head * HEAD_SIZE, low + (head + 1) * HEAD_SIZE)
        early_ref[:, at] = turned(q_ref[rows, source], cos_ref[rows, :], sin_ref[rows, :])


def own_kernel(group, q_ref, k_ref, v_ref, p_ref, cos_ref, sin_ref, out_ref, rot_ref, acc_ref, top_ref, sum_ref):
    rank = lax.axis_index("ctx")
    half = q_ref.shape[0] // 2
    rows = pl.ds(first_begin(rank, half), half)
    biases = tile_biases(half_positions(p_ref, rank, True), [(0, True)])
    for head in range(rot_ref.shape[1] // HEAD_SIZE):
        at, shared, _ = head_slices(head, group, 0)
        query = turned(q_ref[rows, at], cos_ref[rows, :], sin_ref[rows, :])
        rot_ref[:, at] = query
        if head % group == 0:
            key = k_ref[rows, shared]
            value = with_ones(v_ref[rows, shared])
        for low, high in ((0, half // 2), (half // 2, half)):
            part = slice(low, high)
            summed, top, total = begin_state(query[part], [key[:high]], [value[:high]], [biases[0][part, :high]])
            acc_ref[part, at] = summed
            top_ref[part, at] = top
            sum_ref[part, at] = total
            out_ref[part, at] = (summed * (1.0 / total)).astype(BF16)


def first_kernel(count, group, own_ref, rot_ref, kv_ref, p_ref, acc_ref, top_ref, sum_ref, out_ref):
    rank = lax.axis_index("ctx")
    width = kv_ref.shape[1] // 2
    depth = rot_ref.shape[1]
    step = jnp.where(rank % 2 == 1, 1, 3)
    used = waits_for_keys(rank)
    out_ref[:, depth : depth + HEAD_SIZE] = kv_ref[:, width - HEAD_SIZE : width]
    out_ref[:, depth + HEAD_SIZE :] = kv_ref[:, 2 * width - HEAD_SIZE :]

    @pl.when(used)
    def _():
        biases = tile_biases(half_positions(p_ref, rank, True), [(distance(rank, step, count), False)])
        for head in range(depth // HEAD_SIZE):
            at, key_at, value_at = head_slices(head, group, width)
            state = acc_ref[:, at], top_ref[:, at], sum_ref[:, at]
            if head % group == 0:
                value = with_ones(kv_ref[:, value_at])
            out_ref[:, at] = finished(added_tile(*state, rot_ref[:, at], kv_ref[:, key_at], value, *biases))

    @pl.when(jnp.logical_not(used))
    def _():
        out_ref[:, :depth] = own_ref[...]


def early_kernel(count, early_ref, near_ref, p_ref, out_ref):
    rank = lax.axis_index("ctx")
    depth = out_ref.shape[1]
    step = jnp.where(rank % 2 == 1, 1, 3)
    reach = jnp.where(waits_for_keys(rank), distance(rank, step, count), FAR)
    biases = tile_biases(half_positions(p_ref, rank, True), [(0, True), (reach, False)])
    keys, values = [], []
    for ref in (early_ref, near_ref):
        begin = ref.shape[1] - 2 * HEAD_SIZE
        keys.append(ref[:, begin : begin + HEAD_SIZE])
        values.append(with_ones(ref[:, begin + HEAD_SIZE :]))
    for head in range(depth // HEAD_SIZE):
        at = slice(head * HEAD_SIZE, (head + 1) * HEAD_SIZE)
        out_ref[:, at] = finished(begin_state(early_ref[:, at], keys, values, biases))


def second_kernel(
    count, group, q_ref, k_ref, v_ref, p_ref, cos_ref, sin_ref, kv_ref, w_hbm, rot_ref, acc_ref, top_ref, sum_ref, w_ref, sem
):
    copy = pltpu.make_async_copy(w_hbm, w_ref, sem)
    copy.start()
    rank = lax.axis_index("ctx")
    half = q_ref.shape[0] // 2
    width = k_ref.shape[1]
    rows = pl.ds(pl.multiple_of(half - first_begin(rank, half), half), half)
    step = jnp.where(rank % 2 == 1, 1, 3)
    reach = jnp.where(waits_for_keys(rank), FAR, distance(rank, step, count))
    biases = tile_biases(half_positions(p_ref, rank, False), [(0, True), (reach, False)])
    for head in range(q_ref.shape[1] // HEAD_SIZE):
        at, key_at, value_at = head_slices(head, group, width)
        query = turned(q_ref[rows, at], cos_ref[rows, :], sin_ref[rows, :])
        rot_ref[:, at] = query
        keys = [k_ref[rows, key_at], kv_ref[:, key_at]]
        if head % group == 0:
            values = [with_ones(v_ref[rows, key_at]), with_ones(kv_ref[:, value_at])]
        acc_ref[:, at], top_ref[:, at], sum_ref[:, at] = begin_state(query, keys, values, biases)
    copy.wait()


def next_kernel(count, group, rot_ref, kv_ref, p_ref, acc_ref, top_ref, sum_ref, *outs):
    rank = lax.axis_index("ctx")
    width = kv_ref.shape[1] // 2
    biases = tile_biases(half_positions(p_ref, rank, False), [(distance(rank, 2, count), False)])
    for head in range(rot_ref.shape[1] // HEAD_SIZE):
        at, key_at, value_at = head_slices(head, group, width)
        state = acc_ref[:, at], top_ref[:, at], sum_ref[:, at]
        if head % group == 0:
            value = with_ones(kv_ref[:, value_at])
        state = added_tile(*state, rot_ref[:, at], kv_ref[:, key_at], value, *biases)
        for out_ref, entries in zip(outs, state):
            out_ref[:, at] = entries


def third_kernel(count, group, heads, rot_ref, kv_ref, p_ref, acc_ref, top_ref, sum_ref, out_ref):
    rank = lax.axis_index("ctx")
    width = kv_ref.shape[1] // 2
    step = jnp.where(rank % 2 == 1, 3, 1)
    biases = tile_biases(half_positions(p_ref, rank, False), [(distance(rank, step, count), False)])
    for number, head in enumerate(heads):
        at, key_at, value_at = head_slices(head, group, width)
        state = acc_ref[:, at], top_ref[:, at], sum_ref[:, at]
        if number == 0 or head % group == 0:
            value = with_ones(kv_ref[:, value_at])
        state = added_tile(*state, rot_ref[:, at], kv_ref[:, key_at], value, *biases)
        out_ref[:, number * HEAD_SIZE : (number + 1) * HEAD_SIZE] = finished(state)


def dot(left, right):
    return jnp.dot(left, right, preferred_element_type=F32)


TILE = 512
LAST_TILE = 256


def other_rows(w_ref, begin, end):
    depth = w_ref.shape[0] // 2
    base = (1 - lax.axis_index("head")) * depth
    return pl.ds(pl.multiple_of(base + begin, HEAD_SIZE), end - begin)


def project_kernel(
    first_ref, last_ref, got_ref, got_last_ref, second0_ref, second1_ref, second2_ref, w_ref, out_hbm, part_ref, held_ref, sems
):
    rank = lax.axis_index("ctx")
    half, depth = first_ref.shape[0], w_ref.shape[0] // 2
    cut = depth - last_ref.shape[1]
    rows = pl.ds(first_begin(rank, half), half)
    mine = pl.ds(pl.multiple_of(lax.axis_index("head") * depth, depth), depth)
    other = other_rows(w_ref, 0, depth)
    first = jnp.concatenate([first_ref[:, :cut], last_ref[...]], axis=1)
    got = jnp.concatenate([got_ref[:, :cut], got_last_ref[...]], axis=1)
    second = jnp.concatenate([second0_ref[...], second1_ref[...], second2_ref[...]], axis=1)
    stacked = jnp.concatenate([first, second], axis=0)
    copies = []
    for tile in range(w_ref.shape[1] // TILE):
        at = slice(tile * TILE, (tile + 1) * TILE)
        both = dot(stacked, w_ref[mine, at])
        part_ref[:, at] = both[half:]
        held_ref[:, at] = (both[:half] + dot(got, w_ref[other, at])).astype(BF16)
        copies.append(pltpu.make_async_copy(held_ref.at[:, at], out_hbm.at[rows, at], sems.at[tile]))
        copies[-1].start()
    for copy in copies:
        copy.wait()


def add_kernel(begin, got_ref, part_ref, w_ref, out_ref):
    rows = other_rows(w_ref, begin, begin + got_ref.shape[1])
    for start in range(0, w_ref.shape[1], TILE):
        at = slice(start, start + TILE)
        out_ref[:, at] = part_ref[:, at] + dot(got_ref[...], w_ref[rows, at])


def last_kernel(begin, got_ref, part_ref, w_ref, begun_hbm, out_hbm, held_ref, sems):
    del begun_hbm
    rank = lax.axis_index("ctx")
    half, depth = got_ref.shape
    out_rows = pl.ds(pl.multiple_of(half - first_begin(rank, half), half), half)
    rows = other_rows(w_ref, begin, begin + depth)
    copies = []
    for tile in range(w_ref.shape[1] // LAST_TILE):
        at = slice(tile * LAST_TILE, (tile + 1) * LAST_TILE)
        added = dot(got_ref[...], w_ref[rows, at])
        held_ref[:, at] = (part_ref[:, at] + added).astype(BF16)
        copies.append(pltpu.make_async_copy(held_ref.at[:, at], out_hbm.at[out_rows, at], sems.at[tile]))
        copies[-1].start()
    for copy in copies:
        copy.wait()


def shards(queries, keys, values, positions, out_weight):
    number, width = queries.shape
    half = number // 2
    count = lax.axis_size("ctx")
    group = width // keys.shape[1]
    columns = out_weight.shape[1]
    tiles = columns // TILE
    in_hbm = lambda array: pltpu.with_memory_space_constraint(array, pltpu.HBM)
    position_row = positions.reshape(1, number)
    table = np.power(500000.0, -2.0 * np.arange(HEAD_SIZE // 2) / HEAD_SIZE).astype(np.float32)
    frequency = jnp.asarray(np.concatenate([table, table])[None, :])
    shape = jax.ShapeDtypeStruct
    vmem = pl.BlockSpec(memory_space=pltpu.VMEM)
    hbm = pl.BlockSpec(memory_space=pltpu.HBM)
    dma = pltpu.SemaphoreType.DMA

    def call(body, name, ins, outs, flops, nbytes, out_specs=None, scratch=(), aliases={}):
        return pl.pallas_call(
            body,
            name=name,
            in_specs=ins,
            out_shape=outs,
            out_specs=out_specs if out_specs is not None else jax.tree.map(lambda _: vmem, outs),
            scratch_shapes=scratch,
            input_output_aliases=aliases,
            compiler_params=pltpu.CompilerParams(vmem_limit_bytes=32 * MIB),
            cost_estimate=pl.CostEstimate(flops=flops // 1024, bytes_accessed=nbytes // 1024, transcendentals=0),
        )

    def pairs(target_of):
        found = [(source, target_of(source) % count) for source in range(count)]
        assert sorted(target for _, target in found) == list(range(count))
        return found

    def swapped(array):
        return lax.ppermute(array, "head", [(0, 1), (1, 0)])

    kv_shape = shape((half, 2 * keys.shape[1]), BF16)
    table_shape = shape((number, HEAD_SIZE), F32)
    rows_shape, state = shape((half, width), BF16), shape((half, width), F32)
    heads = width // HEAD_SIZE
    cut = heads - group
    some_shape = shape((half, cut * HEAD_SIZE), BF16)
    some_state = shape((half, cut * HEAD_SIZE), F32)
    last_shape = shape((half, group * HEAD_SIZE), BF16)
    early, near, onward, k_rot, v, q, p, cosine, sinus = call(
        functools.partial(keys_kernel, count),
        "rotate_keys",
        [hbm] * 5,
        [shape((half, (group + 2) * HEAD_SIZE), BF16), kv_shape, kv_shape]
        + [shape(keys.shape, BF16)] * 2
        + [shape(queries.shape, BF16), shape((1, number), jnp.int32), table_shape, table_shape],
        4 * MIB,
        4 * MIB,
        scratch=[pltpu.VMEM(keys.shape, BF16), pltpu.VMEM((1, HEAD_SIZE), F32), dma((5,))],
    )(*(in_hbm(array) for array in (keys, values, queries, position_row, frequency)))
    early_got = swapped(early)
    near_got = lax.ppermute(near, "ctx", pairs(lambda r: r + 3 if r % 2 else r + 1))
    own, rot, acc, top, total = call(
        functools.partial(own_kernel, group),
        "own_tiles",
        [vmem] * 6,
        [some_shape, some_shape, some_state, some_state, some_state],
        256 * MIB,
        4 * MIB,
    )(q, k_rot, v, p, cosine, sinus)
    onward, rot = lax.optimization_barrier((onward, rot))
    next_got = lax.ppermute(onward, "ctx", pairs(lambda r: r + 2))
    first = call(
        functools.partial(first_kernel, count, group),
        "first_rows",
        [vmem] * 7,
        shape((half, (cut + 2) * HEAD_SIZE), BF16),
        256 * MIB,
        4 * MIB,
    )(own, rot, near_got, p, acc, top, total)
    first_got = swapped(first)
    q, first = lax.optimization_barrier((q, first))
    rot, *state_now, w = call(
        functools.partial(second_kernel, count, group),
        "second_rows",
        [vmem] * 7 + [hbm],
        [rows_shape, state, state, state, shape(out_weight.shape, BF16)],
        1024 * MIB,
        12 * MIB,
        scratch=[dma(())],
    )(q, k_rot, v, p, cosine, sinus, near_got, in_hbm(out_weight))
    early, rot = lax.optimization_barrier((early, rot))
    attend_early = call(
        functools.partial(early_kernel, count), "early_rows", [vmem] * 3, last_shape, 256 * MIB, 4 * MIB
    )
    last = attend_early(early, first, p)
    rot, next_got, last, early_got = lax.optimization_barrier((rot, next_got, last, early_got))
    last_got = lax.ppermute(next_got, "ctx", pairs(lambda r: r + 1 - 2 * (r % 2)))
    state_now = call(
        functools.partial(next_kernel, count, group),
        "next_tile",
        [vmem] * 6,
        [state, state, state],
        512 * MIB,
        4 * MIB,
        aliases={3: 0, 4: 1, 5: 2},
    )(rot, next_got, p, *state_now)
    parts = range(cut), range(cut, heads - 1), range(heads - 1, heads)
    seconds, seconds_got = [], []
    for part in parts:
        second = call(
            functools.partial(third_kernel, count, group, part),
            "last_tile",
            [vmem] * 6,
            shape((half, len(part) * HEAD_SIZE), BF16),
            256 * MIB,
            4 * MIB,
        )(rot, last_got, p, *state_now)
        seconds_got.append(swapped(second))
        rot, second, first_got = lax.optimization_barrier((rot, second, first_got))
        seconds.append(second)
    sum_shape = shape((half, columns), F32)
    early_got, seconds[-1] = lax.optimization_barrier((early_got, seconds[-1]))
    begun, partial_sum = call(
        project_kernel,
        "project_first",
        [vmem] * 8,
        [shape((number, columns), BF16), sum_shape],
        3072 * MIB,
        8 * MIB,
        out_specs=[hbm, vmem],
        scratch=[pltpu.VMEM((half, columns), BF16), dma((tiles,))],
    )(first, last, first_got, attend_early(early_got, first_got, p), *seconds, w)
    for part, got in zip(parts[:-1], seconds_got):
        partial_sum = call(
            functools.partial(add_kernel, part[0] * HEAD_SIZE),
            "project_second",
            [vmem] * 3,
            sum_shape,
            512 * MIB,
            4 * MIB,
        )(got, partial_sum, w)
    return call(
        functools.partial(last_kernel, parts[-1][0] * HEAD_SIZE),
        "project_last",
        [vmem] * 3 + [hbm],
        shape((number, columns), BF16),
        512 * MIB,
        4 * MIB,
        out_specs=hbm,
        scratch=[pltpu.VMEM((half, columns), BF16), dma((columns // LAST_TILE,))],
        aliases={3: 0},
    )(seconds_got[-1], partial_sum, w, begun)


def solution(mesh):
    in_specs = (P("ctx", "head"), P("ctx", "head"), P("ctx", "head"), P("ctx"), P(None, "head"))
    out_specs = P("ctx", "head")
    return jax.shard_map(shards, mesh=mesh, in_specs=in_specs, out_specs=out_specs, check_vma=False)
```

profile of v0, /device:TPU:0, one launch (start us, length us, event | category | flops | bytes accessed | tf_op | source)
XLA Modules:
  0.0 36.5 jit_solution(10379884667426292079)
XLA Ops:
  0.0 1.6 %rotate_keys.1 = (bf16[256,768]{1,0:T(8,128)(2,1)S(1)}, bf16[256,512]{1,0:T(8,128)(2,1)S(1)}, bf16[256,512]{1,0:T(8,128)(2,1)S(1)}, bf16[512,256]{1,0:T(8,128)(2...) custom-call(bf16[512,256]{1,0:T(8,128)(2,1)} %k_hbm.1, ...), custom_call_target="tpu_custom_call" | custom-call | flops 4096 | bytes 4096 | tf_op jit(solution)/shard_map/rotate_keys/pallas_call | solution.py:396
  1.6 3.0 %collective-permute-start.2 = (bf16[256,768]{1,0:T(8,128)(2,1)S(1)}, bf16[256,768]{1,0:T(8,128)(2,1)S(1)}, u32[]{:S(2)}, u32[]{:S(2)}) collective-permute-start(bf16[256,768]{1,0:T(8,128)(2,1)S(1)} %get-tuple-element.68.early_ref), channel_id=1, source_target_pairs={{0,1},{1,0},{2,3},{3,2},{4,5},{5,4},{6,7},{7,6},{8,9},{9,8},{10,11... | collective-permute-start | bytes 1179656 | tf_op jit(solution)/shard_map/ppermute | solution.py:386
  4.6 0.0 collective-permute-start
  4.6 1.0 %own_tiles.1 = (bf16[256,512]{1,0:T(8,128)(2,1)S(1)}, bf16[256,512]{1,0:T(8,128)(2,1)S(1)}, f32[256,512]{1,0:T(8,128)S(1)}, f32[256,512]{1,0:T(8,128)S(1)}, f32[256,512]{1,0:T(8,128)S(1)}) custom-call(bf16[512,1024]{1,0:T(8,128)(2,1)S(1)} %get-tuple-element.64.q_ref, bf16[512,256]{1,0:T(8,128)(2,1)S(1)} %get-tuple-element.51.k_ref, ...), custom_call_target="tpu_custom_call" | custom-call | flops 262144 | bytes 4096 | tf_op jit(solution)/shard_map/own_tiles/pallas_call | solution.py:409
  5.6 1.6 %collective-permute-start.1 = (bf16[256,512]{1,0:T(8,128)(2,1)S(1)}, bf16[256,512]{1,0:T(8,128)(2,1)S(1)}, u32[]{:S(2)}, u32[]{:S(2)}) collective-permute-start(bf16[256,512]{1,0:T(8,128)(2,1)S(1)} %get-tuple-element.67), channel_id=1, source_target_pairs={{0,4},{2,6},{4,8},{6,10},{8,12},{10,14},{12,16},{14,18},{16,20},{1... | collective-permute-start | bytes 786440 | tf_op jit(solution)/shard_map/ppermute | solution.py:418
  7.2 5.1 %collective-permute-done.kv_ref = bf16[256,512]{1,0:T(8,128)(2,1)S(1)} collective-permute-done((bf16[256,512]{1,0:T(8,128)(2,1)S(1)}, bf16[256,512]{1,0:T(8,128)(2,1)S(1)}, u32[]{:S(2)}, u32[]{:S(2)}) %collective-permute-start) | collective-permute-done | bytes 262176 | tf_op jit(solution)/shard_map/ppermute | solution.py:408
  12.2 0.2 first_rows.1.near_ref.first_ref
  12.5 0.1 collective-permute-start.4
  12.6 3.4 %second_rows.1 = (bf16[256,1024]{1,0:T(8,128)(2,1)S(1)}, f32[256,1024]{1,0:T(8,128)S(1)}, f32[256,1024]{1,0:T(8,128)S(1)}, f32[256,1024]{1,0:T(8,128)S(1)}, bf16[2048,2048]{1,0:T(8,128)(2,1)S(1)}) custom-call(bf16[512,1024]{1,0:T(8,128)(2,1)S(1)} %get-tuple-element.64.q_ref, bf16[512,256]{1,0:T(8,128)(2,1)S(1)} %get-tuple-element.51.k_ref, ...), custom_call_target="tpu_custom_call" | custom-call | flops 1048576 | bytes 12288 | tf_op jit(solution)/shard_map/second_rows/pallas_call | solution.py:429
  16.0 1.1 %early_rows.2.last_ref = bf16[256,512]{1,0:T(8,128)(2,1)S(1)} custom-call(bf16[256,768]{1,0:T(8,128)(2,1)S(1)} %get-tuple-element.68.early_ref, bf16[256,768]{1,0:T(8,128)(2,1)S(1)} %first_rows.1.near_ref.first_ref, s32[1,512]{1,0:T(1,128)S(1)} %get-tuple-element.53.p_ref), custom_call_target="tpu_custom_call" | custom-call | flops 262144 | bytes 4096 | tf_op jit(solution)/shard_map/early_rows/pallas_call | solution.py:442
  17.1 0.5 %collective-permute-done.1.kv_ref = bf16[256,512]{1,0:T(8,128)(2,1)S(1)} collective-permute-done((bf16[256,512]{1,0:T(8,128)(2,1)S(1)}, bf16[256,512]{1,0:T(8,128)(2,1)S(1)}, u32[]{:S(2)}, u32[]{:S(2)}) %collective-permute-start.1) | collective-permute-done | bytes 262176 | tf_op jit(solution)/shard_map/ppermute | solution.py:418
  17.6 0.0 collective-permute-done.2.early_ref
  17.6 1.0 %collective-permute-start.3 = (bf16[256,512]{1,0:T(8,128)(2,1)S(1)}, bf16[256,512]{1,0:T(8,128)(2,1)S(1)}, u32[]{:S(2)}, u32[]{:S(2)}) collective-permute-start(bf16[256,512]{1,0:T(8,128)(2,1)S(1)} %collective-permute-done.1.kv_ref), channel_id=1, source_target_pairs={{0,2},{2,0},{4,6},{6,4},{8,10},{10,8},{12,14},{14,12},{16,18},{18,... | collective-permute-start | bytes 786440 | tf_op jit(solution)/shard_map/ppermute | solution.py:444
  18.6 1.7 %next_tile.1 = (f32[256,1024]{1,0:T(8,128)S(1)}, f32[256,1024]{1,0:T(8,128)S(1)}, f32[256,1024]{1,0:T(8,128)S(1)}) custom-call(bf16[256,1024]{1,0:T(8,128)(2,1)S(1)} %get-tuple-element.80.rot_ref, bf16[256,512]{1,0:T(8,128)(2,1)S(1)} %collective-permute-done.1.kv_ref, ...), custom_call_target="tpu_custom_call", output_to_operand_aliasing={{0}: (3, {}), {1}: (4, {}), {2}: (5, {})} | custom-call | flops 524288 | bytes 4096 | tf_op jit(solution)/shard_map/next_tile/pallas_call | solution.py:445
  20.4 0.0 collective-permute-done.3.kv_ref
  20.4 0.8 %last_tile.3.second0_ref = bf16[256,512]{1,0:T(8,128)(2,1)S(1)} custom-call(bf16[256,1024]{1,0:T(8,128)(2,1)S(1)} %get-tuple-element.80.rot_ref, bf16[256,512]{1,0:T(8,128)(2,1)S(1)} %collective-permute-done.3.kv_ref, s32[1,512]{1,0:T(1,128)S(1)} %get-tuple-element.53.p_ref, f32[256,1024]{1,0:T(8,128)S(1)} %get-tuple-element.75.acc_ref, ...), custom_call_target="tpu_custom_call" | custom-call | flops 262144 | bytes 4096 | tf_op jit(solution)/shard_map/last_tile/pallas_call | solution.py:457
  21.2 0.6 %collective-permute-start.7 = (bf16[256,512]{1,0:T(8,128)(2,1)S(1)}, bf16[256,512]{1,0:T(8,128)(2,1)S(1)}, u32[]{:S(2)}, u32[]{:S(2)}) collective-permute-start(bf16[256,512]{1,0:T(8,128)(2,1)S(1)} %last_tile.3.second0_ref), channel_id=1, source_target_pairs={{0,1},{1,0},{2,3},{3,2},{4,5},{5,4},{6,7},{7,6},{8,9},{9,8},{10,11... | collective-permute-start | bytes 786440 | tf_op jit(solution)/shard_map/ppermute | solution.py:386
  21.8 0.4 %collective-permute-done.4.near_ref.got_ref = bf16[256,768]{1,0:T(8,128)(2,1)S(1)} collective-permute-done((bf16[256,768]{1,0:T(8,128)(2,1)S(1)}, bf16[256,768]{1,0:T(8,128)(2,1)S(1)}, u32[]{:S(2)}, u32[]{:S(2)}) %collective-permute-start.4) | collective-permute-done | bytes 393248 | tf_op jit(solution)/shard_map/ppermute | solution.py:386
  22.2 0.7 %last_tile.4.second1_ref = bf16[256,384]{1,0:T(8,128)(2,1)S(1)} custom-call(bf16[256,1024]{1,0:T(8,128)(2,1)S(1)} %get-tuple-element.80.rot_ref, bf16[256,512]{1,0:T(8,128)(2,1)S(1)} %collective-permute-done.3.kv_ref, s32[1,512]{1,0:T(1,128)S(1)} %get-tuple-element.53.p_ref, f32[256,1024]{1,0:T(8,128)S(1)} %get-tuple-element.75.acc_ref, ...), custom_call_target="tpu_custom_call" | custom-call | flops 262144 | bytes 4096 | tf_op jit(solution)/shard_map/last_tile/pallas_call | solution.py:457
  22.9 1.8 %collective-permute-start.6 = (bf16[256,384]{1,0:T(8,128)(2,1)S(1)}, bf16[256,384]{1,0:T(8,128)(2,1)S(1)}, u32[]{:S(2)}, u32[]{:S(2)}) collective-permute-start(bf16[256,384]{1,0:T(8,128)(2,1)S(1)} %last_tile.4.second1_ref), channel_id=1, source_target_pairs={{0,1},{1,0},{2,3},{3,2},{4,5},{5,4},{6,7},{7,6},{8,9},{9,8},{10,11... | collective-permute-start | bytes 589832 | tf_op jit(solution)/shard_map/ppermute | solution.py:386
  24.7 0.5 %last_tile.5.second2_ref = bf16[256,128]{1,0:T(8,128)(2,1)S(1)} custom-call(bf16[256,1024]{1,0:T(8,128)(2,1)S(1)} %get-tuple-element.80.rot_ref, bf16[256,512]{1,0:T(8,128)(2,1)S(1)} %collective-permute-done.3.kv_ref, s32[1,512]{1,0:T(1,128)S(1)} %get-tuple-element.53.p_ref, f32[256,1024]{1,0:T(8,128)S(1)} %get-tuple-element.75.acc_ref, ...), custom_call_target="tpu_custom_call" | custom-call | flops 262144 | bytes 4096 | tf_op jit(solution)/shard_map/last_tile/pallas_call | solution.py:457
  25.2 0.4 collective-permute-start.5
  25.5 1.1 %early_rows.3.got_last_ref = bf16[256,512]{1,0:T(8,128)(2,1)S(1)} custom-call(bf16[256,768]{1,0:T(8,128)(2,1)S(1)} %collective-permute-done.2.early_ref, bf16[256,768]{1,0:T(8,128)(2,1)S(1)} %collective-permute-done.4.near_ref.got_ref, s32[1,512]{1,0:T(1,128)S(1)} %get-tuple-element.53.p_ref), custom_call_target="tpu_custom_call" | custom-call | flops 262144 | bytes 4096 | tf_op jit(solution)/shard_map/early_rows/pallas_call | solution.py:479
  26.7 4.2 %project_first.1 = (bf16[512,2048]{1,0:T(8,128)(2,1)}, f32[256,2048]{1,0:T(8,128)S(1)}) custom-call(bf16[256,768]{1,0:T(8,128)(2,1)S(1)} %first_rows.1.near_ref.first_ref, bf16[256,512]{1,0:T(8,128)(2,1)S(1)} %early_rows.2.last_ref, bf16[256,768]{1,0:T(8,128)(2,1)S(1)} %collective-permute-done.4.near_ref.got_ref, ...), custom_call_target="tpu_custom_call" | custom-call | flops 3145728 | bytes 8192 | tf_op jit(solution)/shard_map/project_first/pallas_call | solution.py:470
  30.9 0.0 collective-permute-done.7.got_ref
  30.9 0.7 %project_second.2.part_ref = f32[256,2048]{1,0:T(8,128)S(1)} custom-call(bf16[256,512]{1,0:T(8,128)(2,1)S(1)} %collective-permute-done.7.got_ref, f32[256,2048]{1,0:T(8,128)S(1)} %get-tuple-element.91.part_ref, bf16[2048,2048]{1,0:T(8,128)(2,1)S(1)} %get-tuple-element.90.w_ref), custom_call_target="tpu_custom_call" | custom-call | flops 524288 | bytes 4096 | tf_op jit(solution)/shard_map/project_second/pallas_call | solution.py:481
  31.7 2.7 %collective-permute-done.6.got_ref = bf16[256,384]{1,0:T(8,128)(2,1)S(1)} collective-permute-done((bf16[256,384]{1,0:T(8,128)(2,1)S(1)}, bf16[256,384]{1,0:T(8,128)(2,1)S(1)}, u32[]{:S(2)}, u32[]{:S(2)}) %collective-permute-start.6) | collective-permute-done | bytes 196640 | tf_op jit(solution)/shard_map/ppermute | solution.py:386
  34.4 0.7 %project_second.3.part_ref = f32[256,2048]{1,0:T(8,128)S(1)} custom-call(bf16[256,384]{1,0:T(8,128)(2,1)S(1)} %collective-permute-done.6.got_ref, f32[256,2048]{1,0:T(8,128)S(1)} %project_second.2.part_ref, bf16[2048,2048]{1,0:T(8,128)(2,1)S(1)} %get-tuple-element.90.w_ref), custom_call_target="tpu_custom_call" | custom-call | flops 524288 | bytes 4096 | tf_op jit(solution)/shard_map/project_second/pallas_call | solution.py:481
  35.1 0.0 collective-permute-done.5.got_ref
  35.1 1.3 %project_last.1 = bf16[512,2048]{1,0:T(8,128)(2,1)} custom-call(bf16[256,128]{1,0:T(8,128)(2,1)S(1)} %collective-permute-done.5.got_ref, f32[256,2048]{1,0:T(8,128)S(1)} %project_second.3.part_ref, bf16[2048,2048]{1,0:T(8,128)(2,1)S(1)} %get-tuple-element.90.w_ref, bf16[512,2048]{1,0:T(8,128)(2,1)} %get-tuple-element.92.begun_hbm), custom_call_target="tpu_custom_call", output_to_operand_aliasing={{}: (3, {})} | custom-call | flops 524288 | bytes 4096 | tf_op jit(solution)/shard_map/project_last/pallas_call | solution.py:489
Async XLA Ops:
  1.6 16.0 %collective-permute-start.2 = (bf16[256,768]{1,0:T(8,128)(2,1)S(1)}, bf16[256,768]{1,0:T(8,128)(2,1)S(1)}, u32[]{:S(2)}, u32[]{:S(2)}) collective-permute-start(bf16[256,768]{1,0:T(8,128)(2,1)S(1)} %get-tuple-element.68.early_ref), channel_id=1, source_target_pairs={{0,1},{1,0},{2,3},{3,2},{4,5},{5,4},{6,7},{7,6},{8,9},{9,8},{10,11... | collective-permute-start | bytes 1179656 | tf_op jit(solution)/shard_map/ppermute | solution.py:386
  4.6 7.6 %collective-permute-start = (bf16[256,512]{1,0:T(8,128)(2,1)S(1)}, bf16[256,512]{1,0:T(8,128)(2,1)S(1)}, u32[]{:S(2)}, u32[]{:S(2)}) collective-permute-start(bf16[256,512]{1,0:T(8,128)(2,1)S(1)} %get-tuple-element.60), channel_id=1, source_target_pairs={{0,2},{2,8},{4,6},{6,12},{8,10},{10,16},{12,14},{14,20},{16,18},{1... | collective-permute-start | bytes 786440 | tf_op jit(solution)/shard_map/ppermute | solution.py:408
  5.6 12.0 %collective-permute-start.1 = (bf16[256,512]{1,0:T(8,128)(2,1)S(1)}, bf16[256,512]{1,0:T(8,128)(2,1)S(1)}, u32[]{:S(2)}, u32[]{:S(2)}) collective-permute-start(bf16[256,512]{1,0:T(8,128)(2,1)S(1)} %get-tuple-element.67), channel_id=1, source_target_pairs={{0,4},{2,6},{4,8},{6,10},{8,12},{10,14},{12,16},{14,18},{16,20},{1... | collective-permute-start | bytes 786440 | tf_op jit(solution)/shard_map/ppermute | solution.py:418
  12.5 9.7 %collective-permute-start.4 = (bf16[256,768]{1,0:T(8,128)(2,1)S(1)}, bf16[256,768]{1,0:T(8,128)(2,1)S(1)}, u32[]{:S(2)}, u32[]{:S(2)}) collective-permute-start(bf16[256,768]{1,0:T(8,128)(2,1)S(1)} %first_rows.1.near_ref.first_ref), channel_id=1, source_target_pairs={{0,1},{1,0},{2,3},{3,2},{4,5},{5,4},{6,7},{7,6},{8,9},{9,8},{10,11... | collective-permute-start | bytes 1179656 | tf_op jit(solution)/shard_map/ppermute | solution.py:386
  17.6 2.8 %collective-permute-start.3 = (bf16[256,512]{1,0:T(8,128)(2,1)S(1)}, bf16[256,512]{1,0:T(8,128)(2,1)S(1)}, u32[]{:S(2)}, u32[]{:S(2)}) collective-permute-start(bf16[256,512]{1,0:T(8,128)(2,1)S(1)} %collective-permute-done.1.kv_ref), channel_id=1, source_target_pairs={{0,2},{2,0},{4,6},{6,4},{8,10},{10,8},{12,14},{14,12},{16,18},{18,... | collective-permute-start | bytes 786440 | tf_op jit(solution)/shard_map/ppermute | solution.py:444
  21.2 9.8 %collective-permute-start.7 = (bf16[256,512]{1,0:T(8,128)(2,1)S(1)}, bf16[256,512]{1,0:T(8,128)(2,1)S(1)}, u32[]{:S(2)}, u32[]{:S(2)}) collective-permute-start(bf16[256,512]{1,0:T(8,128)(2,1)S(1)} %last_tile.3.second0_ref), channel_id=1, source_target_pairs={{0,1},{1,0},{2,3},{3,2},{4,5},{5,4},{6,7},{7,6},{8,9},{9,8},{10,11... | collective-permute-start | bytes 786440 | tf_op jit(solution)/shard_map/ppermute | solution.py:386
  22.9 11.5 %collective-permute-start.6 = (bf16[256,384]{1,0:T(8,128)(2,1)S(1)}, bf16[256,384]{1,0:T(8,128)(2,1)S(1)}, u32[]{:S(2)}, u32[]{:S(2)}) collective-permute-start(bf16[256,384]{1,0:T(8,128)(2,1)S(1)} %last_tile.4.second1_ref), channel_id=1, source_target_pairs={{0,1},{1,0},{2,3},{3,2},{4,5},{5,4},{6,7},{7,6},{8,9},{9,8},{10,11... | collective-permute-start | bytes 589832 | tf_op jit(solution)/shard_map/ppermute | solution.py:386
  25.2 9.9 %collective-permute-start.5 = (bf16[256,128]{1,0:T(8,128)(2,1)S(1)}, bf16[256,128]{1,0:T(8,128)(2,1)S(1)}, u32[]{:S(2)}, u32[]{:S(2)}) collective-permute-start(bf16[256,128]{1,0:T(8,128)(2,1)S(1)} %last_tile.5.second2_ref), channel_id=1, source_target_pairs={{0,1},{1,0},{2,3},{3,2},{4,5},{5,4},{6,7},{7,6},{8,9},{9,8},{10,11... | collective-permute-start | bytes 196616 | tf_op jit(solution)/shard_map/ppermute | solution.py:386
where the time goes:
time: 36.9 us; the launch traced here: 36.5 us
  Pallas kernels  19.1 us (52%)
  waiting for transfers between devices  8.6 us (23%)
  starting transfers between devices  8.53 us (23%)
    ppermute x5, starting transfers between devices, swapped(): return lax.ppermute(array, 'head', [(0, 1), (1, 0)])  5.93 us
    ppermute x1, waiting for transfers between devices, shards(): lax.ppermute(near, 'ctx', pairs(lambda r: r + 3 if r % 2 else r + 1))  5.05 us
    pallas_call x1, Pallas kernels, shards(): call(project_kernel, 'project_first', [vmem] * 8, [shape((number, columns...  4.24 us
    pallas_call x1, Pallas kernels, shards(): call(functools.partial(second_kernel, count, group), 'second_rows', [vmem...  3.39 us
    ppermute x5, waiting for transfers between devices, swapped(): return lax.ppermute(array, 'head', [(0, 1), (1, 0)])  3.09 us
    pallas_call x3, Pallas kernels, shards(): call(functools.partial(third_kernel, count, group, part), 'last_tile', [v...  1.95 us
    pallas_call x1, Pallas kernels, shards(): call(functools.partial(next_kernel, count, group), 'next_tile', [vmem] *...  1.73 us
    pallas_call x1, Pallas kernels, shards(): call(functools.partial(keys_kernel, count), 'rotate_keys', [hbm] * 5, [sh...  1.63 us
  transfers between devices with their start and end apart: 8, of which 4 were waited for; matrix products, arithmetic and copies ran while one was open for 0% of the time, Pallas kernels for 44%

commit v1 on v0

--- a/solution.py
+++ b/solution.py
@@ -125,7 +125,7 @@
 
 
 def keys_kernel(
-    count, k_hbm, v_hbm, q_hbm, p_hbm, f_hbm, early_ref, near_ref, next_ref, rot_ref, v_ref, q_ref, p_ref, cos_ref, sin_ref,
+    count, k_hbm, v_hbm, q_hbm, p_hbm, f_hbm, near_ref, next_ref, rot_ref, v_ref, q_ref, p_ref, cos_ref, sin_ref,
     k_ref, f_ref, sems,
 ):
     pairs = ((p_hbm, p_ref), (f_hbm, f_ref), (k_hbm, k_ref), (v_hbm, v_ref), (q_hbm, q_ref))
@@ -161,16 +161,21 @@
     rows = pl.ds(pl.multiple_of(jnp.where(rank + 2 >= count, half, 0), half), half)
     next_ref[:, :width] = rot_ref[rows, :]
     next_ref[:, width:] = v_ref[rows, :]
+    copies[4].wait()
+
+
+def pack_kernel(q_ref, k_ref, v_ref, cos_ref, sin_ref, out_ref):
+    rank = lax.axis_index("ctx")
+    half, width = out_ref.shape[0], k_ref.shape[1]
     rows = pl.ds(first_begin(rank, half), half)
-    begin, late = early_ref.shape[1] - 2 * HEAD_SIZE, slice(width - HEAD_SIZE, width)
-    early_ref[:, begin : begin + HEAD_SIZE] = rot_ref[rows, late]
-    early_ref[:, begin + HEAD_SIZE :] = v_ref[rows, late]
-    copies[4].wait()
+    begin, late = out_ref.shape[1] - 2 * HEAD_SIZE, slice(width - HEAD_SIZE, width)
+    out_ref[:, begin : begin + HEAD_SIZE] = k_ref[rows, late]
+    out_ref[:, begin + HEAD_SIZE :] = v_ref[rows, late]
     low = q_ref.shape[1] - begin
     for head in range(begin // HEAD_SIZE):
         at = slice(head * HEAD_SIZE, (head + 1) * HEAD_SIZE)
         source = slice(low + head * HEAD_SIZE, low + (head + 1) * HEAD_SIZE)
-        early_ref[:, at] = turned(q_ref[rows, source], cos_ref[rows, :], sin_ref[rows, :])
+        out_ref[:, at] = turned(q_ref[rows, source], cos_ref[rows, :], sin_ref[rows, :])
 
 
 def own_kernel(group, q_ref, k_ref, v_ref, p_ref, cos_ref, sin_ref, out_ref, rot_ref, acc_ref, top_ref, sum_ref):
@@ -374,7 +379,7 @@
             scratch_shapes=scratch,
             input_output_aliases=aliases,
             compiler_params=pltpu.CompilerParams(vmem_limit_bytes=32 * MIB),
-            cost_estimate=pl.CostEstimate(flops=flops // 1024, bytes_accessed=nbytes // 1024, transcendentals=0),
+            cost_estimate=pl.CostEstimate(flops=flops, bytes_accessed=nbytes, transcendentals=0),
         )
 
     def pairs(target_of):
@@ -393,19 +398,23 @@
     some_shape = shape((half, cut * HEAD_SIZE), BF16)
     some_state = shape((half, cut * HEAD_SIZE), F32)
     last_shape = shape((half, group * HEAD_SIZE), BF16)
-    early, near, onward, k_rot, v, q, p, cosine, sinus = call(
+    near, onward, k_rot, v, q, p, cosine, sinus = call(
         functools.partial(keys_kernel, count),
         "rotate_keys",
         [hbm] * 5,
-        [shape((half, (group + 2) * HEAD_SIZE), BF16), kv_shape, kv_shape]
+        [kv_shape, kv_shape]
         + [shape(keys.shape, BF16)] * 2
         + [shape(queries.shape, BF16), shape((1, number), jnp.int32), table_shape, table_shape],
         4 * MIB,
         4 * MIB,
         scratch=[pltpu.VMEM(keys.shape, BF16), pltpu.VMEM((1, HEAD_SIZE), F32), dma((5,))],
     )(*(in_hbm(array) for array in (keys, values, queries, position_row, frequency)))
+    near_got = lax.ppermute(near, "ctx", pairs(lambda r: r + 3 if r % 2 else r + 1))
+    early = call(pack_kernel, "pack_early", [vmem] * 5, shape((half, (group + 2) * HEAD_SIZE), BF16), MIB, MIB)(
+        q, k_rot, v, cosine, sinus
+    )
+    early, q = lax.optimization_barrier((early, q))
     early_got = swapped(early)
-    near_got = lax.ppermute(near, "ctx", pairs(lambda r: r + 3 if r % 2 else r + 1))
     own, rot, acc, top, total = call(
         functools.partial(own_kernel, group),
         "own_tiles",

time: 36.9 us -> 36 us (0.976)
  waiting for transfers between devices: 8.6 us -> 6.29 us
  starting transfers between devices: 8.53 us -> 10.2 us
    ppermute x1, waiting for transfers between devices: 5.05 us -> 2.77 us  [shards(): lax.ppermute(near, 'ctx', pairs(lambda r: r + 3 if r % 2 else r + 1))]
    ppermute x5, starting transfers between devices: 5.93 us -> 7.92 us  [swapped(): return lax.ppermute(array, 'head', [(0, 1), (1, 0)])]
    ppermute x1, starting transfers between devices: 1.03 us -> 0.16 us  [shards(): lax.ppermute(next_got, 'ctx', pairs(lambda r: r + 1 - 2 * (r % 2)))]
    ppermute x1, starting transfers between devices: 0.01 us -> 0.5 us  [shards(): lax.ppermute(near, 'ctx', pairs(lambda r: r + 3 if r % 2 else r + 1))]
    pallas_call x1 -> x2, Pallas kernels: 1.63 us -> 1.66 us  [the longest x1 1.46 us: shards(): call(functools.partial(keys_kernel, count), 'rotate_keys', [hbm] * 5, [kv...]
  transfers between devices with their start and end apart: 8 -> 8, of which waited for: 4 -> 5; matrix products, arithmetic and copies ran while one was open for 0% -> 0% of each run, Pallas kernels for 44% -> 46%
where the time goes in v1:
time: 36 us; the launch traced here: 35.8 us
  Pallas kernels  19.1 us (53%)
  starting transfers between devices  10.2 us (28%)
  waiting for transfers between devices  6.29 us (17%)
    ppermute x5, starting transfers between devices, swapped(): return lax.ppermute(array, 'head', [(0, 1), (1, 0)])  7.92 us
    pallas_call x1, Pallas kernels, shards(): call(project_kernel, 'project_first', [vmem] * 8, [shape((number, columns...  4.21 us
    pallas_call x1, Pallas kernels, shards(): call(functools.partial(second_kernel, count, group), 'second_rows', [vmem...  3.39 us
    ppermute x5, waiting for transfers between devices, swapped(): return lax.ppermute(array, 'head', [(0, 1), (1, 0)])  3.06 us
    ppermute x1, waiting for transfers between devices, shards(): lax.ppermute(near, 'ctx', pairs(lambda r: r + 3 if r % 2 else r + 1))  2.77 us
    pallas_call x3, Pallas kernels, shards(): call(functools.partial(third_kernel, count, group, part), 'last_tile', [v...  1.95 us
    pallas_call x1, Pallas kernels, shards(): call(functools.partial(next_kernel, count, group), 'next_tile', [vmem] *...  1.73 us
    ppermute x1, starting transfers between devices, shards(): next_got = lax.ppermute(onward, 'ctx', pairs(lambda r: r + 2))  1.57 us
  transfers between devices with their start and end apart: 8, of which 5 were waited for; matrix products, arithmetic and copies ran while one was open for 0% of the time, Pallas kernels for 46%

profile of v1, /device:TPU:0, one launch (start us, length us, event | category | flops | bytes accessed | tf_op | source)
XLA Modules:
  0.0 35.8 jit_solution(15853501575207424133)
XLA Ops:
  0.0 1.5 %rotate_keys.1 = (bf16[256,512]{1,0:T(8,128)(2,1)S(1)}, bf16[256,512]{1,0:T(8,128)(2,1)S(1)}, bf16[512,256]{1,0:T(8,128)(2,1)S(1)}, bf16[512,256]{1,0:T(8,128)(2...) custom-call(bf16[512,256]{1,0:T(8,128)(2,1)} %k_hbm.1, ...), custom_call_target="tpu_custom_call" | custom-call | flops 4194304 | bytes 4194304 | tf_op jit(solution)/shard_map/rotate_keys/pallas_call | solution.py:401
  1.5 0.5 %collective-permute-start = (bf16[256,512]{1,0:T(8,128)(2,1)S(1)}, bf16[256,512]{1,0:T(8,128)(2,1)S(1)}, u32[]{:S(2)}, u32[]{:S(2)}) collective-permute-start(bf16[256,512]{1,0:T(8,128)(2,1)S(1)} %get-tuple-element.62), channel_id=1, source_target_pairs={{0,2},{2,8},{4,6},{6,12},{8,10},{10,16},{12,14},{14,20},{16,18},{1... | collective-permute-start | bytes 786440 | tf_op jit(solution)/shard_map/ppermute | solution.py:412
  2.0 0.2 pack_early.1.early_ref
  2.2 2.6 %collective-permute-start.2 = (bf16[256,768]{1,0:T(8,128)(2,1)S(1)}, bf16[256,768]{1,0:T(8,128)(2,1)S(1)}, u32[]{:S(2)}, u32[]{:S(2)}) collective-permute-start(bf16[256,768]{1,0:T(8,128)(2,1)S(1)} %pack_early.1.early_ref), channel_id=1, source_target_pairs={{0,1},{1,0},{2,3},{3,2},{4,5},{5,4},{6,7},{7,6},{8,9},{9,8},{10,11... | collective-permute-start | bytes 1179656 | tf_op jit(solution)/shard_map/ppermute | solution.py:391
  4.8 1.0 %own_tiles.1 = (bf16[256,512]{1,0:T(8,128)(2,1)S(1)}, bf16[256,512]{1,0:T(8,128)(2,1)S(1)}, f32[256,512]{1,0:T(8,128)S(1)}, f32[256,512]{1,0:T(8,128)S(1)}, f32[256,512]{1,0:T(8,128)S(1)}) custom-call(bf16[512,1024]{1,0:T(8,128)(2,1)S(1)} %get-tuple-element.66.q_ref, bf16[512,256]{1,0:T(8,128)(2,1)S(1)} %get-tuple-element.51.k_ref, ...), custom_call_target="tpu_custom_call" | custom-call | flops 268435456 | bytes 4194304 | tf_op jit(solution)/shard_map/own_tiles/pallas_call | solution.py:418
  5.7 1.6 %collective-permute-start.1 = (bf16[256,512]{1,0:T(8,128)(2,1)S(1)}, bf16[256,512]{1,0:T(8,128)(2,1)S(1)}, u32[]{:S(2)}, u32[]{:S(2)}) collective-permute-start(bf16[256,512]{1,0:T(8,128)(2,1)S(1)} %get-tuple-element.69), channel_id=1, source_target_pairs={{0,4},{2,6},{4,8},{6,10},{8,12},{10,14},{12,16},{14,18},{16,20},{1... | collective-permute-start | bytes 786440 | tf_op jit(solution)/shard_map/ppermute | solution.py:427
  7.3 2.8 %collective-permute-done.kv_ref = bf16[256,512]{1,0:T(8,128)(2,1)S(1)} collective-permute-done((bf16[256,512]{1,0:T(8,128)(2,1)S(1)}, bf16[256,512]{1,0:T(8,128)(2,1)S(1)}, u32[]{:S(2)}, u32[]{:S(2)}) %collective-permute-start) | collective-permute-done | bytes 262176 | tf_op jit(solution)/shard_map/ppermute | solution.py:412
  10.1 0.2 first_rows.1.near_ref.first_ref
  10.3 2.1 %collective-permute-start.4 = (bf16[256,768]{1,0:T(8,128)(2,1)S(1)}, bf16[256,768]{1,0:T(8,128)(2,1)S(1)}, u32[]{:S(2)}, u32[]{:S(2)}) collective-permute-start(bf16[256,768]{1,0:T(8,128)(2,1)S(1)} %first_rows.1.near_ref.first_ref), channel_id=1, source_target_pairs={{0,1},{1,0},{2,3},{3,2},{4,5},{5,4},{6,7},{7,6},{8,9},{9,8},{10,11... | collective-permute-start | bytes 1179656 | tf_op jit(solution)/shard_map/ppermute | solution.py:391
  12.3 3.4 %second_rows.1 = (bf16[256,1024]{1,0:T(8,128)(2,1)S(1)}, f32[256,1024]{1,0:T(8,128)S(1)}, f32[256,1024]{1,0:T(8,128)S(1)}, f32[256,1024]{1,0:T(8,128)S(1)}, bf16[2048,2048]{1,0:T(8,128)(2,1)S(1)}) custom-call(bf16[512,1024]{1,0:T(8,128)(2,1)S(1)} %get-tuple-element.66.q_ref, bf16[512,256]{1,0:T(8,128)(2,1)S(1)} %get-tuple-element.51.k_ref, ...), custom_call_target="tpu_custom_call" | custom-call | flops 1073741824 | bytes 12582912 | tf_op jit(solution)/shard_map/second_rows/pallas_call | solution.py:438
  15.7 1.1 %early_rows.2.last_ref = bf16[256,512]{1,0:T(8,128)(2,1)S(1)} custom-call(bf16[256,768]{1,0:T(8,128)(2,1)S(1)} %pack_early.1.early_ref, bf16[256,768]{1,0:T(8,128)(2,1)S(1)} %first_rows.1.near_ref.first_ref, s32[1,512]{1,0:T(1,128)S(1)} %get-tuple-element.57.p_ref), custom_call_target="tpu_custom_call" | custom-call | flops 268435456 | bytes 4194304 | tf_op jit(solution)/shard_map/early_rows/pallas_call | solution.py:451
  16.9 0.5 %collective-permute-done.1.kv_ref = bf16[256,512]{1,0:T(8,128)(2,1)S(1)} collective-permute-done((bf16[256,512]{1,0:T(8,128)(2,1)S(1)}, bf16[256,512]{1,0:T(8,128)(2,1)S(1)}, u32[]{:S(2)}, u32[]{:S(2)}) %collective-permute-start.1) | collective-permute-done | bytes 262176 | tf_op jit(solution)/shard_map/ppermute | solution.py:427
  17.3 0.0 collective-permute-done.2.early_ref
  17.3 0.2 collective-permute-start.3
  17.5 1.7 %next_tile.1 = (f32[256,1024]{1,0:T(8,128)S(1)}, f32[256,1024]{1,0:T(8,128)S(1)}, f32[256,1024]{1,0:T(8,128)S(1)}) custom-call(bf16[256,1024]{1,0:T(8,128)(2,1)S(1)} %get-tuple-element.82.rot_ref, bf16[256,512]{1,0:T(8,128)(2,1)S(1)} %collective-permute-done.1.kv_ref, ...), custom_call_target="tpu_custom_call", output_to_operand_aliasing={{0}: (3, {}), {1}: (4, {}), {2}: (5, {})} | custom-call | flops 536870912 | bytes 4194304 | tf_op jit(solution)/shard_map/next_tile/pallas_call | solution.py:454
  19.2 0.0 collective-permute-done.3.kv_ref
  19.2 0.8 %last_tile.3.second0_ref = bf16[256,512]{1,0:T(8,128)(2,1)S(1)} custom-call(bf16[256,1024]{1,0:T(8,128)(2,1)S(1)} %get-tuple-element.82.rot_ref, bf16[256,512]{1,0:T(8,128)(2,1)S(1)} %collective-permute-done.3.kv_ref, s32[1,512]{1,0:T(1,128)S(1)} %get-tuple-element.57.p_ref, f32[256,1024]{1,0:T(8,128)S(1)} %get-tuple-element.77.acc_ref, ...), custom_call_target="tpu_custom_call" | custom-call | flops 268435456 | bytes 4194304 | tf_op jit(solution)/shard_map/last_tile/pallas_call | solution.py:466
  20.0 1.0 %collective-permute-start.7 = (bf16[256,512]{1,0:T(8,128)(2,1)S(1)}, bf16[256,512]{1,0:T(8,128)(2,1)S(1)}, u32[]{:S(2)}, u32[]{:S(2)}) collective-permute-start(bf16[256,512]{1,0:T(8,128)(2,1)S(1)} %last_tile.3.second0_ref), channel_id=1, source_target_pairs={{0,1},{1,0},{2,3},{3,2},{4,5},{5,4},{6,7},{7,6},{8,9},{9,8},{10,11... | collective-permute-start | bytes 786440 | tf_op jit(solution)/shard_map/ppermute | solution.py:391
  21.0 1.4 %collective-permute-done.4.near_ref.got_ref = bf16[256,768]{1,0:T(8,128)(2,1)S(1)} collective-permute-done((bf16[256,768]{1,0:T(8,128)(2,1)S(1)}, bf16[256,768]{1,0:T(8,128)(2,1)S(1)}, u32[]{:S(2)}, u32[]{:S(2)}) %collective-permute-start.4) | collective-permute-done | bytes 393248 | tf_op jit(solution)/shard_map/ppermute | solution.py:391
  22.4 0.7 %last_tile.4.second1_ref = bf16[256,384]{1,0:T(8,128)(2,1)S(1)} custom-call(bf16[256,1024]{1,0:T(8,128)(2,1)S(1)} %get-tuple-element.82.rot_ref, bf16[256,512]{1,0:T(8,128)(2,1)S(1)} %collective-permute-done.3.kv_ref, s32[1,512]{1,0:T(1,128)S(1)} %get-tuple-element.57.p_ref, f32[256,1024]{1,0:T(8,128)S(1)} %get-tuple-element.77.acc_ref, ...), custom_call_target="tpu_custom_call" | custom-call | flops 268435456 | bytes 4194304 | tf_op jit(solution)/shard_map/last_tile/pallas_call | solution.py:466
  23.1 2.2 %collective-permute-start.6 = (bf16[256,384]{1,0:T(8,128)(2,1)S(1)}, bf16[256,384]{1,0:T(8,128)(2,1)S(1)}, u32[]{:S(2)}, u32[]{:S(2)}) collective-permute-start(bf16[256,384]{1,0:T(8,128)(2,1)S(1)} %last_tile.4.second1_ref), channel_id=1, source_target_pairs={{0,1},{1,0},{2,3},{3,2},{4,5},{5,4},{6,7},{7,6},{8,9},{9,8},{10,11... | collective-permute-start | bytes 589832 | tf_op jit(solution)/shard_map/ppermute | solution.py:391
  25.3 0.5 %last_tile.5.second2_ref = bf16[256,128]{1,0:T(8,128)(2,1)S(1)} custom-call(bf16[256,1024]{1,0:T(8,128)(2,1)S(1)} %get-tuple-element.82.rot_ref, bf16[256,512]{1,0:T(8,128)(2,1)S(1)} %collective-permute-done.3.kv_ref, s32[1,512]{1,0:T(1,128)S(1)} %get-tuple-element.57.p_ref, f32[256,1024]{1,0:T(8,128)S(1)} %get-tuple-element.77.acc_ref, ...), custom_call_target="tpu_custom_call" | custom-call | flops 268435456 | bytes 4194304 | tf_op jit(solution)/shard_map/last_tile/pallas_call | solution.py:466
  25.8 0.1 collective-permute-start.5
  25.8 1.1 %early_rows.3.got_last_ref = bf16[256,512]{1,0:T(8,128)(2,1)S(1)} custom-call(bf16[256,768]{1,0:T(8,128)(2,1)S(1)} %collective-permute-done.2.early_ref, bf16[256,768]{1,0:T(8,128)(2,1)S(1)} %collective-permute-done.4.near_ref.got_ref, s32[1,512]{1,0:T(1,128)S(1)} %get-tuple-element.57.p_ref), custom_call_target="tpu_custom_call" | custom-call | flops 268435456 | bytes 4194304 | tf_op jit(solution)/shard_map/early_rows/pallas_call | solution.py:488
  27.0 4.2 %project_first.1 = (bf16[512,2048]{1,0:T(8,128)(2,1)}, f32[256,2048]{1,0:T(8,128)S(1)}) custom-call(bf16[256,768]{1,0:T(8,128)(2,1)S(1)} %first_rows.1.near_ref.first_ref, bf16[256,512]{1,0:T(8,128)(2,1)S(1)} %early_rows.2.last_ref, bf16[256,768]{1,0:T(8,128)(2,1)S(1)} %collective-permute-done.4.near_ref.got_ref, ...), custom_call_target="tpu_custom_call" | custom-call | flops 3221225472 | bytes 8388608 | tf_op jit(solution)/shard_map/project_first/pallas_call | solution.py:479
  31.2 0.0 collective-permute-done.7.got_ref
  31.2 0.7 %project_second.2.part_ref = f32[256,2048]{1,0:T(8,128)S(1)} custom-call(bf16[256,512]{1,0:T(8,128)(2,1)S(1)} %collective-permute-done.7.got_ref, f32[256,2048]{1,0:T(8,128)S(1)} %get-tuple-element.93.part_ref, bf16[2048,2048]{1,0:T(8,128)(2,1)S(1)} %get-tuple-element.92.w_ref), custom_call_target="tpu_custom_call" | custom-call | flops 536870912 | bytes 4194304 | tf_op jit(solution)/shard_map/project_second/pallas_call | solution.py:490
  32.0 1.6 %collective-permute-done.6.got_ref = bf16[256,384]{1,0:T(8,128)(2,1)S(1)} collective-permute-done((bf16[256,384]{1,0:T(8,128)(2,1)S(1)}, bf16[256,384]{1,0:T(8,128)(2,1)S(1)}, u32[]{:S(2)}, u32[]{:S(2)}) %collective-permute-start.6) | collective-permute-done | bytes 196640 | tf_op jit(solution)/shard_map/ppermute | solution.py:391
  33.5 0.7 %project_second.3.part_ref = f32[256,2048]{1,0:T(8,128)S(1)} custom-call(bf16[256,384]{1,0:T(8,128)(2,1)S(1)} %collective-permute-done.6.got_ref, f32[256,2048]{1,0:T(8,128)S(1)} %project_second.2.part_ref, bf16[2048,2048]{1,0:T(8,128)(2,1)S(1)} %get-tuple-element.92.w_ref), custom_call_target="tpu_custom_call" | custom-call | flops 536870912 | bytes 4194304 | tf_op jit(solution)/shard_map/project_second/pallas_call | solution.py:490
  34.3 0.1 collective-permute-done.5.got_ref
  34.4 1.2 %project_last.1 = bf16[512,2048]{1,0:T(8,128)(2,1)} custom-call(bf16[256,128]{1,0:T(8,128)(2,1)S(1)} %collective-permute-done.5.got_ref, f32[256,2048]{1,0:T(8,128)S(1)} %project_second.3.part_ref, bf16[2048,2048]{1,0:T(8,128)(2,1)S(1)} %get-tuple-element.92.w_ref, bf16[512,2048]{1,0:T(8,128)(2,1)} %get-tuple-element.94.begun_hbm), custom_call_target="tpu_custom_call", output_to_operand_aliasing={{}: (3, {})} | custom-call | flops 536870912 | bytes 4194304 | tf_op jit(solution)/shard_map/project_last/pallas_call | solution.py:498
Async XLA Ops:
  1.5 8.6 %collective-permute-start = (bf16[256,512]{1,0:T(8,128)(2,1)S(1)}, bf16[256,512]{1,0:T(8,128)(2,1)S(1)}, u32[]{:S(2)}, u32[]{:S(2)}) collective-permute-start(bf16[256,512]{1,0:T(8,128)(2,1)S(1)} %get-tuple-element.62), channel_id=1, source_target_pairs={{0,2},{2,8},{4,6},{6,12},{8,10},{10,16},{12,14},{14,20},{16,18},{1... | collective-permute-start | bytes 786440 | tf_op jit(solution)/shard_map/ppermute | solution.py:412
  2.2 15.1 %collective-permute-start.2 = (bf16[256,768]{1,0:T(8,128)(2,1)S(1)}, bf16[256,768]{1,0:T(8,128)(2,1)S(1)}, u32[]{:S(2)}, u32[]{:S(2)}) collective-permute-start(bf16[256,768]{1,0:T(8,128)(2,1)S(1)} %pack_early.1.early_ref), channel_id=1, source_target_pairs={{0,1},{1,0},{2,3},{3,2},{4,5},{5,4},{6,7},{7,6},{8,9},{9,8},{10,11... | collective-permute-start | bytes 1179656 | tf_op jit(solution)/shard_map/ppermute | solution.py:391
  5.7 11.6 %collective-permute-start.1 = (bf16[256,512]{1,0:T(8,128)(2,1)S(1)}, bf16[256,512]{1,0:T(8,128)(2,1)S(1)}, u32[]{:S(2)}, u32[]{:S(2)}) collective-permute-start(bf16[256,512]{1,0:T(8,128)(2,1)S(1)} %get-tuple-element.69), channel_id=1, source_target_pairs={{0,4},{2,6},{4,8},{6,10},{8,12},{10,14},{12,16},{14,18},{16,20},{1... | collective-permute-start | bytes 786440 | tf_op jit(solution)/shard_map/ppermute | solution.py:427
  10.3 12.1 %collective-permute-start.4 = (bf16[256,768]{1,0:T(8,128)(2,1)S(1)}, bf16[256,768]{1,0:T(8,128)(2,1)S(1)}, u32[]{:S(2)}, u32[]{:S(2)}) collective-permute-start(bf16[256,768]{1,0:T(8,128)(2,1)S(1)} %first_rows.1.near_ref.first_ref), channel_id=1, source_target_pairs={{0,1},{1,0},{2,3},{3,2},{4,5},{5,4},{6,7},{7,6},{8,9},{9,8},{10,11... | collective-permute-start | bytes 1179656 | tf_op jit(solution)/shard_map/ppermute | solution.py:391
  17.3 1.9 %collective-permute-start.3 = (bf16[256,512]{1,0:T(8,128)(2,1)S(1)}, bf16[256,512]{1,0:T(8,128)(2,1)S(1)}, u32[]{:S(2)}, u32[]{:S(2)}) collective-permute-start(bf16[256,512]{1,0:T(8,128)(2,1)S(1)} %collective-permute-done.1.kv_ref), channel_id=1, source_target_pairs={{0,2},{2,0},{4,6},{6,4},{8,10},{10,8},{12,14},{14,12},{16,18},{18,... | collective-permute-start | bytes 786440 | tf_op jit(solution)/shard_map/ppermute | solution.py:453
  20.0 11.2 %collective-permute-start.7 = (bf16[256,512]{1,0:T(8,128)(2,1)S(1)}, bf16[256,512]{1,0:T(8,128)(2,1)S(1)}, u32[]{:S(2)}, u32[]{:S(2)}) collective-permute-start(bf16[256,512]{1,0:T(8,128)(2,1)S(1)} %last_tile.3.second0_ref), channel_id=1, source_target_pairs={{0,1},{1,0},{2,3},{3,2},{4,5},{5,4},{6,7},{7,6},{8,9},{9,8},{10,11... | collective-permute-start | bytes 786440 | tf_op jit(solution)/shard_map/ppermute | solution.py:391
  23.1 10.4 %collective-permute-start.6 = (bf16[256,384]{1,0:T(8,128)(2,1)S(1)}, bf16[256,384]{1,0:T(8,128)(2,1)S(1)}, u32[]{:S(2)}, u32[]{:S(2)}) collective-permute-start(bf16[256,384]{1,0:T(8,128)(2,1)S(1)} %last_tile.4.second1_ref), channel_id=1, source_target_pairs={{0,1},{1,0},{2,3},{3,2},{4,5},{5,4},{6,7},{7,6},{8,9},{9,8},{10,11... | collective-permute-start | bytes 589832 | tf_op jit(solution)/shard_map/ppermute | solution.py:391
  25.8 8.6 %collective-permute-start.5 = (bf16[256,128]{1,0:T(8,128)(2,1)S(1)}, bf16[256,128]{1,0:T(8,128)(2,1)S(1)}, u32[]{:S(2)}, u32[]{:S(2)}) collective-permute-start(bf16[256,128]{1,0:T(8,128)(2,1)S(1)} %last_tile.5.second2_ref), channel_id=1, source_target_pairs={{0,1},{1,0},{2,3},{3,2},{4,5},{5,4},{6,7},{7,6},{8,9},{9,8},{10,11... | collective-permute-start | bytes 196616 | tf_op jit(solution)/shard_map/ppermute | solution.py:391

commit v2 on v1

--- a/solution.py
+++ b/solution.py
@@ -205,9 +205,6 @@
     depth = rot_ref.shape[1]
     step = jnp.where(rank % 2 == 1, 1, 3)
     used = waits_for_keys(rank)
-    out_ref[:, depth : depth + HEAD_SIZE] = kv_ref[:, width - HEAD_SIZE : width]
-    out_ref[:, depth + HEAD_SIZE :] = kv_ref[:, 2 * width - HEAD_SIZE :]
-
     @pl.when(used)
     def _():
         biases = tile_biases(half_positions(p_ref, rank, True), [(distance(rank, step, count), False)])
@@ -220,20 +217,18 @@
 
     @pl.when(jnp.logical_not(used))
     def _():
-        out_ref[:, :depth] = own_ref[...]
+        out_ref[...] = own_ref[...]
 
 
 def early_kernel(count, early_ref, near_ref, p_ref, out_ref):
     rank = lax.axis_index("ctx")
     depth = out_ref.shape[1]
+    width = near_ref.shape[1] // 2
     step = jnp.where(rank % 2 == 1, 1, 3)
     reach = jnp.where(waits_for_keys(rank), distance(rank, step, count), FAR)
     biases = tile_biases(half_positions(p_ref, rank, True), [(0, True), (reach, False)])
-    keys, values = [], []
-    for ref in (early_ref, near_ref):
-        begin = ref.shape[1] - 2 * HEAD_SIZE
-        keys.append(ref[:, begin : begin + HEAD_SIZE])
-        values.append(with_ones(ref[:, begin + HEAD_SIZE :]))
+    keys = [early_ref[:, depth : depth + HEAD_SIZE], near_ref[:, width - HEAD_SIZE : width]]
+    values = [with_ones(early_ref[:, depth + HEAD_SIZE :]), with_ones(near_ref[:, 2 * width - HEAD_SIZE :])]
     for head in range(depth // HEAD_SIZE):
         at = slice(head * HEAD_SIZE, (head + 1) * HEAD_SIZE)
         out_ref[:, at] = finished(begin_state(early_ref[:, at], keys, values, biases))
@@ -304,25 +299,29 @@
     return pl.ds(pl.multiple_of(base + begin, HEAD_SIZE), end - begin)
 
 
-def project_kernel(
-    first_ref, last_ref, got_ref, got_last_ref, second0_ref, second1_ref, second2_ref, w_ref, out_hbm, part_ref, held_ref, sems
-):
-    rank = lax.axis_index("ctx")
+def project_kernel(first_ref, last_ref, second0_ref, second1_ref, second2_ref, w_ref, sum_ref, part_ref):
     half, depth = first_ref.shape[0], w_ref.shape[0] // 2
-    cut = depth - last_ref.shape[1]
-    rows = pl.ds(first_begin(rank, half), half)
     mine = pl.ds(pl.multiple_of(lax.axis_index("head") * depth, depth), depth)
-    other = other_rows(w_ref, 0, depth)
-    first = jnp.concatenate([first_ref[:, :cut], last_ref[...]], axis=1)
-    got = jnp.concatenate([got_ref[:, :cut], got_last_ref[...]], axis=1)
+    first = jnp.concatenate([first_ref[...], last_ref[...]], axis=1)
     second = jnp.concatenate([second0_ref[...], second1_ref[...], second2_ref[...]], axis=1)
     stacked = jnp.concatenate([first, second], axis=0)
+    for tile in range(w_ref.shape[1] // TILE):
+        at = slice(tile * TILE, (tile + 1) * TILE)
+        both = dot(stacked, w_ref[mine, at])
+        sum_ref[:, at] = both[:half]
+        part_ref[:, at] = both[half:]
+
+
+def first_out_kernel(got_ref, got_last_ref, sum_ref, w_ref, out_hbm, held_ref, sems):
+    rank = lax.axis_index("ctx")
+    half, depth = got_ref.shape[0], w_ref.shape[0] // 2
+    rows = pl.ds(first_begin(rank, half), half)
+    other = other_rows(w_ref, 0, depth)
+    got = jnp.concatenate([got_ref[...], got_last_ref[...]], axis=1)
     copies = []
     for tile in range(w_ref.shape[1] // TILE):
         at = slice(tile * TILE, (tile + 1) * TILE)
-        both = dot(stacked, w_ref[mine, at])
-        part_ref[:, at] = both[half:]
-        held_ref[:, at] = (both[:half] + dot(got, w_ref[other, at])).astype(BF16)
+        held_ref[:, at] = (sum_ref[:, at] + dot(got, w_ref[other, at])).astype(BF16)
         copies.append(pltpu.make_async_copy(held_ref.at[:, at], out_hbm.at[rows, at], sems.at[tile]))
         copies[-1].start()
     for copy in copies:
@@ -409,7 +408,8 @@
         4 * MIB,
         scratch=[pltpu.VMEM(keys.shape, BF16), pltpu.VMEM((1, HEAD_SIZE), F32), dma((5,))],
     )(*(in_hbm(array) for array in (keys, values, queries, position_row, frequency)))
-    near_got = lax.ppermute(near, "ctx", pairs(lambda r: r + 3 if r % 2 else r + 1))
+    near_pairs = pairs(lambda r: r + 3 if r % 2 else r + 1)
+    near_got = lax.ppermute(near, "ctx", near_pairs)
     early = call(pack_kernel, "pack_early", [vmem] * 5, shape((half, (group + 2) * HEAD_SIZE), BF16), MIB, MIB)(
         q, k_rot, v, cosine, sinus
     )
@@ -429,7 +429,7 @@
         functools.partial(first_kernel, count, group),
         "first_rows",
         [vmem] * 7,
-        shape((half, (cut + 2) * HEAD_SIZE), BF16),
+        some_shape,
         256 * MIB,
         4 * MIB,
     )(own, rot, near_got, p, acc, top, total)
@@ -448,7 +448,7 @@
     attend_early = call(
         functools.partial(early_kernel, count), "early_rows", [vmem] * 3, last_shape, 256 * MIB, 4 * MIB
     )
-    last = attend_early(early, first, p)
+    last = attend_early(early, near_got, p)
     rot, next_got, last, early_got = lax.optimization_barrier((rot, next_got, last, early_got))
     last_got = lax.ppermute(next_got, "ctx", pairs(lambda r: r + 1 - 2 * (r % 2)))
     state_now = call(
@@ -461,6 +461,7 @@
         aliases={3: 0, 4: 1, 5: 2},
     )(rot, next_got, p, *state_now)
     parts = range(cut), range(cut, heads - 1), range(heads - 1, heads)
+    rot, first_got = lax.optimization_barrier((rot, first_got))
     seconds, seconds_got = [], []
     for part in parts:
         second = call(
@@ -472,20 +473,27 @@
             4 * MIB,
         )(rot, last_got, p, *state_now)
         seconds_got.append(swapped(second))
-        rot, second, first_got = lax.optimization_barrier((rot, second, first_got))
+        rot, second, first_got, early_got = lax.optimization_barrier((rot, second, first_got, early_got))
         seconds.append(second)
+        if len(seconds) == 2:
+            other_near = lax.ppermute(early_got[:, group * HEAD_SIZE :], "ctx", near_pairs)
     sum_shape = shape((half, columns), F32)
-    early_got, seconds[-1] = lax.optimization_barrier((early_got, seconds[-1]))
-    begun, partial_sum = call(
-        project_kernel,
+    first_sum, partial_sum = call(
+        project_kernel, "project_own", [vmem] * 6, [sum_shape, sum_shape], 2048 * MIB, 8 * MIB
+    )(first, last, *seconds, w)
+    early_got, partial_sum, first_sum = lax.optimization_barrier((early_got, partial_sum, first_sum))
+    got_last = attend_early(early_got, other_near, p)
+    begun = call(
+        first_out_kernel,
         "project_first",
-        [vmem] * 8,
-        [shape((number, columns), BF16), sum_shape],
-        3072 * MIB,
+        [vmem] * 4,
+        shape((number, columns), BF16),
+        1024 * MIB,
         8 * MIB,
-        out_specs=[hbm, vmem],
+        out_specs=hbm,
         scratch=[pltpu.VMEM((half, columns), BF16), dma((tiles,))],
-    )(first, last, first_got, attend_early(early_got, first_got, p), *seconds, w)
+    )(first_got, got_last, first_sum, w)
+    begun, partial_sum = lax.optimization_barrier((begun, partial_sum))
     for part, got in zip(parts[:-1], seconds_got):
         partial_sum = call(
             functools.partial(add_kernel, part[0] * HEAD_SIZE),

time: 36 us -> 38.5 us (1.069)
  starting transfers between devices: 10.2 us -> 11.4 us
  waiting for transfers between devices: 6.29 us -> 7.41 us
    ppermute x1 -> x2, waiting for transfers between devices: 2.77 us -> 6.6 us  [the longest x1 3.83 us: shards(): lax.ppermute(early_got[:, group * HEAD_SIZE:], 'ctx', near_pairs)]
    ppermute x5, waiting for transfers between devices: 3.06 us -> 0.19 us  [swapped(): return lax.ppermute(array, 'head', [(0, 1), (1, 0)])]
    ppermute x5, starting transfers between devices: 7.92 us -> 9.16 us  [swapped(): return lax.ppermute(array, 'head', [(0, 1), (1, 0)])]
    pallas_call x3 -> x4, Pallas kernels: 6.46 us -> 6.74 us  [the longest x1 2.36 us: shards(): call(project_kernel, 'project_own', [vmem] * 6, [sum_shape, sum_shape], 2...]
  transfers between devices with their start and end apart: 8 -> 9, of which waited for: 5 -> 4; matrix products, arithmetic and copies ran while one was open for 0% -> 0% of each run, Pallas kernels for 46% -> 41%
where the time goes in v2:
time: 38.5 us; the launch traced here: 38.3 us
  Pallas kernels  19.2 us (50%)
  starting transfers between devices  11.4 us (30%)
  waiting for transfers between devices  7.41 us (19%)
    ppermute x5, starting transfers between devices, swapped(): return lax.ppermute(array, 'head', [(0, 1), (1, 0)])  9.16 us
    ppermute x1, waiting for transfers between devices, shards(): lax.ppermute(early_got[:, group * HEAD_SIZE:], 'ctx', near_pairs)  3.83 us
    pallas_call x1, Pallas kernels, shards(): call(functools.partial(second_kernel, count, group), 'second_rows', [vmem...  3.39 us
    ppermute x1, waiting for transfers between devices, shards(): near_got = lax.ppermute(near, 'ctx', near_pairs)  2.77 us
    pallas_call x1, Pallas kernels, shards(): call(project_kernel, 'project_own', [vmem] * 6, [sum_shape, sum_shape], 2...  2.36 us
    pallas_call x1, Pallas kernels, shards(): call(first_out_kernel, 'project_first', [vmem] * 4, shape((number, column...  2.08 us
    pallas_call x3, Pallas kernels, shards(): call(functools.partial(third_kernel, count, group, part), 'last_tile', [v...  1.95 us
    pallas_call x1, Pallas kernels, shards(): call(functools.partial(next_kernel, count, group), 'next_tile', [vmem] *...  1.73 us
  transfers between devices with their start and end apart: 9, of which 4 were waited for; matrix products, arithmetic and copies ran while one was open for 0% of the time, Pallas kernels for 41%

profile of v2, /device:TPU:0, one launch (start us, length us, event | category | flops | bytes accessed | tf_op | source)
XLA Modules:
  0.0 38.3 jit_solution(15762508312109306283)
XLA Ops:
  0.0 1.5 %rotate_keys.1 = (bf16[256,512]{1,0:T(8,128)(2,1)S(1)}, bf16[256,512]{1,0:T(8,128)(2,1)S(1)}, bf16[512,256]{1,0:T(8,128)(2,1)S(1)}, bf16[512,256]{1,0:T(8,128)(2...) custom-call(bf16[512,256]{1,0:T(8,128)(2,1)} %k_hbm.1, ...), custom_call_target="tpu_custom_call" | custom-call | flops 4194304 | bytes 4194304 | tf_op jit(solution)/shard_map/rotate_keys/pallas_call | solution.py:400
  1.5 0.5 %collective-permute-start = (bf16[256,512]{1,0:T(8,128)(2,1)S(1)}, bf16[256,512]{1,0:T(8,128)(2,1)S(1)}, u32[]{:S(2)}, u32[]{:S(2)}) collective-permute-start(bf16[256,512]{1,0:T(8,128)(2,1)S(1)} %get-tuple-element.70), channel_id=1, source_target_pairs={{0,2},{2,8},{4,6},{6,12},{8,10},{10,16},{12,14},{14,20},{16,18},{1... | collective-permute-start | bytes 786440 | tf_op jit(solution)/shard_map/ppermute | solution.py:412
  2.0 0.2 pack_early.1.early_ref
  2.2 2.6 %collective-permute-start.2 = (bf16[256,768]{1,0:T(8,128)(2,1)S(1)}, bf16[256,768]{1,0:T(8,128)(2,1)S(1)}, u32[]{:S(2)}, u32[]{:S(2)}) collective-permute-start(bf16[256,768]{1,0:T(8,128)(2,1)S(1)} %pack_early.1.early_ref), channel_id=1, source_target_pairs={{0,1},{1,0},{2,3},{3,2},{4,5},{5,4},{6,7},{7,6},{8,9},{9,8},{10,11... | collective-permute-start | bytes 1179656 | tf_op jit(solution)/shard_map/ppermute | solution.py:390
  4.8 1.0 %own_tiles.1 = (bf16[256,512]{1,0:T(8,128)(2,1)S(1)}, bf16[256,512]{1,0:T(8,128)(2,1)S(1)}, f32[256,512]{1,0:T(8,128)S(1)}, f32[256,512]{1,0:T(8,128)S(1)}, f32[256,512]{1,0:T(8,128)S(1)}) custom-call(bf16[512,1024]{1,0:T(8,128)(2,1)S(1)} %get-tuple-element.74.q_ref, bf16[512,256]{1,0:T(8,128)(2,1)S(1)} %get-tuple-element.59.k_ref, ...), custom_call_target="tpu_custom_call" | custom-call | flops 268435456 | bytes 4194304 | tf_op jit(solution)/shard_map/own_tiles/pallas_call | solution.py:418
  5.7 1.6 %collective-permute-start.1 = (bf16[256,512]{1,0:T(8,128)(2,1)S(1)}, bf16[256,512]{1,0:T(8,128)(2,1)S(1)}, u32[]{:S(2)}, u32[]{:S(2)}) collective-permute-start(bf16[256,512]{1,0:T(8,128)(2,1)S(1)} %get-tuple-element.77), channel_id=1, source_target_pairs={{0,4},{2,6},{4,8},{6,10},{8,12},{10,14},{12,16},{14,18},{16,20},{1... | collective-permute-start | bytes 786440 | tf_op jit(solution)/shard_map/ppermute | solution.py:427
  7.3 2.8 %collective-permute-done.kv_ref.near_ref = bf16[256,512]{1,0:T(8,128)(2,1)S(1)} collective-permute-done((bf16[256,512]{1,0:T(8,128)(2,1)S(1)}, bf16[256,512]{1,0:T(8,128)(2,1)S(1)}, u32[]{:S(2)}, u32[]{:S(2)}) %collective-permute-start) | collective-permute-done | bytes 262176 | tf_op jit(solution)/shard_map/ppermute | solution.py:412
  10.1 2.1 %collective-permute-start.3 = (bf16[256,512]{1,0:T(8,128)(2,1)S(1)}, bf16[256,512]{1,0:T(8,128)(2,1)S(1)}, u32[]{:S(2)}, u32[]{:S(2)}) collective-permute-start(bf16[256,512]{1,0:T(8,128)(2,1)S(1)} %first_rows.1.first_ref), channel_id=1, source_target_pairs={{0,1},{1,0},{2,3},{3,2},{4,5},{5,4},{6,7},{7,6},{8,9},{9,8},{10,11... | collective-permute-start | bytes 786440 | tf_op jit(solution)/shard_map/ppermute | solution.py:390
  12.1 3.4 %second_rows.1 = (bf16[256,1024]{1,0:T(8,128)(2,1)S(1)}, f32[256,1024]{1,0:T(8,128)S(1)}, f32[256,1024]{1,0:T(8,128)S(1)}, f32[256,1024]{1,0:T(8,128)S(1)}, bf16[2048,2048]{1,0:T(8,128)(2,1)S(1)}) custom-call(bf16[512,1024]{1,0:T(8,128)(2,1)S(1)} %get-tuple-element.74.q_ref, bf16[512,256]{1,0:T(8,128)(2,1)S(1)} %get-tuple-element.59.k_ref, ...), custom_call_target="tpu_custom_call" | custom-call | flops 1073741824 | bytes 12582912 | tf_op jit(solution)/shard_map/second_rows/pallas_call | solution.py:438
  15.5 1.2 %early_rows.2.last_ref = bf16[256,512]{1,0:T(8,128)(2,1)S(1)} custom-call(bf16[256,768]{1,0:T(8,128)(2,1)S(1)} %pack_early.1.early_ref, bf16[256,512]{1,0:T(8,128)(2,1)S(1)} %collective-permute-done.kv_ref.near_ref, s32[1,512]{1,0:T(1,128)S(1)} %get-tuple-element.65.p_ref), custom_call_target="tpu_custom_call" | custom-call | flops 268435456 | bytes 4194304 | tf_op jit(solution)/shard_map/early_rows/pallas_call | solution.py:451
  16.7 0.6 %collective-permute-done.1.kv_ref = bf16[256,512]{1,0:T(8,128)(2,1)S(1)} collective-permute-done((bf16[256,512]{1,0:T(8,128)(2,1)S(1)}, bf16[256,512]{1,0:T(8,128)(2,1)S(1)}, u32[]{:S(2)}, u32[]{:S(2)}) %collective-permute-start.1) | collective-permute-done | bytes 262176 | tf_op jit(solution)/shard_map/ppermute | solution.py:427
  17.3 0.0 collective-permute-done.2.early_ref
  17.3 0.2 collective-permute-start.4
  17.5 1.7 %next_tile.1 = (f32[256,1024]{1,0:T(8,128)S(1)}, f32[256,1024]{1,0:T(8,128)S(1)}, f32[256,1024]{1,0:T(8,128)S(1)}) custom-call(bf16[256,1024]{1,0:T(8,128)(2,1)S(1)} %get-tuple-element.93.rot_ref, bf16[256,512]{1,0:T(8,128)(2,1)S(1)} %collective-permute-done.1.kv_ref, ...), custom_call_target="tpu_custom_call", output_to_operand_aliasing={{0}: (3, {}), {1}: (4, {}), {2}: (5, {})} | custom-call | flops 536870912 | bytes 4194304 | tf_op jit(solution)/shard_map/next_tile/pallas_call | solution.py:454
  19.2 0.2 collective-permute-done.3.got_ref
  19.4 0.0 collective-permute-done.4.kv_ref
  19.4 0.8 %last_tile.3.second0_ref = bf16[256,512]{1,0:T(8,128)(2,1)S(1)} custom-call(bf16[256,1024]{1,0:T(8,128)(2,1)S(1)} %get-tuple-element.93.rot_ref, bf16[256,512]{1,0:T(8,128)(2,1)S(1)} %collective-permute-done.4.kv_ref, s32[1,512]{1,0:T(1,128)S(1)} %get-tuple-element.65.p_ref, f32[256,1024]{1,0:T(8,128)S(1)} %get-tuple-element.85.acc_ref, ...), custom_call_target="tpu_custom_call" | custom-call | flops 268435456 | bytes 4194304 | tf_op jit(solution)/shard_map/last_tile/pallas_call | solution.py:467
  20.2 2.4 %collective-permute-start.7 = (bf16[256,512]{1,0:T(8,128)(2,1)S(1)}, bf16[256,512]{1,0:T(8,128)(2,1)S(1)}, u32[]{:S(2)}, u32[]{:S(2)}) collective-permute-start(bf16[256,512]{1,0:T(8,128)(2,1)S(1)} %last_tile.3.second0_ref), channel_id=1, source_target_pairs={{0,1},{1,0},{2,3},{3,2},{4,5},{5,4},{6,7},{7,6},{8,9},{9,8},{10,11... | collective-permute-start | bytes 786440 | tf_op jit(solution)/shard_map/ppermute | solution.py:390
  22.6 0.7 %last_tile.4.second1_ref = bf16[256,384]{1,0:T(8,128)(2,1)S(1)} custom-call(bf16[256,1024]{1,0:T(8,128)(2,1)S(1)} %get-tuple-element.93.rot_ref, bf16[256,512]{1,0:T(8,128)(2,1)S(1)} %collective-permute-done.4.kv_ref, s32[1,512]{1,0:T(1,128)S(1)} %get-tuple-element.65.p_ref, f32[256,1024]{1,0:T(8,128)S(1)} %get-tuple-element.85.acc_ref, ...), custom_call_target="tpu_custom_call" | custom-call | flops 268435456 | bytes 4194304 | tf_op jit(solution)/shard_map/last_tile/pallas_call | solution.py:467
  23.2 0.1 collective-permute-start.6
  23.3 0.5 %last_tile.5.second2_ref = bf16[256,128]{1,0:T(8,128)(2,1)S(1)} custom-call(bf16[256,1024]{1,0:T(8,128)(2,1)S(1)} %get-tuple-element.93.rot_ref, bf16[256,512]{1,0:T(8,128)(2,1)S(1)} %collective-permute-done.4.kv_ref, s32[1,512]{1,0:T(1,128)S(1)} %get-tuple-element.65.p_ref, f32[256,1024]{1,0:T(8,128)S(1)} %get-tuple-element.85.acc_ref, ...), custom_call_target="tpu_custom_call" | custom-call | flops 268435456 | bytes 4194304 | tf_op jit(solution)/shard_map/last_tile/pallas_call | solution.py:467
  23.8 2.1 %collective-permute-start.5 = (bf16[256,128]{1,0:T(8,128)(2,1)S(1)}, bf16[256,128]{1,0:T(8,128)(2,1)S(1)}, u32[]{:S(2)}, u32[]{:S(2)}) collective-permute-start(bf16[256,128]{1,0:T(8,128)(2,1)S(1)} %last_tile.5.second2_ref), channel_id=1, source_target_pairs={{0,1},{1,0},{2,3},{3,2},{4,5},{5,4},{6,7},{7,6},{8,9},{9,8},{10,11... | collective-permute-start | bytes 196616 | tf_op jit(solution)/shard_map/ppermute | solution.py:390
  25.9 0.0 collective-permute-start.8
  25.9 2.4 %project_own.1 = (f32[256,2048]{1,0:T(8,128)S(1)}, f32[256,2048]{1,0:T(8,128)S(1)}) custom-call(bf16[256,512]{1,0:T(8,128)(2,1)S(1)} %first_rows.1.first_ref, bf16[256,512]{1,0:T(8,128)(2,1)S(1)} %early_rows.2.last_ref, bf16[256,512]{1,0:T(8,128)(2,1)S(1)} %last_tile.3.second0_ref, bf16[256,384]{1,0:T(8,128)(2,1)S(1)} %last_tile.4.second1_ref, ...), custom_call_target="tpu_custom_call" | custom-call | flops 2147483648 | bytes 8388608 | tf_op jit(solution)/shard_map/project_own/pallas_call | solution.py:481
  28.3 3.8 %collective-permute-done.8.near_ref = bf16[256,256]{1,0:T(8,128)(2,1)S(1)} collective-permute-done((bf16[256,256]{1,0:T(8,128)(2,1)S(1)}, bf16[256,256]{1,0:T(8,128)(2,1)S(1)}, u32[]{:S(2)}, u32[]{:S(2)}) %collective-permute-start.8) | collective-permute-done | bytes 131104 | tf_op jit(solution)/shard_map/ppermute | solution.py:479
  32.1 1.1 %early_rows.3.got_last_ref = bf16[256,512]{1,0:T(8,128)(2,1)S(1)} custom-call(bf16[256,768]{1,0:T(8,128)(2,1)S(1)} %collective-permute-done.2.early_ref, bf16[256,256]{1,0:T(8,128)(2,1)S(1)} %collective-permute-done.8.near_ref, s32[1,512]{1,0:T(1,128)S(1)} %get-tuple-element.65.p_ref), custom_call_target="tpu_custom_call" | custom-call | flops 268435456 | bytes 4194304 | tf_op jit(solution)/shard_map/early_rows/pallas_call | solution.py:485
  33.3 2.1 %project_first.1.begun_hbm = bf16[512,2048]{1,0:T(8,128)(2,1)} custom-call(bf16[256,512]{1,0:T(8,128)(2,1)S(1)} %collective-permute-done.3.got_ref, bf16[256,512]{1,0:T(8,128)(2,1)S(1)} %early_rows.3.got_last_ref, f32[256,2048]{1,0:T(8,128)S(1)} %get-tuple-element.107.sum_ref, bf16[2048,2048]{1,0:T(8,128)(2,1)S(1)} %get-tuple-element.103.w_ref), custom_call_target="tpu_custom_call" | custom-call | flops 1073741824 | bytes 8388608 | tf_op jit(solution)/shard_map/project_first/pallas_call | solution.py:486
  35.3 0.0 collective-permute-done.7.got_ref
  35.4 0.7 %project_second.2.part_ref = f32[256,2048]{1,0:T(8,128)S(1)} custom-call(bf16[256,512]{1,0:T(8,128)(2,1)S(1)} %collective-permute-done.7.got_ref, f32[256,2048]{1,0:T(8,128)S(1)} %get-tuple-element.109.part_ref, bf16[2048,2048]{1,0:T(8,128)(2,1)S(1)} %get-tuple-element.103.w_ref), custom_call_target="tpu_custom_call" | custom-call | flops 536870912 | bytes 4194304 | tf_op jit(solution)/shard_map/project_second/pallas_call | solution.py:498
  36.1 0.0 collective-permute-done.6.got_ref
  36.1 0.7 %project_second.3.part_ref = f32[256,2048]{1,0:T(8,128)S(1)} custom-call(bf16[256,384]{1,0:T(8,128)(2,1)S(1)} %collective-permute-done.6.got_ref, f32[256,2048]{1,0:T(8,128)S(1)} %project_second.2.part_ref, bf16[2048,2048]{1,0:T(8,128)(2,1)S(1)} %get-tuple-element.103.w_ref), custom_call_target="tpu_custom_call" | custom-call | flops 536870912 | bytes 4194304 | tf_op jit(solution)/shard_map/project_second/pallas_call | solution.py:498
  36.9 1.3 %project_last.1 = bf16[512,2048]{1,0:T(8,128)(2,1)} custom-call(bf16[256,128]{1,0:T(8,128)(2,1)S(1)} %collective-permute-done.5.got_ref, f32[256,2048]{1,0:T(8,128)S(1)} %project_second.3.part_ref, bf16[2048,2048]{1,0:T(8,128)(2,1)S(1)} %get-tuple-element.103.w_ref, bf16[512,2048]{1,0:T(8,128)(2,1)} %project_first.1.begun_hbm), custom_call_target="tpu_custom_call", output_to_operand_aliasing={{}: (3, {})} | custom-call | flops 536870912 | bytes 4194304 | tf_op jit(solution)/shard_map/project_last/pallas_call | solution.py:506
  (3 shorter events, 0.0 us)
Async XLA Ops:
  1.5 8.6 %collective-permute-start = (bf16[256,512]{1,0:T(8,128)(2,1)S(1)}, bf16[256,512]{1,0:T(8,128)(2,1)S(1)}, u32[]{:S(2)}, u32[]{:S(2)}) collective-permute-start(bf16[256,512]{1,0:T(8,128)(2,1)S(1)} %get-tuple-element.70), channel_id=1, source_target_pairs={{0,2},{2,8},{4,6},{6,12},{8,10},{10,16},{12,14},{14,20},{16,18},{1... | collective-permute-start | bytes 786440 | tf_op jit(solution)/shard_map/ppermute | solution.py:412
  2.2 15.1 %collective-permute-start.2 = (bf16[256,768]{1,0:T(8,128)(2,1)S(1)}, bf16[256,768]{1,0:T(8,128)(2,1)S(1)}, u32[]{:S(2)}, u32[]{:S(2)}) collective-permute-start(bf16[256,768]{1,0:T(8,128)(2,1)S(1)} %pack_early.1.early_ref), channel_id=1, source_target_pairs={{0,1},{1,0},{2,3},{3,2},{4,5},{5,4},{6,7},{7,6},{8,9},{9,8},{10,11... | collective-permute-start | bytes 1179656 | tf_op jit(solution)/shard_map/ppermute | solution.py:390
  5.7 11.6 %collective-permute-start.1 = (bf16[256,512]{1,0:T(8,128)(2,1)S(1)}, bf16[256,512]{1,0:T(8,128)(2,1)S(1)}, u32[]{:S(2)}, u32[]{:S(2)}) collective-permute-start(bf16[256,512]{1,0:T(8,128)(2,1)S(1)} %get-tuple-element.77), channel_id=1, source_target_pairs={{0,4},{2,6},{4,8},{6,10},{8,12},{10,14},{12,16},{14,18},{16,20},{1... | collective-permute-start | bytes 786440 | tf_op jit(solution)/shard_map/ppermute | solution.py:427
  10.1 9.3 %collective-permute-start.3 = (bf16[256,512]{1,0:T(8,128)(2,1)S(1)}, bf16[256,512]{1,0:T(8,128)(2,1)S(1)}, u32[]{:S(2)}, u32[]{:S(2)}) collective-permute-start(bf16[256,512]{1,0:T(8,128)(2,1)S(1)} %first_rows.1.first_ref), channel_id=1, source_target_pairs={{0,1},{1,0},{2,3},{3,2},{4,5},{5,4},{6,7},{7,6},{8,9},{9,8},{10,11... | collective-permute-start | bytes 786440 | tf_op jit(solution)/shard_map/ppermute | solution.py:390
  17.3 2.1 %collective-permute-start.4 = (bf16[256,512]{1,0:T(8,128)(2,1)S(1)}, bf16[256,512]{1,0:T(8,128)(2,1)S(1)}, u32[]{:S(2)}, u32[]{:S(2)}) collective-permute-start(bf16[256,512]{1,0:T(8,128)(2,1)S(1)} %collective-permute-done.1.kv_ref), channel_id=1, source_target_pairs={{0,2},{2,0},{4,6},{6,4},{8,10},{10,8},{12,14},{14,12},{16,18},{18,... | collective-permute-start | bytes 786440 | tf_op jit(solution)/shard_map/ppermute | solution.py:453
  20.2 15.2 %collective-permute-start.7 = (bf16[256,512]{1,0:T(8,128)(2,1)S(1)}, bf16[256,512]{1,0:T(8,128)(2,1)S(1)}, u32[]{:S(2)}, u32[]{:S(2)}) collective-permute-start(bf16[256,512]{1,0:T(8,128)(2,1)S(1)} %last_tile.3.second0_ref), channel_id=1, source_target_pairs={{0,1},{1,0},{2,3},{3,2},{4,5},{5,4},{6,7},{7,6},{8,9},{9,8},{10,11... | collective-permute-start | bytes 786440 | tf_op jit(solution)/shard_map/ppermute | solution.py:390
  23.2 12.9 %collective-permute-start.6 = (bf16[256,384]{1,0:T(8,128)(2,1)S(1)}, bf16[256,384]{1,0:T(8,128)(2,1)S(1)}, u32[]{:S(2)}, u32[]{:S(2)}) collective-permute-start(bf16[256,384]{1,0:T(8,128)(2,1)S(1)} %last_tile.4.second1_ref), channel_id=1, source_target_pairs={{0,1},{1,0},{2,3},{3,2},{4,5},{5,4},{6,7},{7,6},{8,9},{9,8},{10,11... | collective-permute-start | bytes 589832 | tf_op jit(solution)/shard_map/ppermute | solution.py:390
  23.8 13.0 %collective-permute-start.5 = (bf16[256,128]{1,0:T(8,128)(2,1)S(1)}, bf16[256,128]{1,0:T(8,128)(2,1)S(1)}, u32[]{:S(2)}, u32[]{:S(2)}) collective-permute-start(bf16[256,128]{1,0:T(8,128)(2,1)S(1)} %last_tile.5.second2_ref), channel_id=1, source_target_pairs={{0,1},{1,0},{2,3},{3,2},{4,5},{5,4},{6,7},{7,6},{8,9},{9,8},{10,11... | collective-permute-start | bytes 196616 | tf_op jit(solution)/shard_map/ppermute | solution.py:390
  25.9 6.2 %collective-permute-start.8 = (bf16[256,256]{1,0:T(8,128)(2,1)S(1)}, bf16[256,256]{1,0:T(8,128)(2,1)S(1)}, u32[]{:S(2)}, u32[]{:S(2)}) collective-permute-start(bf16[256,256]{1,0:T(8,128)(2,1)S(1)} %slice.3), channel_id=1, source_target_pairs={{0,2},{2,8},{4,6},{6,12},{8,10},{10,16},{12,14},{14,20},{16,18},{1... | collective-permute-start | bytes 393224 | tf_op jit(solution)/shard_map/ppermute | solution.py:479

commit v3 on v2

--- a/solution.py
+++ b/solution.py
@@ -393,10 +393,11 @@
     table_shape = shape((number, HEAD_SIZE), F32)
     rows_shape, state = shape((half, width), BF16), shape((half, width), F32)
     heads = width // HEAD_SIZE
-    cut = heads - group
+    moved = group - 1
+    cut = heads - moved
     some_shape = shape((half, cut * HEAD_SIZE), BF16)
     some_state = shape((half, cut * HEAD_SIZE), F32)
-    last_shape = shape((half, group * HEAD_SIZE), BF16)
+    last_shape = shape((half, moved * HEAD_SIZE), BF16)
     near, onward, k_rot, v, q, p, cosine, sinus = call(
         functools.partial(keys_kernel, count),
         "rotate_keys",
@@ -410,7 +411,7 @@
     )(*(in_hbm(array) for array in (keys, values, queries, position_row, frequency)))
     near_pairs = pairs(lambda r: r + 3 if r % 2 else r + 1)
     near_got = lax.ppermute(near, "ctx", near_pairs)
-    early = call(pack_kernel, "pack_early", [vmem] * 5, shape((half, (group + 2) * HEAD_SIZE), BF16), MIB, MIB)(
+    early = call(pack_kernel, "pack_early", [vmem] * 5, shape((half, (moved + 2) * HEAD_SIZE), BF16), MIB, MIB)(
         q, k_rot, v, cosine, sinus
     )
     early, q = lax.optimization_barrier((early, q))
@@ -444,12 +445,9 @@
         12 * MIB,
         scratch=[dma(())],
     )(q, k_rot, v, p, cosine, sinus, near_got, in_hbm(out_weight))
-    early, rot = lax.optimization_barrier((early, rot))
-    attend_early = call(
-        functools.partial(early_kernel, count), "early_rows", [vmem] * 3, last_shape, 256 * MIB, 4 * MIB
-    )
-    last = attend_early(early, near_got, p)
-    rot, next_got, last, early_got = lax.optimization_barrier((rot, next_got, last, early_got))
+    rot, early_got = lax.optimization_barrier((rot, early_got))
+    other_near = lax.ppermute(early_got[:, moved * HEAD_SIZE :], "ctx", near_pairs)
+    rot, next_got = lax.optimization_barrier((rot, next_got))
     last_got = lax.ppermute(next_got, "ctx", pairs(lambda r: r + 1 - 2 * (r % 2)))
     state_now = call(
         functools.partial(next_kernel, count, group),
@@ -460,8 +458,7 @@
         4 * MIB,
         aliases={3: 0, 4: 1, 5: 2},
     )(rot, next_got, p, *state_now)
-    parts = range(cut), range(cut, heads - 1), range(heads - 1, heads)
-    rot, first_got = lax.optimization_barrier((rot, first_got))
+    parts = range(heads // 2), range(heads // 2, heads - 1), range(heads - 1, heads)
     seconds, seconds_got = [], []
     for part in parts:
         second = call(
@@ -473,10 +470,15 @@
             4 * MIB,
         )(rot, last_got, p, *state_now)
         seconds_got.append(swapped(second))
-        rot, second, first_got, early_got = lax.optimization_barrier((rot, second, first_got, early_got))
+        if len(seconds) == 0:
+            rot, second, first_got = lax.optimization_barrier((rot, second, first_got))
+        else:
+            rot, second, other_near, early = lax.optimization_barrier((rot, second, other_near, early))
         seconds.append(second)
-        if len(seconds) == 2:
-            other_near = lax.ppermute(early_got[:, group * HEAD_SIZE :], "ctx", near_pairs)
+    attend_early = call(
+        functools.partial(early_kernel, count), "early_rows", [vmem] * 3, last_shape, 256 * MIB, 4 * MIB
+    )
+    last = attend_early(early, near_got, p)
     sum_shape = shape((half, columns), F32)
     first_sum, partial_sum = call(
         project_kernel, "project_own", [vmem] * 6, [sum_shape, sum_shape], 2048 * MIB, 8 * MIB

time: 38.5 us -> 36.3 us (0.943)
  waiting for transfers between devices: 7.41 us -> 6.31 us
  starting transfers between devices: 11.4 us -> 10.5 us
    ppermute x1, waiting for transfers between devices: 3.83 us -> 0.47 us  [shards(): lax.ppermute(early_got[:, moved * HEAD_SIZE:], 'ctx', near_pairs)]
    ppermute x5, starting transfers between devices: 9.16 us -> 7.71 us  [swapped(): return lax.ppermute(array, 'head', [(0, 1), (1, 0)])]
    ppermute x1, waiting for transfers between devices: 0.62 us -> 1.88 us  [shards(): next_got = lax.ppermute(onward, 'ctx', pairs(lambda r: r + 2))]
    ppermute x5, waiting for transfers between devices: 0.19 us -> 1.3 us  [swapped(): return lax.ppermute(array, 'head', [(0, 1), (1, 0)])]
    ppermute x1, starting transfers between devices: 0.01 us -> 0.59 us  [shards(): lax.ppermute(early_got[:, moved * HEAD_SIZE:], 'ctx', near_pairs)]
  transfers between devices with their start and end apart: 9 -> 9, of which waited for: 4 -> 4; matrix products, arithmetic and copies ran while one was open for 0% -> 0% of each run, Pallas kernels for 41% -> 45%
where the time goes in v3:
time: 36.3 us; the launch traced here: 36.1 us
  Pallas kernels  19 us (52%)
  starting transfers between devices  10.5 us (29%)
  waiting for transfers between devices  6.31 us (17%)
    ppermute x5, starting transfers between devices, swapped(): return lax.ppermute(array, 'head', [(0, 1), (1, 0)])  7.71 us
    pallas_call x1, Pallas kernels, shards(): call(functools.partial(second_kernel, count, group), 'second_rows', [vmem...  3.39 us
    ppermute x1, waiting for transfers between devices, shards(): near_got = lax.ppermute(near, 'ctx', near_pairs)  2.65 us
    pallas_call x1, Pallas kernels, shards(): call(project_kernel, 'project_own', [vmem] * 6, [sum_shape, sum_shape], 2...  2.38 us
    pallas_call x1, Pallas kernels, shards(): call(first_out_kernel, 'project_first', [vmem] * 4, shape((number, column...  2.08 us
    pallas_call x3, Pallas kernels, shards(): call(functools.partial(third_kernel, count, group, part), 'last_tile', [v...  1.95 us
    ppermute x1, waiting for transfers between devices, shards(): next_got = lax.ppermute(onward, 'ctx', pairs(lambda r: r + 2))  1.88 us
    pallas_call x1, Pallas kernels, shards(): call(functools.partial(next_kernel, count, group), 'next_tile', [vmem] *...  1.73 us
  transfers between devices with their start and end apart: 9, of which 4 were waited for; matrix products, arithmetic and copies ran while one was open for 0% of the time, Pallas kernels for 45%

profile of v3, /device:TPU:0, one launch (start us, length us, event | category | flops | bytes accessed | tf_op | source)
XLA Modules:
  0.0 36.1 jit_solution(16538283674631722761)
XLA Ops:
  0.0 1.5 %rotate_keys.1 = (bf16[256,512]{1,0:T(8,128)(2,1)S(1)}, bf16[256,512]{1,0:T(8,128)(2,1)S(1)}, bf16[512,256]{1,0:T(8,128)(2,1)S(1)}, bf16[512,256]{1,0:T(8,128)(2...) custom-call(bf16[512,256]{1,0:T(8,128)(2,1)} %k_hbm.1, ...), custom_call_target="tpu_custom_call" | custom-call | flops 4194304 | bytes 4194304 | tf_op jit(solution)/shard_map/rotate_keys/pallas_call | solution.py:401
  1.5 0.5 %collective-permute-start = (bf16[256,512]{1,0:T(8,128)(2,1)S(1)}, bf16[256,512]{1,0:T(8,128)(2,1)S(1)}, u32[]{:S(2)}, u32[]{:S(2)}) collective-permute-start(bf16[256,512]{1,0:T(8,128)(2,1)S(1)} %get-tuple-element.64), channel_id=1, source_target_pairs={{0,2},{2,8},{4,6},{6,12},{8,10},{10,16},{12,14},{14,20},{16,18},{1... | collective-permute-start | bytes 786440 | tf_op jit(solution)/shard_map/ppermute | solution.py:413
  2.0 0.2 pack_early.1.early_ref
  2.1 2.6 %collective-permute-start.1 = (bf16[256,640]{1,0:T(8,128)(2,1)S(1)}, bf16[256,640]{1,0:T(8,128)(2,1)S(1)}, u32[]{:S(2)}, u32[]{:S(2)}) collective-permute-start(bf16[256,640]{1,0:T(8,128)(2,1)S(1)} %pack_early.1.early_ref), channel_id=1, source_target_pairs={{0,1},{1,0},{2,3},{3,2},{4,5},{5,4},{6,7},{7,6},{8,9},{9,8},{10,11... | collective-permute-start | bytes 983048 | tf_op jit(solution)/shard_map/ppermute | solution.py:390
  4.7 1.1 %own_tiles.1 = (bf16[256,640]{1,0:T(8,128)(2,1)S(1)}, bf16[256,640]{1,0:T(8,128)(2,1)S(1)}, f32[256,640]{1,0:T(8,128)S(1)}, f32[256,640]{1,0:T(8,128)S(1)}, f32[256,640]{1,0:T(8,128)S(1)}) custom-call(bf16[512,1024]{1,0:T(8,128)(2,1)S(1)} %get-tuple-element.68.q_ref, bf16[512,256]{1,0:T(8,128)(2,1)S(1)} %get-tuple-element.54.k_ref, ...), custom_call_target="tpu_custom_call" | custom-call | flops 268435456 | bytes 4194304 | tf_op jit(solution)/shard_map/own_tiles/pallas_call | solution.py:419
  5.8 1.6 %collective-permute-start.2 = (bf16[256,512]{1,0:T(8,128)(2,1)S(1)}, bf16[256,512]{1,0:T(8,128)(2,1)S(1)}, u32[]{:S(2)}, u32[]{:S(2)}) collective-permute-start(bf16[256,512]{1,0:T(8,128)(2,1)S(1)} %get-tuple-element.72), channel_id=1, source_target_pairs={{0,4},{2,6},{4,8},{6,10},{8,12},{10,14},{12,16},{14,18},{16,20},{1... | collective-permute-start | bytes 786440 | tf_op jit(solution)/shard_map/ppermute | solution.py:428
  7.4 2.6 %collective-permute-done.kv_ref.near_ref = bf16[256,512]{1,0:T(8,128)(2,1)S(1)} collective-permute-done((bf16[256,512]{1,0:T(8,128)(2,1)S(1)}, bf16[256,512]{1,0:T(8,128)(2,1)S(1)}, u32[]{:S(2)}, u32[]{:S(2)}) %collective-permute-start) | collective-permute-done | bytes 262176 | tf_op jit(solution)/shard_map/ppermute | solution.py:413
  10.1 2.1 %collective-permute-start.4 = (bf16[256,640]{1,0:T(8,128)(2,1)S(1)}, bf16[256,640]{1,0:T(8,128)(2,1)S(1)}, u32[]{:S(2)}, u32[]{:S(2)}) collective-permute-start(bf16[256,640]{1,0:T(8,128)(2,1)S(1)} %first_rows.1.first_ref), channel_id=1, source_target_pairs={{0,1},{1,0},{2,3},{3,2},{4,5},{5,4},{6,7},{7,6},{8,9},{9,8},{10,11... | collective-permute-start | bytes 983048 | tf_op jit(solution)/shard_map/ppermute | solution.py:390
  12.1 3.4 %second_rows.1 = (bf16[256,1024]{1,0:T(8,128)(2,1)S(1)}, f32[256,1024]{1,0:T(8,128)S(1)}, f32[256,1024]{1,0:T(8,128)S(1)}, f32[256,1024]{1,0:T(8,128)S(1)}, bf16[2048,2048]{1,0:T(8,128)(2,1)S(1)}) custom-call(bf16[512,1024]{1,0:T(8,128)(2,1)S(1)} %get-tuple-element.68.q_ref, bf16[512,256]{1,0:T(8,128)(2,1)S(1)} %get-tuple-element.54.k_ref, ...), custom_call_target="tpu_custom_call" | custom-call | flops 1073741824 | bytes 12582912 | tf_op jit(solution)/shard_map/second_rows/pallas_call | solution.py:439
  15.5 0.0 collective-permute-done.1.early_ref
  15.6 1.9 %collective-permute-done.2.kv_ref = bf16[256,512]{1,0:T(8,128)(2,1)S(1)} collective-permute-done((bf16[256,512]{1,0:T(8,128)(2,1)S(1)}, bf16[256,512]{1,0:T(8,128)(2,1)S(1)}, u32[]{:S(2)}, u32[]{:S(2)}) %collective-permute-start.2) | collective-permute-done | bytes 262176 | tf_op jit(solution)/shard_map/ppermute | solution.py:428
  17.4 0.2 collective-permute-start.3
  17.6 0.6 %collective-permute-start.5 = (bf16[256,256]{1,0:T(8,128)(2,1)S(1)}, bf16[256,256]{1,0:T(8,128)(2,1)S(1)}, u32[]{:S(2)}, u32[]{:S(2)}) collective-permute-start(bf16[256,256]{1,0:T(8,128)(2,1)S(1)} %slice.3), channel_id=1, source_target_pairs={{0,2},{2,8},{4,6},{6,12},{8,10},{10,16},{12,14},{14,20},{16,18},{1... | collective-permute-start | bytes 393224 | tf_op jit(solution)/shard_map/ppermute | solution.py:449
  18.2 1.7 %next_tile.1 = (f32[256,1024]{1,0:T(8,128)S(1)}, f32[256,1024]{1,0:T(8,128)S(1)}, f32[256,1024]{1,0:T(8,128)S(1)}) custom-call(bf16[256,1024]{1,0:T(8,128)(2,1)S(1)} %get-tuple-element.83.rot_ref, bf16[256,512]{1,0:T(8,128)(2,1)S(1)} %collective-permute-done.2.kv_ref, ...), custom_call_target="tpu_custom_call", output_to_operand_aliasing={{0}: (3, {}), {1}: (4, {}), {2}: (5, {})} | custom-call | flops 536870912 | bytes 4194304 | tf_op jit(solution)/shard_map/next_tile/pallas_call | solution.py:452
  19.9 0.0 collective-permute-done.3.kv_ref
  19.9 0.8 %last_tile.3.second0_ref = bf16[256,512]{1,0:T(8,128)(2,1)S(1)} custom-call(bf16[256,1024]{1,0:T(8,128)(2,1)S(1)} %get-tuple-element.83.rot_ref, bf16[256,512]{1,0:T(8,128)(2,1)S(1)} %collective-permute-done.3.kv_ref, s32[1,512]{1,0:T(1,128)S(1)} %get-tuple-element.59.p_ref, f32[256,1024]{1,0:T(8,128)S(1)} %get-tuple-element.78.acc_ref, ...), custom_call_target="tpu_custom_call" | custom-call | flops 268435456 | bytes 4194304 | tf_op jit(solution)/shard_map/last_tile/pallas_call | solution.py:464
  20.7 0.8 %collective-permute-start.8 = (bf16[256,512]{1,0:T(8,128)(2,1)S(1)}, bf16[256,512]{1,0:T(8,128)(2,1)S(1)}, u32[]{:S(2)}, u32[]{:S(2)}) collective-permute-start(bf16[256,512]{1,0:T(8,128)(2,1)S(1)} %last_tile.3.second0_ref), channel_id=1, source_target_pairs={{0,1},{1,0},{2,3},{3,2},{4,5},{5,4},{6,7},{7,6},{8,9},{9,8},{10,11... | collective-permute-start | bytes 786440 | tf_op jit(solution)/shard_map/ppermute | solution.py:390
  21.6 0.0 collective-permute-done.4.got_ref
  21.6 0.7 %last_tile.4.second1_ref = bf16[256,384]{1,0:T(8,128)(2,1)S(1)} custom-call(bf16[256,1024]{1,0:T(8,128)(2,1)S(1)} %get-tuple-element.83.rot_ref, bf16[256,512]{1,0:T(8,128)(2,1)S(1)} %collective-permute-done.3.kv_ref, s32[1,512]{1,0:T(1,128)S(1)} %get-tuple-element.59.p_ref, f32[256,1024]{1,0:T(8,128)S(1)} %get-tuple-element.78.acc_ref, ...), custom_call_target="tpu_custom_call" | custom-call | flops 268435456 | bytes 4194304 | tf_op jit(solution)/shard_map/last_tile/pallas_call | solution.py:464
  22.2 1.3 %collective-permute-start.7 = (bf16[256,384]{1,0:T(8,128)(2,1)S(1)}, bf16[256,384]{1,0:T(8,128)(2,1)S(1)}, u32[]{:S(2)}, u32[]{:S(2)}) collective-permute-start(bf16[256,384]{1,0:T(8,128)(2,1)S(1)} %last_tile.4.second1_ref), channel_id=1, source_target_pairs={{0,1},{1,0},{2,3},{3,2},{4,5},{5,4},{6,7},{7,6},{8,9},{9,8},{10,11... | collective-permute-start | bytes 589832 | tf_op jit(solution)/shard_map/ppermute | solution.py:390
  23.6 0.5 %collective-permute-done.5.near_ref = bf16[256,256]{1,0:T(8,128)(2,1)S(1)} collective-permute-done((bf16[256,256]{1,0:T(8,128)(2,1)S(1)}, bf16[256,256]{1,0:T(8,128)(2,1)S(1)}, u32[]{:S(2)}, u32[]{:S(2)}) %collective-permute-start.5) | collective-permute-done | bytes 131104 | tf_op jit(solution)/shard_map/ppermute | solution.py:449
  24.0 0.5 %last_tile.5.second2_ref = bf16[256,128]{1,0:T(8,128)(2,1)S(1)} custom-call(bf16[256,1024]{1,0:T(8,128)(2,1)S(1)} %get-tuple-element.83.rot_ref, bf16[256,512]{1,0:T(8,128)(2,1)S(1)} %collective-permute-done.3.kv_ref, s32[1,512]{1,0:T(1,128)S(1)} %get-tuple-element.59.p_ref, f32[256,1024]{1,0:T(8,128)S(1)} %get-tuple-element.78.acc_ref, ...), custom_call_target="tpu_custom_call" | custom-call | flops 268435456 | bytes 4194304 | tf_op jit(solution)/shard_map/last_tile/pallas_call | solution.py:464
  24.5 0.9 %collective-permute-start.6 = (bf16[256,128]{1,0:T(8,128)(2,1)S(1)}, bf16[256,128]{1,0:T(8,128)(2,1)S(1)}, u32[]{:S(2)}, u32[]{:S(2)}) collective-permute-start(bf16[256,128]{1,0:T(8,128)(2,1)S(1)} %last_tile.5.second2_ref), channel_id=1, source_target_pairs={{0,1},{1,0},{2,3},{3,2},{4,5},{5,4},{6,7},{7,6},{8,9},{9,8},{10,11... | collective-permute-start | bytes 196616 | tf_op jit(solution)/shard_map/ppermute | solution.py:390
  25.5 1.0 %early_rows.2.last_ref = bf16[256,384]{1,0:T(8,128)(2,1)S(1)} custom-call(bf16[256,640]{1,0:T(8,128)(2,1)S(1)} %pack_early.1.early_ref, bf16[256,512]{1,0:T(8,128)(2,1)S(1)} %collective-permute-done.kv_ref.near_ref, s32[1,512]{1,0:T(1,128)S(1)} %get-tuple-element.59.p_ref), custom_call_target="tpu_custom_call" | custom-call | flops 268435456 | bytes 4194304 | tf_op jit(solution)/shard_map/early_rows/pallas_call | solution.py:481
  26.4 2.4 %project_own.1 = (f32[256,2048]{1,0:T(8,128)S(1)}, f32[256,2048]{1,0:T(8,128)S(1)}) custom-call(bf16[256,640]{1,0:T(8,128)(2,1)S(1)} %first_rows.1.first_ref, bf16[256,384]{1,0:T(8,128)(2,1)S(1)} %early_rows.2.last_ref, bf16[256,512]{1,0:T(8,128)(2,1)S(1)} %last_tile.3.second0_ref, bf16[256,384]{1,0:T(8,128)(2,1)S(1)} %last_tile.4.second1_ref, ...), custom_call_target="tpu_custom_call" | custom-call | flops 2147483648 | bytes 8388608 | tf_op jit(solution)/shard_map/project_own/pallas_call | solution.py:483
  28.8 1.0 %early_rows.3.got_last_ref = bf16[256,384]{1,0:T(8,128)(2,1)S(1)} custom-call(bf16[256,640]{1,0:T(8,128)(2,1)S(1)} %collective-permute-done.1.early_ref, bf16[256,256]{1,0:T(8,128)(2,1)S(1)} %collective-permute-done.5.near_ref, s32[1,512]{1,0:T(1,128)S(1)} %get-tuple-element.59.p_ref), custom_call_target="tpu_custom_call" | custom-call | flops 268435456 | bytes 4194304 | tf_op jit(solution)/shard_map/early_rows/pallas_call | solution.py:487
  29.8 2.1 %project_first.1.begun_hbm = bf16[512,2048]{1,0:T(8,128)(2,1)} custom-call(bf16[256,640]{1,0:T(8,128)(2,1)S(1)} %collective-permute-done.4.got_ref, bf16[256,384]{1,0:T(8,128)(2,1)S(1)} %early_rows.3.got_last_ref, f32[256,2048]{1,0:T(8,128)S(1)} %get-tuple-element.97.sum_ref, bf16[2048,2048]{1,0:T(8,128)(2,1)S(1)} %get-tuple-element.92.w_ref), custom_call_target="tpu_custom_call" | custom-call | flops 1073741824 | bytes 8388608 | tf_op jit(solution)/shard_map/project_first/pallas_call | solution.py:488
  31.9 0.7 %project_second.2.part_ref = f32[256,2048]{1,0:T(8,128)S(1)} custom-call(bf16[256,512]{1,0:T(8,128)(2,1)S(1)} %collective-permute-done.8.got_ref, f32[256,2048]{1,0:T(8,128)S(1)} %get-tuple-element.99.part_ref, bf16[2048,2048]{1,0:T(8,128)(2,1)S(1)} %get-tuple-element.92.w_ref), custom_call_target="tpu_custom_call" | custom-call | flops 536870912 | bytes 4194304 | tf_op jit(solution)/shard_map/project_second/pallas_call | solution.py:500
  32.6 1.3 %collective-permute-done.7.got_ref = bf16[256,384]{1,0:T(8,128)(2,1)S(1)} collective-permute-done((bf16[256,384]{1,0:T(8,128)(2,1)S(1)}, bf16[256,384]{1,0:T(8,128)(2,1)S(1)}, u32[]{:S(2)}, u32[]{:S(2)}) %collective-permute-start.7) | collective-permute-done | bytes 196640 | tf_op jit(solution)/shard_map/ppermute | solution.py:390
  33.9 0.7 %project_second.3.part_ref = f32[256,2048]{1,0:T(8,128)S(1)} custom-call(bf16[256,384]{1,0:T(8,128)(2,1)S(1)} %collective-permute-done.7.got_ref, f32[256,2048]{1,0:T(8,128)S(1)} %project_second.2.part_ref, bf16[2048,2048]{1,0:T(8,128)(2,1)S(1)} %get-tuple-element.92.w_ref), custom_call_target="tpu_custom_call" | custom-call | flops 536870912 | bytes 4194304 | tf_op jit(solution)/shard_map/project_second/pallas_call | solution.py:500
  34.7 0.0 collective-permute-done.6.got_ref
  34.7 1.3 %project_last.1 = bf16[512,2048]{1,0:T(8,128)(2,1)} custom-call(bf16[256,128]{1,0:T(8,128)(2,1)S(1)} %collective-permute-done.6.got_ref, f32[256,2048]{1,0:T(8,128)S(1)} %project_second.3.part_ref, bf16[2048,2048]{1,0:T(8,128)(2,1)S(1)} %get-tuple-element.92.w_ref, bf16[512,2048]{1,0:T(8,128)(2,1)} %project_first.1.begun_hbm), custom_call_target="tpu_custom_call", output_to_operand_aliasing={{}: (3, {})} | custom-call | flops 536870912 | bytes 4194304 | tf_op jit(solution)/shard_map/project_last/pallas_call | solution.py:508
  (3 shorter events, 0.0 us)
Async XLA Ops:
  1.5 8.6 %collective-permute-start = (bf16[256,512]{1,0:T(8,128)(2,1)S(1)}, bf16[256,512]{1,0:T(8,128)(2,1)S(1)}, u32[]{:S(2)}, u32[]{:S(2)}) collective-permute-start(bf16[256,512]{1,0:T(8,128)(2,1)S(1)} %get-tuple-element.64), channel_id=1, source_target_pairs={{0,2},{2,8},{4,6},{6,12},{8,10},{10,16},{12,14},{14,20},{16,18},{1... | collective-permute-start | bytes 786440 | tf_op jit(solution)/shard_map/ppermute | solution.py:413
  2.1 13.4 %collective-permute-start.1 = (bf16[256,640]{1,0:T(8,128)(2,1)S(1)}, bf16[256,640]{1,0:T(8,128)(2,1)S(1)}, u32[]{:S(2)}, u32[]{:S(2)}) collective-permute-start(bf16[256,640]{1,0:T(8,128)(2,1)S(1)} %pack_early.1.early_ref), channel_id=1, source_target_pairs={{0,1},{1,0},{2,3},{3,2},{4,5},{5,4},{6,7},{7,6},{8,9},{9,8},{10,11... | collective-permute-start | bytes 983048 | tf_op jit(solution)/shard_map/ppermute | solution.py:390
  5.8 11.6 %collective-permute-start.2 = (bf16[256,512]{1,0:T(8,128)(2,1)S(1)}, bf16[256,512]{1,0:T(8,128)(2,1)S(1)}, u32[]{:S(2)}, u32[]{:S(2)}) collective-permute-start(bf16[256,512]{1,0:T(8,128)(2,1)S(1)} %get-tuple-element.72), channel_id=1, source_target_pairs={{0,4},{2,6},{4,8},{6,10},{8,12},{10,14},{12,16},{14,18},{16,20},{1... | collective-permute-start | bytes 786440 | tf_op jit(solution)/shard_map/ppermute | solution.py:428
  10.1 11.5 %collective-permute-start.4 = (bf16[256,640]{1,0:T(8,128)(2,1)S(1)}, bf16[256,640]{1,0:T(8,128)(2,1)S(1)}, u32[]{:S(2)}, u32[]{:S(2)}) collective-permute-start(bf16[256,640]{1,0:T(8,128)(2,1)S(1)} %first_rows.1.first_ref), channel_id=1, source_target_pairs={{0,1},{1,0},{2,3},{3,2},{4,5},{5,4},{6,7},{7,6},{8,9},{9,8},{10,11... | collective-permute-start | bytes 983048 | tf_op jit(solution)/shard_map/ppermute | solution.py:390
  17.4 2.5 %collective-permute-start.3 = (bf16[256,512]{1,0:T(8,128)(2,1)S(1)}, bf16[256,512]{1,0:T(8,128)(2,1)S(1)}, u32[]{:S(2)}, u32[]{:S(2)}) collective-permute-start(bf16[256,512]{1,0:T(8,128)(2,1)S(1)} %collective-permute-done.2.kv_ref), channel_id=1, source_target_pairs={{0,2},{2,0},{4,6},{6,4},{8,10},{10,8},{12,14},{14,12},{16,18},{18,... | collective-permute-start | bytes 786440 | tf_op jit(solution)/shard_map/ppermute | solution.py:451
  17.6 6.4 %collective-permute-start.5 = (bf16[256,256]{1,0:T(8,128)(2,1)S(1)}, bf16[256,256]{1,0:T(8,128)(2,1)S(1)}, u32[]{:S(2)}, u32[]{:S(2)}) collective-permute-start(bf16[256,256]{1,0:T(8,128)(2,1)S(1)} %slice.3), channel_id=1, source_target_pairs={{0,2},{2,8},{4,6},{6,12},{8,10},{10,16},{12,14},{14,20},{16,18},{1... | collective-permute-start | bytes 393224 | tf_op jit(solution)/shard_map/ppermute | solution.py:449
  20.7 11.2 %collective-permute-start.8 = (bf16[256,512]{1,0:T(8,128)(2,1)S(1)}, bf16[256,512]{1,0:T(8,128)(2,1)S(1)}, u32[]{:S(2)}, u32[]{:S(2)}) collective-permute-start(bf16[256,512]{1,0:T(8,128)(2,1)S(1)} %last_tile.3.second0_ref), channel_id=1, source_target_pairs={{0,1},{1,0},{2,3},{3,2},{4,5},{5,4},{6,7},{7,6},{8,9},{9,8},{10,11... | collective-permute-start | bytes 786440 | tf_op jit(solution)/shard_map/ppermute | solution.py:390
  22.2 11.7 %collective-permute-start.7 = (bf16[256,384]{1,0:T(8,128)(2,1)S(1)}, bf16[256,384]{1,0:T(8,128)(2,1)S(1)}, u32[]{:S(2)}, u32[]{:S(2)}) collective-permute-start(bf16[256,384]{1,0:T(8,128)(2,1)S(1)} %last_tile.4.second1_ref), channel_id=1, source_target_pairs={{0,1},{1,0},{2,3},{3,2},{4,5},{5,4},{6,7},{7,6},{8,9},{9,8},{10,11... | collective-permute-start | bytes 589832 | tf_op jit(solution)/shard_map/ppermute | solution.py:390
  24.5 10.1 %collective-permute-start.6 = (bf16[256,128]{1,0:T(8,128)(2,1)S(1)}, bf16[256,128]{1,0:T(8,128)(2,1)S(1)}, u32[]{:S(2)}, u32[]{:S(2)}) collective-permute-start(bf16[256,128]{1,0:T(8,128)(2,1)S(1)} %last_tile.5.second2_ref), channel_id=1, source_target_pairs={{0,1},{1,0},{2,3},{3,2},{4,5},{5,4},{6,7},{7,6},{8,9},{9,8},{10,11... | collective-permute-start | bytes 196616 | tf_op jit(solution)/shard_map/ppermute | solution.py:390

commit v4 on v3

--- a/solution.py
+++ b/solution.py
@@ -445,9 +445,7 @@
         12 * MIB,
         scratch=[dma(())],
     )(q, k_rot, v, p, cosine, sinus, near_got, in_hbm(out_weight))
-    rot, early_got = lax.optimization_barrier((rot, early_got))
-    other_near = lax.ppermute(early_got[:, moved * HEAD_SIZE :], "ctx", near_pairs)
-    rot, next_got = lax.optimization_barrier((rot, next_got))
+    rot, next_got, early_got = lax.optimization_barrier((rot, next_got, early_got))
     last_got = lax.ppermute(next_got, "ctx", pairs(lambda r: r + 1 - 2 * (r % 2)))
     state_now = call(
         functools.partial(next_kernel, count, group),
@@ -469,11 +467,12 @@
             256 * MIB,
             4 * MIB,
         )(rot, last_got, p, *state_now)
-        seconds_got.append(swapped(second))
+        if len(seconds) < 2:
+            seconds_got.append(swapped(second))
         if len(seconds) == 0:
-            rot, second, first_got = lax.optimization_barrier((rot, second, first_got))
-        else:
-            rot, second, other_near, early = lax.optimization_barrier((rot, second, other_near, early))
+            rot, second, first_got, early_got = lax.optimization_barrier((rot, second, first_got, early_got))
+            other_near = lax.ppermute(early_got[:, moved * HEAD_SIZE :], "ctx", near_pairs)
+        rot, second, early = lax.optimization_barrier((rot, second, early))
         seconds.append(second)
     attend_early = call(
         functools.partial(early_kernel, count), "early_rows", [vmem] * 3, last_shape, 256 * MIB, 4 * MIB
@@ -483,7 +482,8 @@
     first_sum, partial_sum = call(
         project_kernel, "project_own", [vmem] * 6, [sum_shape, sum_shape], 2048 * MIB, 8 * MIB
     )(first, last, *seconds, w)
-    early_got, partial_sum, first_sum = lax.optimization_barrier((early_got, partial_sum, first_sum))
+    early_got, partial_sum, first_sum, second = lax.optimization_barrier((early_got, partial_sum, first_sum, seconds[-1]))
+    seconds_got.append(swapped(second))
     got_last = attend_early(early_got, other_near, p)
     begun = call(
         first_out_kernel,

time: 36.3 us -> 36.2 us (level)
    ppermute x1, waiting for transfers between devices: 0.47 us -> 2.01 us  [shards(): lax.ppermute(early_got[:, moved * HEAD_SIZE:], 'ctx', near_pairs)]
    ppermute x5, waiting for transfers between devices: 1.3 us -> 0.01 us  [swapped(): return lax.ppermute(array, 'head', [(0, 1), (1, 0)])]
  transfers between devices with their start and end apart: 9 -> 9, of which waited for: 4 -> 3; matrix products, arithmetic and copies ran while one was open for 0% -> 0% of each run, Pallas kernels for 45% -> 45%
where the time goes in v4:
time: 36.2 us; the launch traced here: 36 us
  Pallas kernels  19 us (52%)
  starting transfers between devices  10.2 us (28%)
  waiting for transfers between devices  6.57 us (18%)
    ppermute x5, starting transfers between devices, swapped(): return lax.ppermute(array, 'head', [(0, 1), (1, 0)])  7.71 us
    pallas_call x1, Pallas kernels, shards(): call(functools.partial(second_kernel, count, group), 'second_rows', [vmem...  3.39 us
    ppermute x1, waiting for transfers between devices, shards(): near_got = lax.ppermute(near, 'ctx', near_pairs)  2.65 us
    pallas_call x1, Pallas kernels, shards(): call(project_kernel, 'project_own', [vmem] * 6, [sum_shape, sum_shape], 2...  2.37 us
    pallas_call x1, Pallas kernels, shards(): call(first_out_kernel, 'project_first', [vmem] * 4, shape((number, column...  2.08 us
    ppermute x1, waiting for transfers between devices, shards(): lax.ppermute(early_got[:, moved * HEAD_SIZE:], 'ctx', near_pairs)  2.01 us
    pallas_call x3, Pallas kernels, shards(): call(functools.partial(third_kernel, count, group, part), 'last_tile', [v...  1.95 us
    ppermute x1, waiting for transfers between devices, shards(): next_got = lax.ppermute(onward, 'ctx', pairs(lambda r: r + 2))  1.89 us
  transfers between devices with their start and end apart: 9, of which 3 were waited for; matrix products, arithmetic and copies ran while one was open for 0% of the time, Pallas kernels for 45%

profile of v4, /device:TPU:0, one launch (start us, length us, event | category | flops | bytes accessed | tf_op | source)
XLA Modules:
  0.0 36.0 jit_solution(12437890743551394251)
XLA Ops:
  0.0 1.5 %rotate_keys.1 = (bf16[256,512]{1,0:T(8,128)(2,1)S(1)}, bf16[256,512]{1,0:T(8,128)(2,1)S(1)}, bf16[512,256]{1,0:T(8,128)(2,1)S(1)}, bf16[512,256]{1,0:T(8,128)(2...) custom-call(bf16[512,256]{1,0:T(8,128)(2,1)} %k_hbm.1, ...), custom_call_target="tpu_custom_call" | custom-call | flops 4194304 | bytes 4194304 | tf_op jit(solution)/shard_map/rotate_keys/pallas_call | solution.py:401
  1.5 0.5 %collective-permute-start = (bf16[256,512]{1,0:T(8,128)(2,1)S(1)}, bf16[256,512]{1,0:T(8,128)(2,1)S(1)}, u32[]{:S(2)}, u32[]{:S(2)}) collective-permute-start(bf16[256,512]{1,0:T(8,128)(2,1)S(1)} %get-tuple-element.66), channel_id=1, source_target_pairs={{0,2},{2,8},{4,6},{6,12},{8,10},{10,16},{12,14},{14,20},{16,18},{1... | collective-permute-start | bytes 786440 | tf_op jit(solution)/shard_map/ppermute | solution.py:413
  2.0 0.2 pack_early.1.early_ref
  2.1 2.6 %collective-permute-start.2 = (bf16[256,640]{1,0:T(8,128)(2,1)S(1)}, bf16[256,640]{1,0:T(8,128)(2,1)S(1)}, u32[]{:S(2)}, u32[]{:S(2)}) collective-permute-start(bf16[256,640]{1,0:T(8,128)(2,1)S(1)} %pack_early.1.early_ref), channel_id=1, source_target_pairs={{0,1},{1,0},{2,3},{3,2},{4,5},{5,4},{6,7},{7,6},{8,9},{9,8},{10,11... | collective-permute-start | bytes 983048 | tf_op jit(solution)/shard_map/ppermute | solution.py:390
  4.7 1.1 %own_tiles.1 = (bf16[256,640]{1,0:T(8,128)(2,1)S(1)}, bf16[256,640]{1,0:T(8,128)(2,1)S(1)}, f32[256,640]{1,0:T(8,128)S(1)}, f32[256,640]{1,0:T(8,128)S(1)}, f32[256,640]{1,0:T(8,128)S(1)}) custom-call(bf16[512,1024]{1,0:T(8,128)(2,1)S(1)} %get-tuple-element.70.q_ref, bf16[512,256]{1,0:T(8,128)(2,1)S(1)} %get-tuple-element.56.k_ref, ...), custom_call_target="tpu_custom_call" | custom-call | flops 268435456 | bytes 4194304 | tf_op jit(solution)/shard_map/own_tiles/pallas_call | solution.py:419
  5.8 1.6 %collective-permute-start.1 = (bf16[256,512]{1,0:T(8,128)(2,1)S(1)}, bf16[256,512]{1,0:T(8,128)(2,1)S(1)}, u32[]{:S(2)}, u32[]{:S(2)}) collective-permute-start(bf16[256,512]{1,0:T(8,128)(2,1)S(1)} %get-tuple-element.72), channel_id=1, source_target_pairs={{0,4},{2,6},{4,8},{6,10},{8,12},{10,14},{12,16},{14,18},{16,20},{1... | collective-permute-start | bytes 786440 | tf_op jit(solution)/shard_map/ppermute | solution.py:428
  7.4 2.6 %collective-permute-done.kv_ref.near_ref = bf16[256,512]{1,0:T(8,128)(2,1)S(1)} collective-permute-done((bf16[256,512]{1,0:T(8,128)(2,1)S(1)}, bf16[256,512]{1,0:T(8,128)(2,1)S(1)}, u32[]{:S(2)}, u32[]{:S(2)}) %collective-permute-start) | collective-permute-done | bytes 262176 | tf_op jit(solution)/shard_map/ppermute | solution.py:413
  10.1 2.1 %collective-permute-start.4 = (bf16[256,640]{1,0:T(8,128)(2,1)S(1)}, bf16[256,640]{1,0:T(8,128)(2,1)S(1)}, u32[]{:S(2)}, u32[]{:S(2)}) collective-permute-start(bf16[256,640]{1,0:T(8,128)(2,1)S(1)} %first_rows.1.first_ref), channel_id=1, source_target_pairs={{0,1},{1,0},{2,3},{3,2},{4,5},{5,4},{6,7},{7,6},{8,9},{9,8},{10,11... | collective-permute-start | bytes 983048 | tf_op jit(solution)/shard_map/ppermute | solution.py:390
  12.1 3.4 %second_rows.1 = (bf16[256,1024]{1,0:T(8,128)(2,1)S(1)}, f32[256,1024]{1,0:T(8,128)S(1)}, f32[256,1024]{1,0:T(8,128)S(1)}, f32[256,1024]{1,0:T(8,128)S(1)}, bf16[2048,2048]{1,0:T(8,128)(2,1)S(1)}) custom-call(bf16[512,1024]{1,0:T(8,128)(2,1)S(1)} %get-tuple-element.70.q_ref, bf16[512,256]{1,0:T(8,128)(2,1)S(1)} %get-tuple-element.56.k_ref, ...), custom_call_target="tpu_custom_call" | custom-call | flops 1073741824 | bytes 12582912 | tf_op jit(solution)/shard_map/second_rows/pallas_call | solution.py:439
  15.5 1.9 %collective-permute-done.1.kv_ref = bf16[256,512]{1,0:T(8,128)(2,1)S(1)} collective-permute-done((bf16[256,512]{1,0:T(8,128)(2,1)S(1)}, bf16[256,512]{1,0:T(8,128)(2,1)S(1)}, u32[]{:S(2)}, u32[]{:S(2)}) %collective-permute-start.1) | collective-permute-done | bytes 262176 | tf_op jit(solution)/shard_map/ppermute | solution.py:428
  17.4 0.2 collective-permute-start.3
  17.6 1.7 %next_tile.1 = (f32[256,1024]{1,0:T(8,128)S(1)}, f32[256,1024]{1,0:T(8,128)S(1)}, f32[256,1024]{1,0:T(8,128)S(1)}) custom-call(bf16[256,1024]{1,0:T(8,128)(2,1)S(1)} %get-tuple-element.89.rot_ref, bf16[256,512]{1,0:T(8,128)(2,1)S(1)} %collective-permute-done.1.kv_ref, ...), custom_call_target="tpu_custom_call", output_to_operand_aliasing={{0}: (3, {}), {1}: (4, {}), {2}: (5, {})} | custom-call | flops 536870912 | bytes 4194304 | tf_op jit(solution)/shard_map/next_tile/pallas_call | solution.py:450
  19.3 0.0 collective-permute-done.3.kv_ref
  19.3 0.8 %last_tile.3.second0_ref = bf16[256,512]{1,0:T(8,128)(2,1)S(1)} custom-call(bf16[256,1024]{1,0:T(8,128)(2,1)S(1)} %get-tuple-element.89.rot_ref, bf16[256,512]{1,0:T(8,128)(2,1)S(1)} %collective-permute-done.3.kv_ref, s32[1,512]{1,0:T(1,128)S(1)} %get-tuple-element.61.p_ref, f32[256,1024]{1,0:T(8,128)S(1)} %get-tuple-element.79.acc_ref, ...), custom_call_target="tpu_custom_call" | custom-call | flops 268435456 | bytes 4194304 | tf_op jit(solution)/shard_map/last_tile/pallas_call | solution.py:462
  20.1 0.9 %collective-permute-start.7 = (bf16[256,512]{1,0:T(8,128)(2,1)S(1)}, bf16[256,512]{1,0:T(8,128)(2,1)S(1)}, u32[]{:S(2)}, u32[]{:S(2)}) collective-permute-start(bf16[256,512]{1,0:T(8,128)(2,1)S(1)} %last_tile.3.second0_ref), channel_id=1, source_target_pairs={{0,1},{1,0},{2,3},{3,2},{4,5},{5,4},{6,7},{7,6},{8,9},{9,8},{10,11... | collective-permute-start | bytes 786440 | tf_op jit(solution)/shard_map/ppermute | solution.py:390
  21.0 0.0 collective-permute-done.4.got_ref
  21.0 0.7 %last_tile.4.second1_ref = bf16[256,384]{1,0:T(8,128)(2,1)S(1)} custom-call(bf16[256,1024]{1,0:T(8,128)(2,1)S(1)} %get-tuple-element.89.rot_ref, bf16[256,512]{1,0:T(8,128)(2,1)S(1)} %collective-permute-done.3.kv_ref, s32[1,512]{1,0:T(1,128)S(1)} %get-tuple-element.61.p_ref, f32[256,1024]{1,0:T(8,128)S(1)} %get-tuple-element.79.acc_ref, ...), custom_call_target="tpu_custom_call" | custom-call | flops 268435456 | bytes 4194304 | tf_op jit(solution)/shard_map/last_tile/pallas_call | solution.py:462
  21.7 1.4 %collective-permute-start.6 = (bf16[256,384]{1,0:T(8,128)(2,1)S(1)}, bf16[256,384]{1,0:T(8,128)(2,1)S(1)}, u32[]{:S(2)}, u32[]{:S(2)}) collective-permute-start(bf16[256,384]{1,0:T(8,128)(2,1)S(1)} %last_tile.4.second1_ref), channel_id=1, source_target_pairs={{0,1},{1,0},{2,3},{3,2},{4,5},{5,4},{6,7},{7,6},{8,9},{9,8},{10,11... | collective-permute-start | bytes 589832 | tf_op jit(solution)/shard_map/ppermute | solution.py:390
  23.1 0.5 %last_tile.5.second2_ref = bf16[256,128]{1,0:T(8,128)(2,1)S(1)} custom-call(bf16[256,1024]{1,0:T(8,128)(2,1)S(1)} %get-tuple-element.89.rot_ref, bf16[256,512]{1,0:T(8,128)(2,1)S(1)} %collective-permute-done.3.kv_ref, s32[1,512]{1,0:T(1,128)S(1)} %get-tuple-element.61.p_ref, f32[256,1024]{1,0:T(8,128)S(1)} %get-tuple-element.79.acc_ref, ...), custom_call_target="tpu_custom_call" | custom-call | flops 268435456 | bytes 4194304 | tf_op jit(solution)/shard_map/last_tile/pallas_call | solution.py:462
  23.6 0.2 collective-permute-start.8
  23.9 1.0 %early_rows.2.last_ref = bf16[256,384]{1,0:T(8,128)(2,1)S(1)} custom-call(bf16[256,640]{1,0:T(8,128)(2,1)S(1)} %pack_early.1.early_ref, bf16[256,512]{1,0:T(8,128)(2,1)S(1)} %collective-permute-done.kv_ref.near_ref, s32[1,512]{1,0:T(1,128)S(1)} %get-tuple-element.61.p_ref), custom_call_target="tpu_custom_call" | custom-call | flops 268435456 | bytes 4194304 | tf_op jit(solution)/shard_map/early_rows/pallas_call | solution.py:480
  24.8 2.4 %project_own.1 = (f32[256,2048]{1,0:T(8,128)S(1)}, f32[256,2048]{1,0:T(8,128)S(1)}) custom-call(bf16[256,640]{1,0:T(8,128)(2,1)S(1)} %first_rows.1.first_ref, bf16[256,384]{1,0:T(8,128)(2,1)S(1)} %early_rows.2.last_ref, bf16[256,512]{1,0:T(8,128)(2,1)S(1)} %last_tile.3.second0_ref, bf16[256,384]{1,0:T(8,128)(2,1)S(1)} %last_tile.4.second1_ref, ...), custom_call_target="tpu_custom_call" | custom-call | flops 2147483648 | bytes 8388608 | tf_op jit(solution)/shard_map/project_own/pallas_call | solution.py:482
  27.2 0.8 %collective-permute-start.5 = (bf16[256,128]{1,0:T(8,128)(2,1)S(1)}, bf16[256,128]{1,0:T(8,128)(2,1)S(1)}, u32[]{:S(2)}, u32[]{:S(2)}) collective-permute-start(bf16[256,128]{1,0:T(8,128)(2,1)S(1)} %last_tile.5.second2_ref), channel_id=1, source_target_pairs={{0,1},{1,0},{2,3},{3,2},{4,5},{5,4},{6,7},{7,6},{8,9},{9,8},{10,11... | collective-permute-start | bytes 196616 | tf_op jit(solution)/shard_map/ppermute | solution.py:390
  28.0 2.0 %collective-permute-done.8.near_ref = bf16[256,256]{1,0:T(8,128)(2,1)S(1)} collective-permute-done((bf16[256,256]{1,0:T(8,128)(2,1)S(1)}, bf16[256,256]{1,0:T(8,128)(2,1)S(1)}, u32[]{:S(2)}, u32[]{:S(2)}) %collective-permute-start.8) | collective-permute-done | bytes 131104 | tf_op jit(solution)/shard_map/ppermute | solution.py:474
  30.0 1.0 %early_rows.3.got_last_ref = bf16[256,384]{1,0:T(8,128)(2,1)S(1)} custom-call(bf16[256,640]{1,0:T(8,128)(2,1)S(1)} %collective-permute-done.2.early_ref, bf16[256,256]{1,0:T(8,128)(2,1)S(1)} %collective-permute-done.8.near_ref, s32[1,512]{1,0:T(1,128)S(1)} %get-tuple-element.61.p_ref), custom_call_target="tpu_custom_call" | custom-call | flops 268435456 | bytes 4194304 | tf_op jit(solution)/shard_map/early_rows/pallas_call | solution.py:487
  31.0 2.1 %project_first.1.begun_hbm = bf16[512,2048]{1,0:T(8,128)(2,1)} custom-call(bf16[256,640]{1,0:T(8,128)(2,1)S(1)} %collective-permute-done.4.got_ref, bf16[256,384]{1,0:T(8,128)(2,1)S(1)} %early_rows.3.got_last_ref, f32[256,2048]{1,0:T(8,128)S(1)} %get-tuple-element.101.sum_ref, bf16[2048,2048]{1,0:T(8,128)(2,1)S(1)} %get-tuple-element.95.w_ref), custom_call_target="tpu_custom_call" | custom-call | flops 1073741824 | bytes 8388608 | tf_op jit(solution)/shard_map/project_first/pallas_call | solution.py:488
  33.1 0.0 collective-permute-done.7.got_ref
  33.1 0.7 %project_second.2.part_ref = f32[256,2048]{1,0:T(8,128)S(1)} custom-call(bf16[256,512]{1,0:T(8,128)(2,1)S(1)} %collective-permute-done.7.got_ref, f32[256,2048]{1,0:T(8,128)S(1)} %get-tuple-element.103.part_ref, bf16[2048,2048]{1,0:T(8,128)(2,1)S(1)} %get-tuple-element.95.w_ref), custom_call_target="tpu_custom_call" | custom-call | flops 536870912 | bytes 4194304 | tf_op jit(solution)/shard_map/project_second/pallas_call | solution.py:500
  33.8 0.0 collective-permute-done.6.got_ref
  33.8 0.7 %project_second.3.part_ref = f32[256,2048]{1,0:T(8,128)S(1)} custom-call(bf16[256,384]{1,0:T(8,128)(2,1)S(1)} %collective-permute-done.6.got_ref, f32[256,2048]{1,0:T(8,128)S(1)} %project_second.2.part_ref, bf16[2048,2048]{1,0:T(8,128)(2,1)S(1)} %get-tuple-element.95.w_ref), custom_call_target="tpu_custom_call" | custom-call | flops 536870912 | bytes 4194304 | tf_op jit(solution)/shard_map/project_second/pallas_call | solution.py:500
  34.6 0.0 collective-permute-done.5.got_ref
  34.6 1.3 %project_last.1 = bf16[512,2048]{1,0:T(8,128)(2,1)} custom-call(bf16[256,128]{1,0:T(8,128)(2,1)S(1)} %collective-permute-done.5.got_ref, f32[256,2048]{1,0:T(8,128)S(1)} %project_second.3.part_ref, bf16[2048,2048]{1,0:T(8,128)(2,1)S(1)} %get-tuple-element.95.w_ref, bf16[512,2048]{1,0:T(8,128)(2,1)} %project_first.1.begun_hbm), custom_call_target="tpu_custom_call", output_to_operand_aliasing={{}: (3, {})} | custom-call | flops 536870912 | bytes 4194304 | tf_op jit(solution)/shard_map/project_last/pallas_call | solution.py:508
  (3 shorter events, 0.0 us)
Async XLA Ops:
  1.5 8.6 %collective-permute-start = (bf16[256,512]{1,0:T(8,128)(2,1)S(1)}, bf16[256,512]{1,0:T(8,128)(2,1)S(1)}, u32[]{:S(2)}, u32[]{:S(2)}) collective-permute-start(bf16[256,512]{1,0:T(8,128)(2,1)S(1)} %get-tuple-element.66), channel_id=1, source_target_pairs={{0,2},{2,8},{4,6},{6,12},{8,10},{10,16},{12,14},{14,20},{16,18},{1... | collective-permute-start | bytes 786440 | tf_op jit(solution)/shard_map/ppermute | solution.py:413
  2.1 15.3 %collective-permute-start.2 = (bf16[256,640]{1,0:T(8,128)(2,1)S(1)}, bf16[256,640]{1,0:T(8,128)(2,1)S(1)}, u32[]{:S(2)}, u32[]{:S(2)}) collective-permute-start(bf16[256,640]{1,0:T(8,128)(2,1)S(1)} %pack_early.1.early_ref), channel_id=1, source_target_pairs={{0,1},{1,0},{2,3},{3,2},{4,5},{5,4},{6,7},{7,6},{8,9},{9,8},{10,11... | collective-permute-start | bytes 983048 | tf_op jit(solution)/shard_map/ppermute | solution.py:390
  5.8 11.6 %collective-permute-start.1 = (bf16[256,512]{1,0:T(8,128)(2,1)S(1)}, bf16[256,512]{1,0:T(8,128)(2,1)S(1)}, u32[]{:S(2)}, u32[]{:S(2)}) collective-permute-start(bf16[256,512]{1,0:T(8,128)(2,1)S(1)} %get-tuple-element.72), channel_id=1, source_target_pairs={{0,4},{2,6},{4,8},{6,10},{8,12},{10,14},{12,16},{14,18},{16,20},{1... | collective-permute-start | bytes 786440 | tf_op jit(solution)/shard_map/ppermute | solution.py:428
  10.1 11.0 %collective-permute-start.4 = (bf16[256,640]{1,0:T(8,128)(2,1)S(1)}, bf16[256,640]{1,0:T(8,128)(2,1)S(1)}, u32[]{:S(2)}, u32[]{:S(2)}) collective-permute-start(bf16[256,640]{1,0:T(8,128)(2,1)S(1)} %first_rows.1.first_ref), channel_id=1, source_target_pairs={{0,1},{1,0},{2,3},{3,2},{4,5},{5,4},{6,7},{7,6},{8,9},{9,8},{10,11... | collective-permute-start | bytes 983048 | tf_op jit(solution)/shard_map/ppermute | solution.py:390
  17.4 1.9 %collective-permute-start.3 = (bf16[256,512]{1,0:T(8,128)(2,1)S(1)}, bf16[256,512]{1,0:T(8,128)(2,1)S(1)}, u32[]{:S(2)}, u32[]{:S(2)}) collective-permute-start(bf16[256,512]{1,0:T(8,128)(2,1)S(1)} %collective-permute-done.1.kv_ref), channel_id=1, source_target_pairs={{0,2},{2,0},{4,6},{6,4},{8,10},{10,8},{12,14},{14,12},{16,18},{18,... | collective-permute-start | bytes 786440 | tf_op jit(solution)/shard_map/ppermute | solution.py:449
  20.1 13.0 %collective-permute-start.7 = (bf16[256,512]{1,0:T(8,128)(2,1)S(1)}, bf16[256,512]{1,0:T(8,128)(2,1)S(1)}, u32[]{:S(2)}, u32[]{:S(2)}) collective-permute-start(bf16[256,512]{1,0:T(8,128)(2,1)S(1)} %last_tile.3.second0_ref), channel_id=1, source_target_pairs={{0,1},{1,0},{2,3},{3,2},{4,5},{5,4},{6,7},{7,6},{8,9},{9,8},{10,11... | collective-permute-start | bytes 786440 | tf_op jit(solution)/shard_map/ppermute | solution.py:390
  21.7 12.1 %collective-permute-start.6 = (bf16[256,384]{1,0:T(8,128)(2,1)S(1)}, bf16[256,384]{1,0:T(8,128)(2,1)S(1)}, u32[]{:S(2)}, u32[]{:S(2)}) collective-permute-start(bf16[256,384]{1,0:T(8,128)(2,1)S(1)} %last_tile.4.second1_ref), channel_id=1, source_target_pairs={{0,1},{1,0},{2,3},{3,2},{4,5},{5,4},{6,7},{7,6},{8,9},{9,8},{10,11... | collective-permute-start | bytes 589832 | tf_op jit(solution)/shard_map/ppermute | solution.py:390
  23.6 6.4 %collective-permute-start.8 = (bf16[256,256]{1,0:T(8,128)(2,1)S(1)}, bf16[256,256]{1,0:T(8,128)(2,1)S(1)}, u32[]{:S(2)}, u32[]{:S(2)}) collective-permute-start(bf16[256,256]{1,0:T(8,128)(2,1)S(1)} %slice.3), channel_id=1, source_target_pairs={{0,2},{2,8},{4,6},{6,12},{8,10},{10,16},{12,14},{14,20},{16,18},{1... | collective-permute-start | bytes 393224 | tf_op jit(solution)/shard_map/ppermute | solution.py:474
  27.2 7.4 %collective-permute-start.5 = (bf16[256,128]{1,0:T(8,128)(2,1)S(1)}, bf16[256,128]{1,0:T(8,128)(2,1)S(1)}, u32[]{:S(2)}, u32[]{:S(2)}) collective-permute-start(bf16[256,128]{1,0:T(8,128)(2,1)S(1)} %last_tile.5.second2_ref), channel_id=1, source_target_pairs={{0,1},{1,0},{2,3},{3,2},{4,5},{5,4},{6,7},{7,6},{8,9},{9,8},{10,11... | collective-permute-start | bytes 196616 | tf_op jit(solution)/shard_map/ppermute | solution.py:390

commit v5 on v4

--- a/solution.py
+++ b/solution.py
@@ -299,11 +299,11 @@
     return pl.ds(pl.multiple_of(base + begin, HEAD_SIZE), end - begin)
 
 
-def project_kernel(first_ref, last_ref, second0_ref, second1_ref, second2_ref, w_ref, sum_ref, part_ref):
+def project_kernel(first_ref, last_ref, second0_ref, second1_ref, w_ref, sum_ref, part_ref):
     half, depth = first_ref.shape[0], w_ref.shape[0] // 2
     mine = pl.ds(pl.multiple_of(lax.axis_index("head") * depth, depth), depth)
     first = jnp.concatenate([first_ref[...], last_ref[...]], axis=1)
-    second = jnp.concatenate([second0_ref[...], second1_ref[...], second2_ref[...]], axis=1)
+    second = jnp.concatenate([second0_ref[...], second1_ref[...]], axis=1)
     stacked = jnp.concatenate([first, second], axis=0)
     for tile in range(w_ref.shape[1] // TILE):
         at = slice(tile * TILE, (tile + 1) * TILE)
@@ -456,7 +456,7 @@
         4 * MIB,
         aliases={3: 0, 4: 1, 5: 2},
     )(rot, next_got, p, *state_now)
-    parts = range(heads // 2), range(heads // 2, heads - 1), range(heads - 1, heads)
+    parts = range(heads // 2), range(heads // 2, heads)
     seconds, seconds_got = [], []
     for part in parts:
         second = call(
@@ -467,8 +467,7 @@
             256 * MIB,
             4 * MIB,
         )(rot, last_got, p, *state_now)
-        if len(seconds) < 2:
-            seconds_got.append(swapped(second))
+        seconds_got.append(swapped(second))
         if len(seconds) == 0:
             rot, second, first_got, early_got = lax.optimization_barrier((rot, second, first_got, early_got))
             other_near = lax.ppermute(early_got[:, moved * HEAD_SIZE :], "ctx", near_pairs)
@@ -480,10 +479,13 @@
     last = attend_early(early, near_got, p)
     sum_shape = shape((half, columns), F32)
     first_sum, partial_sum = call(
-        project_kernel, "project_own", [vmem] * 6, [sum_shape, sum_shape], 2048 * MIB, 8 * MIB
+        project_kernel, "project_own", [vmem] * 5, [sum_shape, sum_shape], 2048 * MIB, 8 * MIB
     )(first, last, *seconds, w)
-    early_got, partial_sum, first_sum, second = lax.optimization_barrier((early_got, partial_sum, first_sum, seconds[-1]))
-    seconds_got.append(swapped(second))
+    partial_sum, first_sum = lax.optimization_barrier((partial_sum, first_sum))
+    partial_sum = call(
+        functools.partial(add_kernel, 0), "project_second", [vmem] * 3, sum_shape, 512 * MIB, 4 * MIB
+    )(seconds_got[0], partial_sum, w)
+    first_sum, partial_sum, early_got = lax.optimization_barrier((first_sum, partial_sum, early_got))
     got_last = attend_early(early_got, other_near, p)
     begun = call(
         first_out_kernel,
@@ -495,16 +497,6 @@
         out_specs=hbm,
         scratch=[pltpu.VMEM((half, columns), BF16), dma((tiles,))],
     )(first_got, got_last, first_sum, w)
-    begun, partial_sum = lax.optimization_barrier((begun, partial_sum))
-    for part, got in zip(parts[:-1], seconds_got):
-        partial_sum = call(
-            functools.partial(add_kernel, part[0] * HEAD_SIZE),
-            "project_second",
-            [vmem] * 3,
-            sum_shape,
-            512 * MIB,
-            4 * MIB,
-        )(got, partial_sum, w)
     return call(
         functools.partial(last_kernel, parts[-1][0] * HEAD_SIZE),
         "project_last",

time: 36.2 us -> 36.3 us (level)
  waiting for transfers between devices: 6.57 us -> 8.34 us
  Pallas kernels: 19 us -> 18.1 us
  starting transfers between devices: 10.2 us -> 9.37 us
    ppermute x5 -> x4, waiting for transfers between devices: 0.01 us -> 3.8 us  [swapped(): return lax.ppermute(array, 'head', [(0, 1), (1, 0)])]
    ppermute x1, waiting for transfers between devices: 2.01 us -> 0.01 us  [shards(): lax.ppermute(early_got[:, moved * HEAD_SIZE:], 'ctx', near_pairs)]
    ppermute x5 -> x4, starting transfers between devices: 7.71 us -> 6.9 us  [swapped(): return lax.ppermute(array, 'head', [(0, 1), (1, 0)])]
    pallas_call x3 -> x2, Pallas kernels: 3.85 us -> 3.12 us  [the longest x1 2.39 us: shards(): call(project_kernel, 'project_own', [vmem] * 5, [sum_shape, sum_shape], 2...]
    pallas_call x3 -> x2, Pallas kernels: 1.95 us -> 1.55 us  [shards(): call(functools.partial(third_kernel, count, group, part), 'last_tile', [v...]
  transfers between devices with their start and end apart: 9 -> 8, of which waited for: 3 -> 4; matrix products, arithmetic and copies ran while one was open for 0% -> 0% of each run, Pallas kernels for 45% -> 42%
where the time goes in v5:
time: 36.3 us; the launch traced here: 36.1 us
  Pallas kernels  18.1 us (50%)
  starting transfers between devices  9.37 us (26%)
  waiting for transfers between devices  8.34 us (23%)
    ppermute x4, starting transfers between devices, swapped(): return lax.ppermute(array, 'head', [(0, 1), (1, 0)])  6.9 us
    ppermute x4, waiting for transfers between devices, swapped(): return lax.ppermute(array, 'head', [(0, 1), (1, 0)])  3.8 us
    pallas_call x1, Pallas kernels, shards(): call(functools.partial(second_kernel, count, group), 'second_rows', [vmem...  3.39 us
    ppermute x1, waiting for transfers between devices, shards(): near_got = lax.ppermute(near, 'ctx', near_pairs)  2.65 us
    pallas_call x1, Pallas kernels, shards(): call(project_kernel, 'project_own', [vmem] * 5, [sum_shape, sum_shape], 2...  2.39 us
    pallas_call x1, Pallas kernels, shards(): call(first_out_kernel, 'project_first', [vmem] * 4, shape((number, column...  2.05 us
    ppermute x1, waiting for transfers between devices, shards(): next_got = lax.ppermute(onward, 'ctx', pairs(lambda r: r + 2))  1.89 us
    pallas_call x1, Pallas kernels, shards(): call(functools.partial(next_kernel, count, group), 'next_tile', [vmem] *...  1.73 us
  transfers between devices with their start and end apart: 8, of which 4 were waited for; matrix products, arithmetic and copies ran while one was open for 0% of the time, Pallas kernels for 42%

profile of v5, /device:TPU:0, one launch (start us, length us, event | category | flops | bytes accessed | tf_op | source)
XLA Modules:
  0.0 36.1 jit_solution(18289007982080323184)
XLA Ops:
  0.0 1.5 %rotate_keys.1 = (bf16[256,512]{1,0:T(8,128)(2,1)S(1)}, bf16[256,512]{1,0:T(8,128)(2,1)S(1)}, bf16[512,256]{1,0:T(8,128)(2,1)S(1)}, bf16[512,256]{1,0:T(8,128)(2...) custom-call(bf16[512,256]{1,0:T(8,128)(2,1)} %k_hbm.1, ...), custom_call_target="tpu_custom_call" | custom-call | flops 4194304 | bytes 4194304 | tf_op jit(solution)/shard_map/rotate_keys/pallas_call | solution.py:401
  1.5 0.5 %collective-permute-start = (bf16[256,512]{1,0:T(8,128)(2,1)S(1)}, bf16[256,512]{1,0:T(8,128)(2,1)S(1)}, u32[]{:S(2)}, u32[]{:S(2)}) collective-permute-start(bf16[256,512]{1,0:T(8,128)(2,1)S(1)} %get-tuple-element.62), channel_id=1, source_target_pairs={{0,2},{2,8},{4,6},{6,12},{8,10},{10,16},{12,14},{14,20},{16,18},{1... | collective-permute-start | bytes 786440 | tf_op jit(solution)/shard_map/ppermute | solution.py:413
  2.0 0.2 pack_early.1.early_ref
  2.1 2.6 %collective-permute-start.2 = (bf16[256,640]{1,0:T(8,128)(2,1)S(1)}, bf16[256,640]{1,0:T(8,128)(2,1)S(1)}, u32[]{:S(2)}, u32[]{:S(2)}) collective-permute-start(bf16[256,640]{1,0:T(8,128)(2,1)S(1)} %pack_early.1.early_ref), channel_id=1, source_target_pairs={{0,1},{1,0},{2,3},{3,2},{4,5},{5,4},{6,7},{7,6},{8,9},{9,8},{10,11... | collective-permute-start | bytes 983048 | tf_op jit(solution)/shard_map/ppermute | solution.py:390
  4.7 1.1 %own_tiles.1 = (bf16[256,640]{1,0:T(8,128)(2,1)S(1)}, bf16[256,640]{1,0:T(8,128)(2,1)S(1)}, f32[256,640]{1,0:T(8,128)S(1)}, f32[256,640]{1,0:T(8,128)S(1)}, f32[256,640]{1,0:T(8,128)S(1)}) custom-call(bf16[512,1024]{1,0:T(8,128)(2,1)S(1)} %get-tuple-element.66.q_ref, bf16[512,256]{1,0:T(8,128)(2,1)S(1)} %get-tuple-element.52.k_ref, ...), custom_call_target="tpu_custom_call" | custom-call | flops 268435456 | bytes 4194304 | tf_op jit(solution)/shard_map/own_tiles/pallas_call | solution.py:419
  5.8 1.6 %collective-permute-start.1 = (bf16[256,512]{1,0:T(8,128)(2,1)S(1)}, bf16[256,512]{1,0:T(8,128)(2,1)S(1)}, u32[]{:S(2)}, u32[]{:S(2)}) collective-permute-start(bf16[256,512]{1,0:T(8,128)(2,1)S(1)} %get-tuple-element.68), channel_id=1, source_target_pairs={{0,4},{2,6},{4,8},{6,10},{8,12},{10,14},{12,16},{14,18},{16,20},{1... | collective-permute-start | bytes 786440 | tf_op jit(solution)/shard_map/ppermute | solution.py:428
  7.4 2.6 %collective-permute-done.kv_ref.near_ref = bf16[256,512]{1,0:T(8,128)(2,1)S(1)} collective-permute-done((bf16[256,512]{1,0:T(8,128)(2,1)S(1)}, bf16[256,512]{1,0:T(8,128)(2,1)S(1)}, u32[]{:S(2)}, u32[]{:S(2)}) %collective-permute-start) | collective-permute-done | bytes 262176 | tf_op jit(solution)/shard_map/ppermute | solution.py:413
  10.1 2.1 %collective-permute-start.4 = (bf16[256,640]{1,0:T(8,128)(2,1)S(1)}, bf16[256,640]{1,0:T(8,128)(2,1)S(1)}, u32[]{:S(2)}, u32[]{:S(2)}) collective-permute-start(bf16[256,640]{1,0:T(8,128)(2,1)S(1)} %first_rows.1.first_ref), channel_id=1, source_target_pairs={{0,1},{1,0},{2,3},{3,2},{4,5},{5,4},{6,7},{7,6},{8,9},{9,8},{10,11... | collective-permute-start | bytes 983048 | tf_op jit(solution)/shard_map/ppermute | solution.py:390
  12.1 3.4 %second_rows.1 = (bf16[256,1024]{1,0:T(8,128)(2,1)S(1)}, f32[256,1024]{1,0:T(8,128)S(1)}, f32[256,1024]{1,0:T(8,128)S(1)}, f32[256,1024]{1,0:T(8,128)S(1)}, bf16[2048,2048]{1,0:T(8,128)(2,1)S(1)}) custom-call(bf16[512,1024]{1,0:T(8,128)(2,1)S(1)} %get-tuple-element.66.q_ref, bf16[512,256]{1,0:T(8,128)(2,1)S(1)} %get-tuple-element.52.k_ref, ...), custom_call_target="tpu_custom_call" | custom-call | flops 1073741824 | bytes 12582912 | tf_op jit(solution)/shard_map/second_rows/pallas_call | solution.py:439
  15.5 1.9 %collective-permute-done.1.kv_ref = bf16[256,512]{1,0:T(8,128)(2,1)S(1)} collective-permute-done((bf16[256,512]{1,0:T(8,128)(2,1)S(1)}, bf16[256,512]{1,0:T(8,128)(2,1)S(1)}, u32[]{:S(2)}, u32[]{:S(2)}) %collective-permute-start.1) | collective-permute-done | bytes 262176 | tf_op jit(solution)/shard_map/ppermute | solution.py:428
  17.4 0.0 collective-permute-done.2.early_ref
  17.4 0.2 collective-permute-start.3
  17.6 1.7 %next_tile.1 = (f32[256,1024]{1,0:T(8,128)S(1)}, f32[256,1024]{1,0:T(8,128)S(1)}, f32[256,1024]{1,0:T(8,128)S(1)}) custom-call(bf16[256,1024]{1,0:T(8,128)(2,1)S(1)} %get-tuple-element.81.rot_ref, bf16[256,512]{1,0:T(8,128)(2,1)S(1)} %collective-permute-done.1.kv_ref, ...), custom_call_target="tpu_custom_call", output_to_operand_aliasing={{0}: (3, {}), {1}: (4, {}), {2}: (5, {})} | custom-call | flops 536870912 | bytes 4194304 | tf_op jit(solution)/shard_map/next_tile/pallas_call | solution.py:450
  19.3 0.0 collective-permute-done.3.kv_ref
  19.3 0.8 %last_tile.2.second0_ref = bf16[256,512]{1,0:T(8,128)(2,1)S(1)} custom-call(bf16[256,1024]{1,0:T(8,128)(2,1)S(1)} %get-tuple-element.81.rot_ref, bf16[256,512]{1,0:T(8,128)(2,1)S(1)} %collective-permute-done.3.kv_ref, s32[1,512]{1,0:T(1,128)S(1)} %get-tuple-element.57.p_ref, f32[256,1024]{1,0:T(8,128)S(1)} %get-tuple-element.75.acc_ref, ...), custom_call_target="tpu_custom_call" | custom-call | flops 268435456 | bytes 4194304 | tf_op jit(solution)/shard_map/last_tile/pallas_call | solution.py:462
  20.1 0.9 %collective-permute-start.6 = (bf16[256,512]{1,0:T(8,128)(2,1)S(1)}, bf16[256,512]{1,0:T(8,128)(2,1)S(1)}, u32[]{:S(2)}, u32[]{:S(2)}) collective-permute-start(bf16[256,512]{1,0:T(8,128)(2,1)S(1)} %last_tile.2.second0_ref), channel_id=1, source_target_pairs={{0,1},{1,0},{2,3},{3,2},{4,5},{5,4},{6,7},{7,6},{8,9},{9,8},{10,11... | collective-permute-start | bytes 786440 | tf_op jit(solution)/shard_map/ppermute | solution.py:390
  21.0 0.0 collective-permute-done.4.got_ref
  21.0 0.8 %last_tile.3.second1_ref = bf16[256,512]{1,0:T(8,128)(2,1)S(1)} custom-call(bf16[256,1024]{1,0:T(8,128)(2,1)S(1)} %get-tuple-element.81.rot_ref, bf16[256,512]{1,0:T(8,128)(2,1)S(1)} %collective-permute-done.3.kv_ref, s32[1,512]{1,0:T(1,128)S(1)} %get-tuple-element.57.p_ref, f32[256,1024]{1,0:T(8,128)S(1)} %get-tuple-element.75.acc_ref, ...), custom_call_target="tpu_custom_call" | custom-call | flops 268435456 | bytes 4194304 | tf_op jit(solution)/shard_map/last_tile/pallas_call | solution.py:462
  21.8 1.4 %collective-permute-start.5 = (bf16[256,512]{1,0:T(8,128)(2,1)S(1)}, bf16[256,512]{1,0:T(8,128)(2,1)S(1)}, u32[]{:S(2)}, u32[]{:S(2)}) collective-permute-start(bf16[256,512]{1,0:T(8,128)(2,1)S(1)} %last_tile.3.second1_ref), channel_id=1, source_target_pairs={{0,1},{1,0},{2,3},{3,2},{4,5},{5,4},{6,7},{7,6},{8,9},{9,8},{10,11... | collective-permute-start | bytes 786440 | tf_op jit(solution)/shard_map/ppermute | solution.py:390
  23.2 0.2 collective-permute-start.7
  23.4 1.0 %early_rows.2.last_ref = bf16[256,384]{1,0:T(8,128)(2,1)S(1)} custom-call(bf16[256,640]{1,0:T(8,128)(2,1)S(1)} %pack_early.1.early_ref, bf16[256,512]{1,0:T(8,128)(2,1)S(1)} %collective-permute-done.kv_ref.near_ref, s32[1,512]{1,0:T(1,128)S(1)} %get-tuple-element.57.p_ref), custom_call_target="tpu_custom_call" | custom-call | flops 268435456 | bytes 4194304 | tf_op jit(solution)/shard_map/early_rows/pallas_call | solution.py:479
  24.4 2.4 %project_own.1 = (f32[256,2048]{1,0:T(8,128)S(1)}, f32[256,2048]{1,0:T(8,128)S(1)}) custom-call(bf16[256,640]{1,0:T(8,128)(2,1)S(1)} %first_rows.1.first_ref, bf16[256,384]{1,0:T(8,128)(2,1)S(1)} %early_rows.2.last_ref, bf16[256,512]{1,0:T(8,128)(2,1)S(1)} %last_tile.2.second0_ref, bf16[256,512]{1,0:T(8,128)(2,1)S(1)} %last_tile.3.second1_ref, ...), custom_call_target="tpu_custom_call" | custom-call | flops 2147483648 | bytes 8388608 | tf_op jit(solution)/shard_map/project_own/pallas_call | solution.py:481
  26.8 2.5 %collective-permute-done.6.got_ref = bf16[256,512]{1,0:T(8,128)(2,1)S(1)} collective-permute-done((bf16[256,512]{1,0:T(8,128)(2,1)S(1)}, bf16[256,512]{1,0:T(8,128)(2,1)S(1)}, u32[]{:S(2)}, u32[]{:S(2)}) %collective-permute-start.6) | collective-permute-done | bytes 262176 | tf_op jit(solution)/shard_map/ppermute | solution.py:390
  29.3 0.7 %project_second.1.part_ref = f32[256,2048]{1,0:T(8,128)S(1)} custom-call(bf16[256,512]{1,0:T(8,128)(2,1)S(1)} %collective-permute-done.6.got_ref, f32[256,2048]{1,0:T(8,128)S(1)} %get-tuple-element.91.part_ref, bf16[2048,2048]{1,0:T(8,128)(2,1)S(1)} %get-tuple-element.87.w_ref), custom_call_target="tpu_custom_call" | custom-call | flops 536870912 | bytes 4194304 | tf_op jit(solution)/shard_map/project_second/pallas_call | solution.py:485
  30.1 0.0 collective-permute-done.7.near_ref
  30.1 1.0 %early_rows.3.got_last_ref = bf16[256,384]{1,0:T(8,128)(2,1)S(1)} custom-call(bf16[256,640]{1,0:T(8,128)(2,1)S(1)} %collective-permute-done.2.early_ref, bf16[256,256]{1,0:T(8,128)(2,1)S(1)} %collective-permute-done.7.near_ref, s32[1,512]{1,0:T(1,128)S(1)} %get-tuple-element.57.p_ref), custom_call_target="tpu_custom_call" | custom-call | flops 268435456 | bytes 4194304 | tf_op jit(solution)/shard_map/early_rows/pallas_call | solution.py:489
  31.0 2.1 %project_first.1.begun_hbm = bf16[512,2048]{1,0:T(8,128)(2,1)} custom-call(bf16[256,640]{1,0:T(8,128)(2,1)S(1)} %collective-permute-done.4.got_ref, bf16[256,384]{1,0:T(8,128)(2,1)S(1)} %early_rows.3.got_last_ref, f32[256,2048]{1,0:T(8,128)S(1)} %get-tuple-element.96.sum_ref, bf16[2048,2048]{1,0:T(8,128)(2,1)S(1)} %get-tuple-element.87.w_ref), custom_call_target="tpu_custom_call" | custom-call | flops 1073741824 | bytes 8388608 | tf_op jit(solution)/shard_map/project_first/pallas_call | solution.py:490
  33.1 1.3 %collective-permute-done.5.got_ref = bf16[256,512]{1,0:T(8,128)(2,1)S(1)} collective-permute-done((bf16[256,512]{1,0:T(8,128)(2,1)S(1)}, bf16[256,512]{1,0:T(8,128)(2,1)S(1)}, u32[]{:S(2)}, u32[]{:S(2)}) %collective-permute-start.5) | collective-permute-done | bytes 262176 | tf_op jit(solution)/shard_map/ppermute | solution.py:390
  34.4 1.6 %project_last.1 = bf16[512,2048]{1,0:T(8,128)(2,1)} custom-call(bf16[256,512]{1,0:T(8,128)(2,1)S(1)} %collective-permute-done.5.got_ref, f32[256,2048]{1,0:T(8,128)S(1)} %project_second.1.part_ref, bf16[2048,2048]{1,0:T(8,128)(2,1)S(1)} %get-tuple-element.87.w_ref, bf16[512,2048]{1,0:T(8,128)(2,1)} %project_first.1.begun_hbm), custom_call_target="tpu_custom_call", output_to_operand_aliasing={{}: (3, {})} | custom-call | flops 536870912 | bytes 4194304 | tf_op jit(solution)/shard_map/project_last/pallas_call | solution.py:500
  (2 shorter events, 0.0 us)
Async XLA Ops:
  1.5 8.6 %collective-permute-start = (bf16[256,512]{1,0:T(8,128)(2,1)S(1)}, bf16[256,512]{1,0:T(8,128)(2,1)S(1)}, u32[]{:S(2)}, u32[]{:S(2)}) collective-permute-start(bf16[256,512]{1,0:T(8,128)(2,1)S(1)} %get-tuple-element.62), channel_id=1, source_target_pairs={{0,2},{2,8},{4,6},{6,12},{8,10},{10,16},{12,14},{14,20},{16,18},{1... | collective-permute-start | bytes 786440 | tf_op jit(solution)/shard_map/ppermute | solution.py:413
  2.1 15.3 %collective-permute-start.2 = (bf16[256,640]{1,0:T(8,128)(2,1)S(1)}, bf16[256,640]{1,0:T(8,128)(2,1)S(1)}, u32[]{:S(2)}, u32[]{:S(2)}) collective-permute-start(bf16[256,640]{1,0:T(8,128)(2,1)S(1)} %pack_early.1.early_ref), channel_id=1, source_target_pairs={{0,1},{1,0},{2,3},{3,2},{4,5},{5,4},{6,7},{7,6},{8,9},{9,8},{10,11... | collective-permute-start | bytes 983048 | tf_op jit(solution)/shard_map/ppermute | solution.py:390
  5.8 11.6 %collective-permute-start.1 = (bf16[256,512]{1,0:T(8,128)(2,1)S(1)}, bf16[256,512]{1,0:T(8,128)(2,1)S(1)}, u32[]{:S(2)}, u32[]{:S(2)}) collective-permute-start(bf16[256,512]{1,0:T(8,128)(2,1)S(1)} %get-tuple-element.68), channel_id=1, source_target_pairs={{0,4},{2,6},{4,8},{6,10},{8,12},{10,14},{12,16},{14,18},{16,20},{1... | collective-permute-start | bytes 786440 | tf_op jit(solution)/shard_map/ppermute | solution.py:428
  10.1 11.0 %collective-permute-start.4 = (bf16[256,640]{1,0:T(8,128)(2,1)S(1)}, bf16[256,640]{1,0:T(8,128)(2,1)S(1)}, u32[]{:S(2)}, u32[]{:S(2)}) collective-permute-start(bf16[256,640]{1,0:T(8,128)(2,1)S(1)} %first_rows.1.first_ref), channel_id=1, source_target_pairs={{0,1},{1,0},{2,3},{3,2},{4,5},{5,4},{6,7},{7,6},{8,9},{9,8},{10,11... | collective-permute-start | bytes 983048 | tf_op jit(solution)/shard_map/ppermute | solution.py:390
  17.4 1.9 %collective-permute-start.3 = (bf16[256,512]{1,0:T(8,128)(2,1)S(1)}, bf16[256,512]{1,0:T(8,128)(2,1)S(1)}, u32[]{:S(2)}, u32[]{:S(2)}) collective-permute-start(bf16[256,512]{1,0:T(8,128)(2,1)S(1)} %collective-permute-done.1.kv_ref), channel_id=1, source_target_pairs={{0,2},{2,0},{4,6},{6,4},{8,10},{10,8},{12,14},{14,12},{16,18},{18,... | collective-permute-start | bytes 786440 | tf_op jit(solution)/shard_map/ppermute | solution.py:449
  20.1 9.2 %collective-permute-start.6 = (bf16[256,512]{1,0:T(8,128)(2,1)S(1)}, bf16[256,512]{1,0:T(8,128)(2,1)S(1)}, u32[]{:S(2)}, u32[]{:S(2)}) collective-permute-start(bf16[256,512]{1,0:T(8,128)(2,1)S(1)} %last_tile.2.second0_ref), channel_id=1, source_target_pairs={{0,1},{1,0},{2,3},{3,2},{4,5},{5,4},{6,7},{7,6},{8,9},{9,8},{10,11... | collective-permute-start | bytes 786440 | tf_op jit(solution)/shard_map/ppermute | solution.py:390
  21.8 12.6 %collective-permute-start.5 = (bf16[256,512]{1,0:T(8,128)(2,1)S(1)}, bf16[256,512]{1,0:T(8,128)(2,1)S(1)}, u32[]{:S(2)}, u32[]{:S(2)}) collective-permute-start(bf16[256,512]{1,0:T(8,128)(2,1)S(1)} %last_tile.3.second1_ref), channel_id=1, source_target_pairs={{0,1},{1,0},{2,3},{3,2},{4,5},{5,4},{6,7},{7,6},{8,9},{9,8},{10,11... | collective-permute-start | bytes 786440 | tf_op jit(solution)/shard_map/ppermute | solution.py:390
  23.2 6.9 %collective-permute-start.7 = (bf16[256,256]{1,0:T(8,128)(2,1)S(1)}, bf16[256,256]{1,0:T(8,128)(2,1)S(1)}, u32[]{:S(2)}, u32[]{:S(2)}) collective-permute-start(bf16[256,256]{1,0:T(8,128)(2,1)S(1)} %slice.3), channel_id=1, source_target_pairs={{0,2},{2,8},{4,6},{6,12},{8,10},{10,16},{12,14},{14,20},{16,18},{1... | collective-permute-start | bytes 393224 | tf_op jit(solution)/shard_map/ppermute | solution.py:473

commit v6 on v3

--- a/solution.py
+++ b/solution.py
@@ -257,28 +257,29 @@
     copy.wait()
 
 
-def next_kernel(count, group, rot_ref, kv_ref, p_ref, acc_ref, top_ref, sum_ref, *outs):
+def next_kernel(count, group, heads, rot_ref, kv_ref, p_ref, acc_ref, top_ref, sum_ref, *outs):
     rank = lax.axis_index("ctx")
     width = kv_ref.shape[1] // 2
     biases = tile_biases(half_positions(p_ref, rank, False), [(distance(rank, 2, count), False)])
-    for head in range(rot_ref.shape[1] // HEAD_SIZE):
+    for number, head in enumerate(heads):
         at, key_at, value_at = head_slices(head, group, width)
         state = acc_ref[:, at], top_ref[:, at], sum_ref[:, at]
-        if head % group == 0:
+        if number == 0 or head % group == 0:
             value = with_ones(kv_ref[:, value_at])
         state = added_tile(*state, rot_ref[:, at], kv_ref[:, key_at], value, *biases)
         for out_ref, entries in zip(outs, state):
-            out_ref[:, at] = entries
-
-
-def third_kernel(count, group, heads, rot_ref, kv_ref, p_ref, acc_ref, top_ref, sum_ref, out_ref):
+            out_ref[:, number * HEAD_SIZE : (number + 1) * HEAD_SIZE] = entries
+
+
+def third_kernel(count, group, heads, base, rot_ref, kv_ref, p_ref, acc_ref, top_ref, sum_ref, out_ref):
     rank = lax.axis_index("ctx")
     width = kv_ref.shape[1] // 2
     step = jnp.where(rank % 2 == 1, 3, 1)
     biases = tile_biases(half_positions(p_ref, rank, False), [(distance(rank, step, count), False)])
     for number, head in enumerate(heads):
         at, key_at, value_at = head_slices(head, group, width)
-        state = acc_ref[:, at], top_ref[:, at], sum_ref[:, at]
+        held = slice((head - base) * HEAD_SIZE, (head - base + 1) * HEAD_SIZE)
+        state = acc_ref[:, held], top_ref[:, held], sum_ref[:, held]
         if number == 0 or head % group == 0:
             value = with_ones(kv_ref[:, value_at])
         state = added_tile(*state, rot_ref[:, at], kv_ref[:, key_at], value, *biases)
@@ -449,26 +450,26 @@
     other_near = lax.ppermute(early_got[:, moved * HEAD_SIZE :], "ctx", near_pairs)
     rot, next_got = lax.optimization_barrier((rot, next_got))
     last_got = lax.ppermute(next_got, "ctx", pairs(lambda r: r + 1 - 2 * (r % 2)))
-    state_now = call(
-        functools.partial(next_kernel, count, group),
-        "next_tile",
-        [vmem] * 6,
-        [state, state, state],
-        512 * MIB,
-        4 * MIB,
-        aliases={3: 0, 4: 1, 5: 2},
-    )(rot, next_got, p, *state_now)
+    def with_next_tile(part, rot):
+        held = shape((half, len(part) * HEAD_SIZE), F32)
+        return call(
+            functools.partial(next_kernel, count, group, part), "next_tile", [vmem] * 6, [held] * 3, 512 * MIB, 4 * MIB
+        )(rot, next_got, p, *state_now)
+
     parts = range(heads // 2), range(heads // 2, heads - 1), range(heads - 1, heads)
     seconds, seconds_got = [], []
     for part in parts:
+        if len(seconds) < 2:
+            base = part[0]
+            held_state = with_next_tile(range(base, base + heads // 2), rot)
         second = call(
-            functools.partial(third_kernel, count, group, part),
+            functools.partial(third_kernel, count, group, part, base),
             "last_tile",
             [vmem] * 6,
             shape((half, len(part) * HEAD_SIZE), BF16),
             256 * MIB,
             4 * MIB,
-        )(rot, last_got, p, *state_now)
+        )(rot, last_got, p, *held_state)
         seconds_got.append(swapped(second))
         if len(seconds) == 0:
             rot, second, first_got = lax.optimization_barrier((rot, second, first_got))

time: 36.3 us -> 35.4 us (0.975)
  waiting for transfers between devices: 6.31 us -> 5.19 us
  starting transfers between devices: 10.5 us -> 11 us
    ppermute x5, waiting for transfers between devices: 1.3 us -> 0.49 us  [swapped(): return lax.ppermute(array, 'head', [(0, 1), (1, 0)])]
    ppermute x5, starting transfers between devices: 7.71 us -> 8.17 us  [swapped(): return lax.ppermute(array, 'head', [(0, 1), (1, 0)])]
    pallas_call x4 -> x5, Pallas kernels: 3.68 us -> 3.51 us  [the longest x3 1.95 us: shards(): call(functools.partial(third_kernel, count, group, part, base), 'last_til...]
where the time goes in v6:
time: 35.4 us; the launch traced here: 35.3 us
  Pallas kernels  18.8 us (53%)
  starting transfers between devices  11 us (31%)
  waiting for transfers between devices  5.19 us (15%)
    ppermute x5, starting transfers between devices, swapped(): return lax.ppermute(array, 'head', [(0, 1), (1, 0)])  8.17 us
    pallas_call x1, Pallas kernels, shards(): call(functools.partial(second_kernel, count, group), 'second_rows', [vmem...  3.39 us
    ppermute x1, waiting for transfers between devices, shards(): near_got = lax.ppermute(near, 'ctx', near_pairs)  2.65 us
    pallas_call x1, Pallas kernels, shards(): call(project_kernel, 'project_own', [vmem] * 6, [sum_shape, sum_shape], 2...  2.37 us
    pallas_call x1, Pallas kernels, shards(): call(first_out_kernel, 'project_first', [vmem] * 4, shape((number, column...  2.08 us
    pallas_call x3, Pallas kernels, shards(): call(functools.partial(third_kernel, count, group, part, base), 'last_til...  1.95 us
    ppermute x1, waiting for transfers between devices, shards(): next_got = lax.ppermute(onward, 'ctx', pairs(lambda r: r + 2))  1.88 us
    ppermute x1, starting transfers between devices, shards(): next_got = lax.ppermute(onward, 'ctx', pairs(lambda r: r + 2))  1.57 us
  transfers between devices with their start and end apart: 9, of which 4 were waited for; matrix products, arithmetic and copies ran while one was open for 0% of the time, Pallas kernels for 45%

profile of v6, /device:TPU:0, one launch (start us, length us, event | category | flops | bytes accessed | tf_op | source)
XLA Modules:
  0.0 35.3 jit_solution(7452946251547720674)
XLA Ops:
  0.0 1.5 %rotate_keys.1 = (bf16[256,512]{1,0:T(8,128)(2,1)S(1)}, bf16[256,512]{1,0:T(8,128)(2,1)S(1)}, bf16[512,256]{1,0:T(8,128)(2,1)S(1)}, bf16[512,256]{1,0:T(8,128)(2...) custom-call(bf16[512,256]{1,0:T(8,128)(2,1)} %k_hbm.1, ...), custom_call_target="tpu_custom_call" | custom-call | flops 4194304 | bytes 4194304 | tf_op jit(solution)/shard_map/rotate_keys/pallas_call | solution.py:402
  1.5 0.5 %collective-permute-start = (bf16[256,512]{1,0:T(8,128)(2,1)S(1)}, bf16[256,512]{1,0:T(8,128)(2,1)S(1)}, u32[]{:S(2)}, u32[]{:S(2)}) collective-permute-start(bf16[256,512]{1,0:T(8,128)(2,1)S(1)} %get-tuple-element.67), channel_id=1, source_target_pairs={{0,2},{2,8},{4,6},{6,12},{8,10},{10,16},{12,14},{14,20},{16,18},{1... | collective-permute-start | bytes 786440 | tf_op jit(solution)/shard_map/ppermute | solution.py:414
  2.0 0.2 pack_early.1.early_ref
  2.1 2.6 %collective-permute-start.1 = (bf16[256,640]{1,0:T(8,128)(2,1)S(1)}, bf16[256,640]{1,0:T(8,128)(2,1)S(1)}, u32[]{:S(2)}, u32[]{:S(2)}) collective-permute-start(bf16[256,640]{1,0:T(8,128)(2,1)S(1)} %pack_early.1.early_ref), channel_id=1, source_target_pairs={{0,1},{1,0},{2,3},{3,2},{4,5},{5,4},{6,7},{7,6},{8,9},{9,8},{10,11... | collective-permute-start | bytes 983048 | tf_op jit(solution)/shard_map/ppermute | solution.py:391
  4.7 1.1 %own_tiles.1 = (bf16[256,640]{1,0:T(8,128)(2,1)S(1)}, bf16[256,640]{1,0:T(8,128)(2,1)S(1)}, f32[256,640]{1,0:T(8,128)S(1)}, f32[256,640]{1,0:T(8,128)S(1)}, f32[256,640]{1,0:T(8,128)S(1)}) custom-call(bf16[512,1024]{1,0:T(8,128)(2,1)S(1)} %get-tuple-element.71.q_ref, bf16[512,256]{1,0:T(8,128)(2,1)S(1)} %get-tuple-element.57.k_ref, ...), custom_call_target="tpu_custom_call" | custom-call | flops 268435456 | bytes 4194304 | tf_op jit(solution)/shard_map/own_tiles/pallas_call | solution.py:420
  5.8 1.6 %collective-permute-start.2 = (bf16[256,512]{1,0:T(8,128)(2,1)S(1)}, bf16[256,512]{1,0:T(8,128)(2,1)S(1)}, u32[]{:S(2)}, u32[]{:S(2)}) collective-permute-start(bf16[256,512]{1,0:T(8,128)(2,1)S(1)} %get-tuple-element.75), channel_id=1, source_target_pairs={{0,4},{2,6},{4,8},{6,10},{8,12},{10,14},{12,16},{14,18},{16,20},{1... | collective-permute-start | bytes 786440 | tf_op jit(solution)/shard_map/ppermute | solution.py:429
  7.4 2.6 %collective-permute-done.kv_ref.near_ref = bf16[256,512]{1,0:T(8,128)(2,1)S(1)} collective-permute-done((bf16[256,512]{1,0:T(8,128)(2,1)S(1)}, bf16[256,512]{1,0:T(8,128)(2,1)S(1)}, u32[]{:S(2)}, u32[]{:S(2)}) %collective-permute-start) | collective-permute-done | bytes 262176 | tf_op jit(solution)/shard_map/ppermute | solution.py:414
  10.1 2.1 %collective-permute-start.4 = (bf16[256,640]{1,0:T(8,128)(2,1)S(1)}, bf16[256,640]{1,0:T(8,128)(2,1)S(1)}, u32[]{:S(2)}, u32[]{:S(2)}) collective-permute-start(bf16[256,640]{1,0:T(8,128)(2,1)S(1)} %first_rows.1.first_ref), channel_id=1, source_target_pairs={{0,1},{1,0},{2,3},{3,2},{4,5},{5,4},{6,7},{7,6},{8,9},{9,8},{10,11... | collective-permute-start | bytes 983048 | tf_op jit(solution)/shard_map/ppermute | solution.py:391
  12.1 3.4 %second_rows.1 = (bf16[256,1024]{1,0:T(8,128)(2,1)S(1)}, f32[256,1024]{1,0:T(8,128)S(1)}, f32[256,1024]{1,0:T(8,128)S(1)}, f32[256,1024]{1,0:T(8,128)S(1)}, bf16[2048,2048]{1,0:T(8,128)(2,1)S(1)}) custom-call(bf16[512,1024]{1,0:T(8,128)(2,1)S(1)} %get-tuple-element.71.q_ref, bf16[512,256]{1,0:T(8,128)(2,1)S(1)} %get-tuple-element.57.k_ref, ...), custom_call_target="tpu_custom_call" | custom-call | flops 1073741824 | bytes 12582912 | tf_op jit(solution)/shard_map/second_rows/pallas_call | solution.py:440
  15.5 0.0 collective-permute-done.1.early_ref
  15.6 1.9 %collective-permute-done.2.kv_ref = bf16[256,512]{1,0:T(8,128)(2,1)S(1)} collective-permute-done((bf16[256,512]{1,0:T(8,128)(2,1)S(1)}, bf16[256,512]{1,0:T(8,128)(2,1)S(1)}, u32[]{:S(2)}, u32[]{:S(2)}) %collective-permute-start.2) | collective-permute-done | bytes 262176 | tf_op jit(solution)/shard_map/ppermute | solution.py:429
  17.4 0.2 collective-permute-start.3
  17.6 0.6 %collective-permute-start.5 = (bf16[256,256]{1,0:T(8,128)(2,1)S(1)}, bf16[256,256]{1,0:T(8,128)(2,1)S(1)}, u32[]{:S(2)}, u32[]{:S(2)}) collective-permute-start(bf16[256,256]{1,0:T(8,128)(2,1)S(1)} %slice.3), channel_id=1, source_target_pairs={{0,2},{2,8},{4,6},{6,12},{8,10},{10,16},{12,14},{14,20},{16,18},{1... | collective-permute-start | bytes 393224 | tf_op jit(solution)/shard_map/ppermute | solution.py:450
  18.2 0.8 %next_tile.2 = (f32[256,512]{1,0:T(8,128)S(1)}, f32[256,512]{1,0:T(8,128)S(1)}, f32[256,512]{1,0:T(8,128)S(1)}) custom-call(bf16[256,1024]{1,0:T(8,128)(2,1)S(1)} %get-tuple-element.89.rot_ref, bf16[256,512]{1,0:T(8,128)(2,1)S(1)} %collective-permute-done.2.kv_ref, s32[1,512]{1,0:T(1,128)S(1)} %get-tuple-element.62.p_ref, ...), custom_call_target="tpu_custom_call" | custom-call | flops 536870912 | bytes 4194304 | tf_op jit(solution)/shard_map/next_tile/pallas_call | solution.py:455
  19.0 0.0 collective-permute-done.3.kv_ref
  19.0 0.8 %last_tile.3.second0_ref = bf16[256,512]{1,0:T(8,128)(2,1)S(1)} custom-call(bf16[256,1024]{1,0:T(8,128)(2,1)S(1)} %get-tuple-element.89.rot_ref, bf16[256,512]{1,0:T(8,128)(2,1)S(1)} %collective-permute-done.3.kv_ref, s32[1,512]{1,0:T(1,128)S(1)} %get-tuple-element.62.p_ref, f32[256,512]{1,0:T(8,128)S(1)} %get-tuple-element.81.acc_ref, ...), custom_call_target="tpu_custom_call" | custom-call | flops 268435456 | bytes 4194304 | tf_op jit(solution)/shard_map/last_tile/pallas_call | solution.py:465
  19.8 0.8 %collective-permute-start.8 = (bf16[256,512]{1,0:T(8,128)(2,1)S(1)}, bf16[256,512]{1,0:T(8,128)(2,1)S(1)}, u32[]{:S(2)}, u32[]{:S(2)}) collective-permute-start(bf16[256,512]{1,0:T(8,128)(2,1)S(1)} %last_tile.3.second0_ref), channel_id=1, source_target_pairs={{0,1},{1,0},{2,3},{3,2},{4,5},{5,4},{6,7},{7,6},{8,9},{9,8},{10,11... | collective-permute-start | bytes 786440 | tf_op jit(solution)/shard_map/ppermute | solution.py:391
  20.6 0.0 collective-permute-done.4.got_ref
  20.6 0.8 %next_tile.3 = (f32[256,512]{1,0:T(8,128)S(1)}, f32[256,512]{1,0:T(8,128)S(1)}, f32[256,512]{1,0:T(8,128)S(1)}) custom-call(bf16[256,1024]{1,0:T(8,128)(2,1)S(1)} %get-tuple-element.89.rot_ref, bf16[256,512]{1,0:T(8,128)(2,1)S(1)} %collective-permute-done.2.kv_ref, s32[1,512]{1,0:T(1,128)S(1)} %get-tuple-element.62.p_ref, ...), custom_call_target="tpu_custom_call" | custom-call | flops 536870912 | bytes 4194304 | tf_op jit(solution)/shard_map/next_tile/pallas_call | solution.py:455
  21.4 0.7 %last_tile.4.second1_ref = bf16[256,384]{1,0:T(8,128)(2,1)S(1)} custom-call(bf16[256,1024]{1,0:T(8,128)(2,1)S(1)} %get-tuple-element.89.rot_ref, bf16[256,512]{1,0:T(8,128)(2,1)S(1)} %collective-permute-done.3.kv_ref, s32[1,512]{1,0:T(1,128)S(1)} %get-tuple-element.62.p_ref, f32[256,512]{1,0:T(8,128)S(1)} %get-tuple-element.85.acc_ref, ...), custom_call_target="tpu_custom_call" | custom-call | flops 268435456 | bytes 4194304 | tf_op jit(solution)/shard_map/last_tile/pallas_call | solution.py:465
  22.1 1.8 %collective-permute-start.7 = (bf16[256,384]{1,0:T(8,128)(2,1)S(1)}, bf16[256,384]{1,0:T(8,128)(2,1)S(1)}, u32[]{:S(2)}, u32[]{:S(2)}) collective-permute-start(bf16[256,384]{1,0:T(8,128)(2,1)S(1)} %last_tile.4.second1_ref), channel_id=1, source_target_pairs={{0,1},{1,0},{2,3},{3,2},{4,5},{5,4},{6,7},{7,6},{8,9},{9,8},{10,11... | collective-permute-start | bytes 589832 | tf_op jit(solution)/shard_map/ppermute | solution.py:391
  23.9 0.2 collective-permute-done.5.near_ref
  24.0 0.5 %last_tile.5.second2_ref = bf16[256,128]{1,0:T(8,128)(2,1)S(1)} custom-call(bf16[256,1024]{1,0:T(8,128)(2,1)S(1)} %get-tuple-element.89.rot_ref, bf16[256,512]{1,0:T(8,128)(2,1)S(1)} %collective-permute-done.3.kv_ref, s32[1,512]{1,0:T(1,128)S(1)} %get-tuple-element.62.p_ref, f32[256,512]{1,0:T(8,128)S(1)} %get-tuple-element.85.acc_ref, ...), custom_call_target="tpu_custom_call" | custom-call | flops 268435456 | bytes 4194304 | tf_op jit(solution)/shard_map/last_tile/pallas_call | solution.py:465
  24.5 0.9 %collective-permute-start.6 = (bf16[256,128]{1,0:T(8,128)(2,1)S(1)}, bf16[256,128]{1,0:T(8,128)(2,1)S(1)}, u32[]{:S(2)}, u32[]{:S(2)}) collective-permute-start(bf16[256,128]{1,0:T(8,128)(2,1)S(1)} %last_tile.5.second2_ref), channel_id=1, source_target_pairs={{0,1},{1,0},{2,3},{3,2},{4,5},{5,4},{6,7},{7,6},{8,9},{9,8},{10,11... | collective-permute-start | bytes 196616 | tf_op jit(solution)/shard_map/ppermute | solution.py:391
  25.5 1.0 %early_rows.2.last_ref = bf16[256,384]{1,0:T(8,128)(2,1)S(1)} custom-call(bf16[256,640]{1,0:T(8,128)(2,1)S(1)} %pack_early.1.early_ref, bf16[256,512]{1,0:T(8,128)(2,1)S(1)} %collective-permute-done.kv_ref.near_ref, s32[1,512]{1,0:T(1,128)S(1)} %get-tuple-element.62.p_ref), custom_call_target="tpu_custom_call" | custom-call | flops 268435456 | bytes 4194304 | tf_op jit(solution)/shard_map/early_rows/pallas_call | solution.py:482
  26.4 2.4 %project_own.1 = (f32[256,2048]{1,0:T(8,128)S(1)}, f32[256,2048]{1,0:T(8,128)S(1)}) custom-call(bf16[256,640]{1,0:T(8,128)(2,1)S(1)} %first_rows.1.first_ref, bf16[256,384]{1,0:T(8,128)(2,1)S(1)} %early_rows.2.last_ref, bf16[256,512]{1,0:T(8,128)(2,1)S(1)} %last_tile.3.second0_ref, bf16[256,384]{1,0:T(8,128)(2,1)S(1)} %last_tile.4.second1_ref, ...), custom_call_target="tpu_custom_call" | custom-call | flops 2147483648 | bytes 8388608 | tf_op jit(solution)/shard_map/project_own/pallas_call | solution.py:484
  28.8 1.0 %early_rows.3.got_last_ref = bf16[256,384]{1,0:T(8,128)(2,1)S(1)} custom-call(bf16[256,640]{1,0:T(8,128)(2,1)S(1)} %collective-permute-done.1.early_ref, bf16[256,256]{1,0:T(8,128)(2,1)S(1)} %collective-permute-done.5.near_ref, s32[1,512]{1,0:T(1,128)S(1)} %get-tuple-element.62.p_ref), custom_call_target="tpu_custom_call" | custom-call | flops 268435456 | bytes 4194304 | tf_op jit(solution)/shard_map/early_rows/pallas_call | solution.py:488
  29.8 2.1 %project_first.1.begun_hbm = bf16[512,2048]{1,0:T(8,128)(2,1)} custom-call(bf16[256,640]{1,0:T(8,128)(2,1)S(1)} %collective-permute-done.4.got_ref, bf16[256,384]{1,0:T(8,128)(2,1)S(1)} %early_rows.3.got_last_ref, f32[256,2048]{1,0:T(8,128)S(1)} %get-tuple-element.103.sum_ref, bf16[2048,2048]{1,0:T(8,128)(2,1)S(1)} %get-tuple-element.98.w_ref), custom_call_target="tpu_custom_call" | custom-call | flops 1073741824 | bytes 8388608 | tf_op jit(solution)/shard_map/project_first/pallas_call | solution.py:489
  31.9 0.7 %project_second.2.part_ref = f32[256,2048]{1,0:T(8,128)S(1)} custom-call(bf16[256,512]{1,0:T(8,128)(2,1)S(1)} %collective-permute-done.8.got_ref, f32[256,2048]{1,0:T(8,128)S(1)} %get-tuple-element.105.part_ref, bf16[2048,2048]{1,0:T(8,128)(2,1)S(1)} %get-tuple-element.98.w_ref), custom_call_target="tpu_custom_call" | custom-call | flops 536870912 | bytes 4194304 | tf_op jit(solution)/shard_map/project_second/pallas_call | solution.py:501
  32.6 0.5 %collective-permute-done.7.got_ref = bf16[256,384]{1,0:T(8,128)(2,1)S(1)} collective-permute-done((bf16[256,384]{1,0:T(8,128)(2,1)S(1)}, bf16[256,384]{1,0:T(8,128)(2,1)S(1)}, u32[]{:S(2)}, u32[]{:S(2)}) %collective-permute-start.7) | collective-permute-done | bytes 196640 | tf_op jit(solution)/shard_map/ppermute | solution.py:391
  33.1 0.7 %project_second.3.part_ref = f32[256,2048]{1,0:T(8,128)S(1)} custom-call(bf16[256,384]{1,0:T(8,128)(2,1)S(1)} %collective-permute-done.7.got_ref, f32[256,2048]{1,0:T(8,128)S(1)} %project_second.2.part_ref, bf16[2048,2048]{1,0:T(8,128)(2,1)S(1)} %get-tuple-element.98.w_ref), custom_call_target="tpu_custom_call" | custom-call | flops 536870912 | bytes 4194304 | tf_op jit(solution)/shard_map/project_second/pallas_call | solution.py:501
  33.8 1.3 %project_last.1 = bf16[512,2048]{1,0:T(8,128)(2,1)} custom-call(bf16[256,128]{1,0:T(8,128)(2,1)S(1)} %collective-permute-done.6.got_ref, f32[256,2048]{1,0:T(8,128)S(1)} %project_second.3.part_ref, bf16[2048,2048]{1,0:T(8,128)(2,1)S(1)} %get-tuple-element.98.w_ref, bf16[512,2048]{1,0:T(8,128)(2,1)} %project_first.1.begun_hbm), custom_call_target="tpu_custom_call", output_to_operand_aliasing={{}: (3, {})} | custom-call | flops 536870912 | bytes 4194304 | tf_op jit(solution)/shard_map/project_last/pallas_call | solution.py:509
  (4 shorter events, 0.0 us)
Async XLA Ops:
  1.5 8.6 %collective-permute-start = (bf16[256,512]{1,0:T(8,128)(2,1)S(1)}, bf16[256,512]{1,0:T(8,128)(2,1)S(1)}, u32[]{:S(2)}, u32[]{:S(2)}) collective-permute-start(bf16[256,512]{1,0:T(8,128)(2,1)S(1)} %get-tuple-element.67), channel_id=1, source_target_pairs={{0,2},{2,8},{4,6},{6,12},{8,10},{10,16},{12,14},{14,20},{16,18},{1... | collective-permute-start | bytes 786440 | tf_op jit(solution)/shard_map/ppermute | solution.py:414
  2.1 13.4 %collective-permute-start.1 = (bf16[256,640]{1,0:T(8,128)(2,1)S(1)}, bf16[256,640]{1,0:T(8,128)(2,1)S(1)}, u32[]{:S(2)}, u32[]{:S(2)}) collective-permute-start(bf16[256,640]{1,0:T(8,128)(2,1)S(1)} %pack_early.1.early_ref), channel_id=1, source_target_pairs={{0,1},{1,0},{2,3},{3,2},{4,5},{5,4},{6,7},{7,6},{8,9},{9,8},{10,11... | collective-permute-start | bytes 983048 | tf_op jit(solution)/shard_map/ppermute | solution.py:391
  5.8 11.6 %collective-permute-start.2 = (bf16[256,512]{1,0:T(8,128)(2,1)S(1)}, bf16[256,512]{1,0:T(8,128)(2,1)S(1)}, u32[]{:S(2)}, u32[]{:S(2)}) collective-permute-start(bf16[256,512]{1,0:T(8,128)(2,1)S(1)} %get-tuple-element.75), channel_id=1, source_target_pairs={{0,4},{2,6},{4,8},{6,10},{8,12},{10,14},{12,16},{14,18},{16,20},{1... | collective-permute-start | bytes 786440 | tf_op jit(solution)/shard_map/ppermute | solution.py:429
  10.1 10.5 %collective-permute-start.4 = (bf16[256,640]{1,0:T(8,128)(2,1)S(1)}, bf16[256,640]{1,0:T(8,128)(2,1)S(1)}, u32[]{:S(2)}, u32[]{:S(2)}) collective-permute-start(bf16[256,640]{1,0:T(8,128)(2,1)S(1)} %first_rows.1.first_ref), channel_id=1, source_target_pairs={{0,1},{1,0},{2,3},{3,2},{4,5},{5,4},{6,7},{7,6},{8,9},{9,8},{10,11... | collective-permute-start | bytes 983048 | tf_op jit(solution)/shard_map/ppermute | solution.py:391
  17.4 1.5 %collective-permute-start.3 = (bf16[256,512]{1,0:T(8,128)(2,1)S(1)}, bf16[256,512]{1,0:T(8,128)(2,1)S(1)}, u32[]{:S(2)}, u32[]{:S(2)}) collective-permute-start(bf16[256,512]{1,0:T(8,128)(2,1)S(1)} %collective-permute-done.2.kv_ref), channel_id=1, source_target_pairs={{0,2},{2,0},{4,6},{6,4},{8,10},{10,8},{12,14},{14,12},{16,18},{18,... | collective-permute-start | bytes 786440 | tf_op jit(solution)/shard_map/ppermute | solution.py:452
  17.6 6.4 %collective-permute-start.5 = (bf16[256,256]{1,0:T(8,128)(2,1)S(1)}, bf16[256,256]{1,0:T(8,128)(2,1)S(1)}, u32[]{:S(2)}, u32[]{:S(2)}) collective-permute-start(bf16[256,256]{1,0:T(8,128)(2,1)S(1)} %slice.3), channel_id=1, source_target_pairs={{0,2},{2,8},{4,6},{6,12},{8,10},{10,16},{12,14},{14,20},{16,18},{1... | collective-permute-start | bytes 393224 | tf_op jit(solution)/shard_map/ppermute | solution.py:450
  19.8 12.1 %collective-permute-start.8 = (bf16[256,512]{1,0:T(8,128)(2,1)S(1)}, bf16[256,512]{1,0:T(8,128)(2,1)S(1)}, u32[]{:S(2)}, u32[]{:S(2)}) collective-permute-start(bf16[256,512]{1,0:T(8,128)(2,1)S(1)} %last_tile.3.second0_ref), channel_id=1, source_target_pairs={{0,1},{1,0},{2,3},{3,2},{4,5},{5,4},{6,7},{7,6},{8,9},{9,8},{10,11... | collective-permute-start | bytes 786440 | tf_op jit(solution)/shard_map/ppermute | solution.py:391
  22.1 11.0 %collective-permute-start.7 = (bf16[256,384]{1,0:T(8,128)(2,1)S(1)}, bf16[256,384]{1,0:T(8,128)(2,1)S(1)}, u32[]{:S(2)}, u32[]{:S(2)}) collective-permute-start(bf16[256,384]{1,0:T(8,128)(2,1)S(1)} %last_tile.4.second1_ref), channel_id=1, source_target_pairs={{0,1},{1,0},{2,3},{3,2},{4,5},{5,4},{6,7},{7,6},{8,9},{9,8},{10,11... | collective-permute-start | bytes 589832 | tf_op jit(solution)/shard_map/ppermute | solution.py:391
  24.5 9.3 %collective-permute-start.6 = (bf16[256,128]{1,0:T(8,128)(2,1)S(1)}, bf16[256,128]{1,0:T(8,128)(2,1)S(1)}, u32[]{:S(2)}, u32[]{:S(2)}) collective-permute-start(bf16[256,128]{1,0:T(8,128)(2,1)S(1)} %last_tile.5.second2_ref), channel_id=1, source_target_pairs={{0,1},{1,0},{2,3},{3,2},{4,5},{5,4},{6,7},{7,6},{8,9},{9,8},{10,11... | collective-permute-start | bytes 196616 | tf_op jit(solution)/shard_map/ppermute | solution.py:391

commit v7 on v6

--- a/solution.py
+++ b/solution.py
@@ -456,12 +456,13 @@
             functools.partial(next_kernel, count, group, part), "next_tile", [vmem] * 6, [held] * 3, 512 * MIB, 4 * MIB
         )(rot, next_got, p, *state_now)
 
-    parts = range(heads // 2), range(heads // 2, heads - 1), range(heads - 1, heads)
+    begin = heads // 2 - 1
+    parts = range(begin), range(begin, heads - 1), range(heads - 1, heads)
     seconds, seconds_got = [], []
     for part in parts:
         if len(seconds) < 2:
             base = part[0]
-            held_state = with_next_tile(range(base, base + heads // 2), rot)
+            held_state = with_next_tile(range(base, begin if base == 0 else heads), rot)
         second = call(
             functools.partial(third_kernel, count, group, part, base),
             "last_tile",

time: 35.4 us -> 35.3 us (level)
  transfers between devices with their start and end apart: 9 -> 9, of which waited for: 4 -> 4; matrix products, arithmetic and copies ran while one was open for 0% -> 0% of each run, Pallas kernels for 45% -> 46%
where the time goes in v7:
time: 35.3 us; the launch traced here: 35.1 us
  Pallas kernels  18.8 us (53%)
  starting transfers between devices  11 us (31%)
  waiting for transfers between devices  5.03 us (14%)
    ppermute x5, starting transfers between devices, swapped(): return lax.ppermute(array, 'head', [(0, 1), (1, 0)])  8.22 us
    pallas_call x1, Pallas kernels, shards(): call(functools.partial(second_kernel, count, group), 'second_rows', [vmem...  3.39 us
    ppermute x1, waiting for transfers between devices, shards(): near_got = lax.ppermute(near, 'ctx', near_pairs)  2.65 us
    pallas_call x1, Pallas kernels, shards(): call(project_kernel, 'project_own', [vmem] * 6, [sum_shape, sum_shape], 2...  2.37 us
    pallas_call x1, Pallas kernels, shards(): call(first_out_kernel, 'project_first', [vmem] * 4, shape((number, column...  2.08 us
    pallas_call x3, Pallas kernels, shards(): call(functools.partial(third_kernel, count, group, part, base), 'last_til...  1.95 us
    ppermute x1, waiting for transfers between devices, shards(): next_got = lax.ppermute(onward, 'ctx', pairs(lambda r: r + 2))  1.88 us
    ppermute x1, starting transfers between devices, shards(): next_got = lax.ppermute(onward, 'ctx', pairs(lambda r: r + 2))  1.57 us
  transfers between devices with their start and end apart: 9, of which 4 were waited for; matrix products, arithmetic and copies ran while one was open for 0% of the time, Pallas kernels for 46%

profile of v7, /device:TPU:0, one launch (start us, length us, event | category | flops | bytes accessed | tf_op | source)
XLA Modules:
  0.0 35.1 jit_solution(11817075391284934421)
XLA Ops:
  0.0 1.5 %rotate_keys.1 = (bf16[256,512]{1,0:T(8,128)(2,1)S(1)}, bf16[256,512]{1,0:T(8,128)(2,1)S(1)}, bf16[512,256]{1,0:T(8,128)(2,1)S(1)}, bf16[512,256]{1,0:T(8,128)(2...) custom-call(bf16[512,256]{1,0:T(8,128)(2,1)} %k_hbm.1, ...), custom_call_target="tpu_custom_call" | custom-call | flops 4194304 | bytes 4194304 | tf_op jit(solution)/shard_map/rotate_keys/pallas_call | solution.py:402
  1.5 0.5 %collective-permute-start = (bf16[256,512]{1,0:T(8,128)(2,1)S(1)}, bf16[256,512]{1,0:T(8,128)(2,1)S(1)}, u32[]{:S(2)}, u32[]{:S(2)}) collective-permute-start(bf16[256,512]{1,0:T(8,128)(2,1)S(1)} %get-tuple-element.67), channel_id=1, source_target_pairs={{0,2},{2,8},{4,6},{6,12},{8,10},{10,16},{12,14},{14,20},{16,18},{1... | collective-permute-start | bytes 786440 | tf_op jit(solution)/shard_map/ppermute | solution.py:414
  2.0 0.2 pack_early.1.early_ref
  2.1 2.6 %collective-permute-start.1 = (bf16[256,640]{1,0:T(8,128)(2,1)S(1)}, bf16[256,640]{1,0:T(8,128)(2,1)S(1)}, u32[]{:S(2)}, u32[]{:S(2)}) collective-permute-start(bf16[256,640]{1,0:T(8,128)(2,1)S(1)} %pack_early.1.early_ref), channel_id=1, source_target_pairs={{0,1},{1,0},{2,3},{3,2},{4,5},{5,4},{6,7},{7,6},{8,9},{9,8},{10,11... | collective-permute-start | bytes 983048 | tf_op jit(solution)/shard_map/ppermute | solution.py:391
  4.7 1.1 %own_tiles.1 = (bf16[256,640]{1,0:T(8,128)(2,1)S(1)}, bf16[256,640]{1,0:T(8,128)(2,1)S(1)}, f32[256,640]{1,0:T(8,128)S(1)}, f32[256,640]{1,0:T(8,128)S(1)}, f32[256,640]{1,0:T(8,128)S(1)}) custom-call(bf16[512,1024]{1,0:T(8,128)(2,1)S(1)} %get-tuple-element.71.q_ref, bf16[512,256]{1,0:T(8,128)(2,1)S(1)} %get-tuple-element.57.k_ref, ...), custom_call_target="tpu_custom_call" | custom-call | flops 268435456 | bytes 4194304 | tf_op jit(solution)/shard_map/own_tiles/pallas_call | solution.py:420
  5.8 1.6 %collective-permute-start.2 = (bf16[256,512]{1,0:T(8,128)(2,1)S(1)}, bf16[256,512]{1,0:T(8,128)(2,1)S(1)}, u32[]{:S(2)}, u32[]{:S(2)}) collective-permute-start(bf16[256,512]{1,0:T(8,128)(2,1)S(1)} %get-tuple-element.75), channel_id=1, source_target_pairs={{0,4},{2,6},{4,8},{6,10},{8,12},{10,14},{12,16},{14,18},{16,20},{1... | collective-permute-start | bytes 786440 | tf_op jit(solution)/shard_map/ppermute | solution.py:429
  7.4 2.6 %collective-permute-done.kv_ref.near_ref = bf16[256,512]{1,0:T(8,128)(2,1)S(1)} collective-permute-done((bf16[256,512]{1,0:T(8,128)(2,1)S(1)}, bf16[256,512]{1,0:T(8,128)(2,1)S(1)}, u32[]{:S(2)}, u32[]{:S(2)}) %collective-permute-start) | collective-permute-done | bytes 262176 | tf_op jit(solution)/shard_map/ppermute | solution.py:414
  10.1 2.1 %collective-permute-start.4 = (bf16[256,640]{1,0:T(8,128)(2,1)S(1)}, bf16[256,640]{1,0:T(8,128)(2,1)S(1)}, u32[]{:S(2)}, u32[]{:S(2)}) collective-permute-start(bf16[256,640]{1,0:T(8,128)(2,1)S(1)} %first_rows.1.first_ref), channel_id=1, source_target_pairs={{0,1},{1,0},{2,3},{3,2},{4,5},{5,4},{6,7},{7,6},{8,9},{9,8},{10,11... | collective-permute-start | bytes 983048 | tf_op jit(solution)/shard_map/ppermute | solution.py:391
  12.1 3.4 %second_rows.1 = (bf16[256,1024]{1,0:T(8,128)(2,1)S(1)}, f32[256,1024]{1,0:T(8,128)S(1)}, f32[256,1024]{1,0:T(8,128)S(1)}, f32[256,1024]{1,0:T(8,128)S(1)}, bf16[2048,2048]{1,0:T(8,128)(2,1)S(1)}) custom-call(bf16[512,1024]{1,0:T(8,128)(2,1)S(1)} %get-tuple-element.71.q_ref, bf16[512,256]{1,0:T(8,128)(2,1)S(1)} %get-tuple-element.57.k_ref, ...), custom_call_target="tpu_custom_call" | custom-call | flops 1073741824 | bytes 12582912 | tf_op jit(solution)/shard_map/second_rows/pallas_call | solution.py:440
  15.5 0.0 collective-permute-done.1.early_ref
  15.6 1.9 %collective-permute-done.2.kv_ref = bf16[256,512]{1,0:T(8,128)(2,1)S(1)} collective-permute-done((bf16[256,512]{1,0:T(8,128)(2,1)S(1)}, bf16[256,512]{1,0:T(8,128)(2,1)S(1)}, u32[]{:S(2)}, u32[]{:S(2)}) %collective-permute-start.2) | collective-permute-done | bytes 262176 | tf_op jit(solution)/shard_map/ppermute | solution.py:429
  17.4 0.2 collective-permute-start.3
  17.6 0.6 %collective-permute-start.5 = (bf16[256,256]{1,0:T(8,128)(2,1)S(1)}, bf16[256,256]{1,0:T(8,128)(2,1)S(1)}, u32[]{:S(2)}, u32[]{:S(2)}) collective-permute-start(bf16[256,256]{1,0:T(8,128)(2,1)S(1)} %slice.3), channel_id=1, source_target_pairs={{0,2},{2,8},{4,6},{6,12},{8,10},{10,16},{12,14},{14,20},{16,18},{1... | collective-permute-start | bytes 393224 | tf_op jit(solution)/shard_map/ppermute | solution.py:450
  18.2 0.7 %next_tile.2 = (f32[256,384]{1,0:T(8,128)S(1)}, f32[256,384]{1,0:T(8,128)S(1)}, f32[256,384]{1,0:T(8,128)S(1)}) custom-call(bf16[256,1024]{1,0:T(8,128)(2,1)S(1)} %get-tuple-element.89.rot_ref, bf16[256,512]{1,0:T(8,128)(2,1)S(1)} %collective-permute-done.2.kv_ref, s32[1,512]{1,0:T(1,128)S(1)} %get-tuple-element.62.p_ref, ...), custom_call_target="tpu_custom_call" | custom-call | flops 536870912 | bytes 4194304 | tf_op jit(solution)/shard_map/next_tile/pallas_call | solution.py:455
  18.9 0.1 collective-permute-done.3.kv_ref
  19.0 0.7 %last_tile.3.second0_ref = bf16[256,384]{1,0:T(8,128)(2,1)S(1)} custom-call(bf16[256,1024]{1,0:T(8,128)(2,1)S(1)} %get-tuple-element.89.rot_ref, bf16[256,512]{1,0:T(8,128)(2,1)S(1)} %collective-permute-done.3.kv_ref, s32[1,512]{1,0:T(1,128)S(1)} %get-tuple-element.62.p_ref, f32[256,384]{1,0:T(8,128)S(1)} %get-tuple-element.81.acc_ref, ...), custom_call_target="tpu_custom_call" | custom-call | flops 268435456 | bytes 4194304 | tf_op jit(solution)/shard_map/last_tile/pallas_call | solution.py:466
  19.6 0.8 %collective-permute-start.8 = (bf16[256,384]{1,0:T(8,128)(2,1)S(1)}, bf16[256,384]{1,0:T(8,128)(2,1)S(1)}, u32[]{:S(2)}, u32[]{:S(2)}) collective-permute-start(bf16[256,384]{1,0:T(8,128)(2,1)S(1)} %last_tile.3.second0_ref), channel_id=1, source_target_pairs={{0,1},{1,0},{2,3},{3,2},{4,5},{5,4},{6,7},{7,6},{8,9},{9,8},{10,11... | collective-permute-start | bytes 589832 | tf_op jit(solution)/shard_map/ppermute | solution.py:391
  20.5 0.9 %next_tile.3 = (f32[256,640]{1,0:T(8,128)S(1)}, f32[256,640]{1,0:T(8,128)S(1)}, f32[256,640]{1,0:T(8,128)S(1)}) custom-call(bf16[256,1024]{1,0:T(8,128)(2,1)S(1)} %get-tuple-element.89.rot_ref, bf16[256,512]{1,0:T(8,128)(2,1)S(1)} %collective-permute-done.2.kv_ref, s32[1,512]{1,0:T(1,128)S(1)} %get-tuple-element.62.p_ref, ...), custom_call_target="tpu_custom_call" | custom-call | flops 536870912 | bytes 4194304 | tf_op jit(solution)/shard_map/next_tile/pallas_call | solution.py:455
  21.4 0.8 %last_tile.4.second1_ref = bf16[256,512]{1,0:T(8,128)(2,1)S(1)} custom-call(bf16[256,1024]{1,0:T(8,128)(2,1)S(1)} %get-tuple-element.89.rot_ref, bf16[256,512]{1,0:T(8,128)(2,1)S(1)} %collective-permute-done.3.kv_ref, s32[1,512]{1,0:T(1,128)S(1)} %get-tuple-element.62.p_ref, f32[256,640]{1,0:T(8,128)S(1)} %get-tuple-element.85.acc_ref, ...), custom_call_target="tpu_custom_call" | custom-call | flops 268435456 | bytes 4194304 | tf_op jit(solution)/shard_map/last_tile/pallas_call | solution.py:466
  22.2 1.9 %collective-permute-start.7 = (bf16[256,512]{1,0:T(8,128)(2,1)S(1)}, bf16[256,512]{1,0:T(8,128)(2,1)S(1)}, u32[]{:S(2)}, u32[]{:S(2)}) collective-permute-start(bf16[256,512]{1,0:T(8,128)(2,1)S(1)} %last_tile.4.second1_ref), channel_id=1, source_target_pairs={{0,1},{1,0},{2,3},{3,2},{4,5},{5,4},{6,7},{7,6},{8,9},{9,8},{10,11... | collective-permute-start | bytes 786440 | tf_op jit(solution)/shard_map/ppermute | solution.py:391
  24.1 0.0 collective-permute-done.5.near_ref
  24.1 0.5 %last_tile.5.second2_ref = bf16[256,128]{1,0:T(8,128)(2,1)S(1)} custom-call(bf16[256,1024]{1,0:T(8,128)(2,1)S(1)} %get-tuple-element.89.rot_ref, bf16[256,512]{1,0:T(8,128)(2,1)S(1)} %collective-permute-done.3.kv_ref, s32[1,512]{1,0:T(1,128)S(1)} %get-tuple-element.62.p_ref, f32[256,640]{1,0:T(8,128)S(1)} %get-tuple-element.85.acc_ref, ...), custom_call_target="tpu_custom_call" | custom-call | flops 268435456 | bytes 4194304 | tf_op jit(solution)/shard_map/last_tile/pallas_call | solution.py:466
  24.6 0.8 %collective-permute-start.6 = (bf16[256,128]{1,0:T(8,128)(2,1)S(1)}, bf16[256,128]{1,0:T(8,128)(2,1)S(1)}, u32[]{:S(2)}, u32[]{:S(2)}) collective-permute-start(bf16[256,128]{1,0:T(8,128)(2,1)S(1)} %last_tile.5.second2_ref), channel_id=1, source_target_pairs={{0,1},{1,0},{2,3},{3,2},{4,5},{5,4},{6,7},{7,6},{8,9},{9,8},{10,11... | collective-permute-start | bytes 196616 | tf_op jit(solution)/shard_map/ppermute | solution.py:391
  25.5 1.0 %early_rows.2.last_ref = bf16[256,384]{1,0:T(8,128)(2,1)S(1)} custom-call(bf16[256,640]{1,0:T(8,128)(2,1)S(1)} %pack_early.1.early_ref, bf16[256,512]{1,0:T(8,128)(2,1)S(1)} %collective-permute-done.kv_ref.near_ref, s32[1,512]{1,0:T(1,128)S(1)} %get-tuple-element.62.p_ref), custom_call_target="tpu_custom_call" | custom-call | flops 268435456 | bytes 4194304 | tf_op jit(solution)/shard_map/early_rows/pallas_call | solution.py:483
  26.4 2.4 %project_own.1 = (f32[256,2048]{1,0:T(8,128)S(1)}, f32[256,2048]{1,0:T(8,128)S(1)}) custom-call(bf16[256,640]{1,0:T(8,128)(2,1)S(1)} %first_rows.1.first_ref, bf16[256,384]{1,0:T(8,128)(2,1)S(1)} %early_rows.2.last_ref, bf16[256,384]{1,0:T(8,128)(2,1)S(1)} %last_tile.3.second0_ref, bf16[256,512]{1,0:T(8,128)(2,1)S(1)} %last_tile.4.second1_ref, ...), custom_call_target="tpu_custom_call" | custom-call | flops 2147483648 | bytes 8388608 | tf_op jit(solution)/shard_map/project_own/pallas_call | solution.py:485
  28.8 1.0 %early_rows.3.got_last_ref = bf16[256,384]{1,0:T(8,128)(2,1)S(1)} custom-call(bf16[256,640]{1,0:T(8,128)(2,1)S(1)} %collective-permute-done.1.early_ref, bf16[256,256]{1,0:T(8,128)(2,1)S(1)} %collective-permute-done.5.near_ref, s32[1,512]{1,0:T(1,128)S(1)} %get-tuple-element.62.p_ref), custom_call_target="tpu_custom_call" | custom-call | flops 268435456 | bytes 4194304 | tf_op jit(solution)/shard_map/early_rows/pallas_call | solution.py:489
  29.8 2.1 %project_first.1.begun_hbm = bf16[512,2048]{1,0:T(8,128)(2,1)} custom-call(bf16[256,640]{1,0:T(8,128)(2,1)S(1)} %collective-permute-done.4.got_ref, bf16[256,384]{1,0:T(8,128)(2,1)S(1)} %early_rows.3.got_last_ref, f32[256,2048]{1,0:T(8,128)S(1)} %get-tuple-element.103.sum_ref, bf16[2048,2048]{1,0:T(8,128)(2,1)S(1)} %get-tuple-element.98.w_ref), custom_call_target="tpu_custom_call" | custom-call | flops 1073741824 | bytes 8388608 | tf_op jit(solution)/shard_map/project_first/pallas_call | solution.py:490
  31.9 0.7 %project_second.2.part_ref = f32[256,2048]{1,0:T(8,128)S(1)} custom-call(bf16[256,384]{1,0:T(8,128)(2,1)S(1)} %collective-permute-done.8.got_ref, f32[256,2048]{1,0:T(8,128)S(1)} %get-tuple-element.105.part_ref, bf16[2048,2048]{1,0:T(8,128)(2,1)S(1)} %get-tuple-element.98.w_ref), custom_call_target="tpu_custom_call" | custom-call | flops 536870912 | bytes 4194304 | tf_op jit(solution)/shard_map/project_second/pallas_call | solution.py:502
  32.6 0.4 %collective-permute-done.7.got_ref = bf16[256,512]{1,0:T(8,128)(2,1)S(1)} collective-permute-done((bf16[256,512]{1,0:T(8,128)(2,1)S(1)}, bf16[256,512]{1,0:T(8,128)(2,1)S(1)}, u32[]{:S(2)}, u32[]{:S(2)}) %collective-permute-start.7) | collective-permute-done | bytes 262176 | tf_op jit(solution)/shard_map/ppermute | solution.py:391
  33.0 0.7 %project_second.3.part_ref = f32[256,2048]{1,0:T(8,128)S(1)} custom-call(bf16[256,512]{1,0:T(8,128)(2,1)S(1)} %collective-permute-done.7.got_ref, f32[256,2048]{1,0:T(8,128)S(1)} %project_second.2.part_ref, bf16[2048,2048]{1,0:T(8,128)(2,1)S(1)} %get-tuple-element.98.w_ref), custom_call_target="tpu_custom_call" | custom-call | flops 536870912 | bytes 4194304 | tf_op jit(solution)/shard_map/project_second/pallas_call | solution.py:502
  33.7 0.0 collective-permute-done.6.got_ref
  33.7 1.3 %project_last.1 = bf16[512,2048]{1,0:T(8,128)(2,1)} custom-call(bf16[256,128]{1,0:T(8,128)(2,1)S(1)} %collective-permute-done.6.got_ref, f32[256,2048]{1,0:T(8,128)S(1)} %project_second.3.part_ref, bf16[2048,2048]{1,0:T(8,128)(2,1)S(1)} %get-tuple-element.98.w_ref, bf16[512,2048]{1,0:T(8,128)(2,1)} %project_first.1.begun_hbm), custom_call_target="tpu_custom_call", output_to_operand_aliasing={{}: (3, {})} | custom-call | flops 536870912 | bytes 4194304 | tf_op jit(solution)/shard_map/project_last/pallas_call | solution.py:510
  (4 shorter events, 0.0 us)
Async XLA Ops:
  1.5 8.6 %collective-permute-start = (bf16[256,512]{1,0:T(8,128)(2,1)S(1)}, bf16[256,512]{1,0:T(8,128)(2,1)S(1)}, u32[]{:S(2)}, u32[]{:S(2)}) collective-permute-start(bf16[256,512]{1,0:T(8,128)(2,1)S(1)} %get-tuple-element.67), channel_id=1, source_target_pairs={{0,2},{2,8},{4,6},{6,12},{8,10},{10,16},{12,14},{14,20},{16,18},{1... | collective-permute-start | bytes 786440 | tf_op jit(solution)/shard_map/ppermute | solution.py:414
  2.1 13.4 %collective-permute-start.1 = (bf16[256,640]{1,0:T(8,128)(2,1)S(1)}, bf16[256,640]{1,0:T(8,128)(2,1)S(1)}, u32[]{:S(2)}, u32[]{:S(2)}) collective-permute-start(bf16[256,640]{1,0:T(8,128)(2,1)S(1)} %pack_early.1.early_ref), channel_id=1, source_target_pairs={{0,1},{1,0},{2,3},{3,2},{4,5},{5,4},{6,7},{7,6},{8,9},{9,8},{10,11... | collective-permute-start | bytes 983048 | tf_op jit(solution)/shard_map/ppermute | solution.py:391
  5.8 11.6 %collective-permute-start.2 = (bf16[256,512]{1,0:T(8,128)(2,1)S(1)}, bf16[256,512]{1,0:T(8,128)(2,1)S(1)}, u32[]{:S(2)}, u32[]{:S(2)}) collective-permute-start(bf16[256,512]{1,0:T(8,128)(2,1)S(1)} %get-tuple-element.75), channel_id=1, source_target_pairs={{0,4},{2,6},{4,8},{6,10},{8,12},{10,14},{12,16},{14,18},{16,20},{1... | collective-permute-start | bytes 786440 | tf_op jit(solution)/shard_map/ppermute | solution.py:429
  10.1 10.4 %collective-permute-start.4 = (bf16[256,640]{1,0:T(8,128)(2,1)S(1)}, bf16[256,640]{1,0:T(8,128)(2,1)S(1)}, u32[]{:S(2)}, u32[]{:S(2)}) collective-permute-start(bf16[256,640]{1,0:T(8,128)(2,1)S(1)} %first_rows.1.first_ref), channel_id=1, source_target_pairs={{0,1},{1,0},{2,3},{3,2},{4,5},{5,4},{6,7},{7,6},{8,9},{9,8},{10,11... | collective-permute-start | bytes 983048 | tf_op jit(solution)/shard_map/ppermute | solution.py:391
  17.4 1.5 %collective-permute-start.3 = (bf16[256,512]{1,0:T(8,128)(2,1)S(1)}, bf16[256,512]{1,0:T(8,128)(2,1)S(1)}, u32[]{:S(2)}, u32[]{:S(2)}) collective-permute-start(bf16[256,512]{1,0:T(8,128)(2,1)S(1)} %collective-permute-done.2.kv_ref), channel_id=1, source_target_pairs={{0,2},{2,0},{4,6},{6,4},{8,10},{10,8},{12,14},{14,12},{16,18},{18,... | collective-permute-start | bytes 786440 | tf_op jit(solution)/shard_map/ppermute | solution.py:452
  17.6 6.5 %collective-permute-start.5 = (bf16[256,256]{1,0:T(8,128)(2,1)S(1)}, bf16[256,256]{1,0:T(8,128)(2,1)S(1)}, u32[]{:S(2)}, u32[]{:S(2)}) collective-permute-start(bf16[256,256]{1,0:T(8,128)(2,1)S(1)} %slice.3), channel_id=1, source_target_pairs={{0,2},{2,8},{4,6},{6,12},{8,10},{10,16},{12,14},{14,20},{16,18},{1... | collective-permute-start | bytes 393224 | tf_op jit(solution)/shard_map/ppermute | solution.py:450
  19.6 12.2 %collective-permute-start.8 = (bf16[256,384]{1,0:T(8,128)(2,1)S(1)}, bf16[256,384]{1,0:T(8,128)(2,1)S(1)}, u32[]{:S(2)}, u32[]{:S(2)}) collective-permute-start(bf16[256,384]{1,0:T(8,128)(2,1)S(1)} %last_tile.3.second0_ref), channel_id=1, source_target_pairs={{0,1},{1,0},{2,3},{3,2},{4,5},{5,4},{6,7},{7,6},{8,9},{9,8},{10,11... | collective-permute-start | bytes 589832 | tf_op jit(solution)/shard_map/ppermute | solution.py:391
  22.2 10.8 %collective-permute-start.7 = (bf16[256,512]{1,0:T(8,128)(2,1)S(1)}, bf16[256,512]{1,0:T(8,128)(2,1)S(1)}, u32[]{:S(2)}, u32[]{:S(2)}) collective-permute-start(bf16[256,512]{1,0:T(8,128)(2,1)S(1)} %last_tile.4.second1_ref), channel_id=1, source_target_pairs={{0,1},{1,0},{2,3},{3,2},{4,5},{5,4},{6,7},{7,6},{8,9},{9,8},{10,11... | collective-permute-start | bytes 786440 | tf_op jit(solution)/shard_map/ppermute | solution.py:391
  24.6 9.1 %collective-permute-start.6 = (bf16[256,128]{1,0:T(8,128)(2,1)S(1)}, bf16[256,128]{1,0:T(8,128)(2,1)S(1)}, u32[]{:S(2)}, u32[]{:S(2)}) collective-permute-start(bf16[256,128]{1,0:T(8,128)(2,1)S(1)} %last_tile.5.second2_ref), channel_id=1, source_target_pairs={{0,1},{1,0},{2,3},{3,2},{4,5},{5,4},{6,7},{7,6},{8,9},{9,8},{10,11... | collective-permute-start | bytes 196616 | tf_op jit(solution)/shard_map/ppermute | solution.py:391
